TPU v7x, 256 devices: a whole 4x4x8 slice. The times are simulated.
256 devices in a mesh: seg: 32 (over y, x, core), fe: 8 (over z).
Axes of the slice: x: 4, y: 4, z: 8, core: 2. Of those that a mesh axis runs over, the one named last changes fastest.
Arguments:
- seg_pos: float32 [3, 4096], P(None, 'seg'), may hold values from 0 to 1
- burgers: float32 [3, 4096], P(None, 'seg'), may hold values from -6 to 6
- seg_tile: int32 [4096], P('seg'), may hold values from 0 to 7
- quad_pos: float32 [3, 524288], P(None, 'fe'), may hold values from 0 to 1
- quad_node: int32 [524288], P('fe'), may hold values from 0 to 65535
- stiffness: float32 [128, 128, 1024], P('seg', None, 'fe'), may hold values from 0.05 to 2
Outputs:
- correction: float32 [3, 128, 128, 1024], P(None, 'seg', None, 'fe')
- stress: float32 [3, 4096], P(None, 'seg')
Inputs may be any that keep to these rules, and one draw needn't show every extreme that they name: `quad_node`: entry q numbers a node of the block of 4 x 128 x 128 nodes whose corner is grid node ((q mod 65536) // 2048 * 4, 0, q // 65536 * 128), first index slowest.
All inputs are finite; a program needn't handle non-finite values.
Results may differ from a plain program's by a relative error of at most 0.0003.
Values sent between devices are 32-bit elements; how exact they have to be, the bound alone decides.
No kernel may reach another device: no remote copies, remote signals or barrier semaphores. Data moves between devices by JAX's collectives and lax.ppermute only.
A program may use at most 128 MiB of HBM per device.

v0:
```python
import math

import jax
import jax.numpy as jnp
from jax import lax
from jax.sharding import PartitionSpec as P

ITERS = 2


CORE = 0.0001
STRENGTH = 0.001
HIGH = lax.Precision.HIGHEST


def with_halo(x, sides, width):
    for axis, dim in sides:
        devices, length = (lax.axis_size(axis), x.shape[dim])
        up = [(i, (i + 1) % devices) for i in range(devices - 1)]
        down = [(j, i) for i, j in up]
        last = lax.slice_in_dim(x, length - width, length, axis=dim)
        first = lax.slice_in_dim(x, 0, width, axis=dim)
        before = lax.ppermute(last, axis, up)
        after = lax.ppermute(first, axis, down)
        x = jnp.concatenate([before, x, after], axis=dim)
    return x


def near_weights(q_pos, q_tile, s_pos, s_tile):
    dist = (q_pos[0][:, None] - s_pos[0][None, :]) ** 2
    dist = dist + (q_pos[1][:, None] - s_pos[1][None, :]) ** 2
    dist = dist + (q_pos[2][:, None] - s_pos[2][None, :]) ** 2
    inverse = lax.rsqrt(dist + CORE)
    near = jnp.abs(q_tile[:, None] - s_tile[None, :]) <= 1
    return jnp.where(near, STRENGTH * (inverse * inverse * inverse), 0.0)


def block_size(length, width):
    return math.gcd(length, 1 << max(9, 20 - max(width, 1).bit_length()))


def traction_terms(q_pos, q_tile, s_pos, s_tile, vectors):
    length = q_pos.shape[1]
    size = block_size(length, s_pos.shape[1])
    count = length // size
    pos_groups = q_pos.reshape(3, count, size).transpose(1, 0, 2)
    tile_groups = q_tile.reshape(count, size)

    def traction_one_group(item):
        weights = near_weights(item[0], item[1], s_pos, s_tile)
        return jnp.einsum("gs,cs->cg", weights, vectors, precision=HIGH)

    terms = lax.map(traction_one_group, (pos_groups, tile_groups))
    return terms.transpose(1, 0, 2).reshape(3, length)


def stress_terms(total, q_pos, q_tile, values, s_pos, s_tile):
    length = q_pos.shape[1]
    size = block_size(length, s_pos.shape[1])
    count = length // size
    pos_groups = q_pos.reshape(3, count, size).transpose(1, 0, 2)
    tile_groups = q_tile.reshape(count, size)
    value_groups = values.reshape(3, count, size).transpose(1, 0, 2)

    def stress_one_group(carry, item):
        weights = near_weights(item[0], item[1], s_pos, s_tile)
        return (carry + jnp.einsum("gs,cg->cs", weights, item[2], precision=HIGH), None)

    result, unused = lax.scan(stress_one_group, total, (pos_groups, tile_groups, value_groups))
    return result


def operate(field, stiffness):
    padded = with_halo(field, (("seg", 1), ("fe", 3)), 1)
    beside = padded[:, 2:, :, 1:-1] + padded[:, :-2, :, 1:-1]
    beside = beside + padded[:, 1:-1, :, 2:] + padded[:, 1:-1, :, :-2]
    rows = jnp.pad(field, ((0, 0), (0, 0), (1, 1), (0, 0)))
    beside = beside + rows[:, :, 2:, :] + rows[:, :, :-2, :]
    return (6.0 + stiffness) * field - beside


def squares(residual):
    return lax.psum(jnp.sum(residual * residual), ("seg", "fe"))


def shards(seg_pos, burgers, seg_tile, quad_pos, quad_node, stiffness):
    n_seg = lax.axis_size("seg")
    column = lax.axis_index("seg")
    block = lax.axis_index("fe")
    s_dev = seg_pos.shape[1]
    q_block = quad_pos.shape[1]
    q_dev = q_block // n_seg
    total_segs = s_dev * n_seg
    total_points = q_block * lax.axis_size("fe")
    wide, tall, deep = stiffness.shape
    my_nodes = lax.dynamic_slice_in_dim(quad_node, column * q_dev, q_dev, 0)
    scale_t = 1.0 / math.sqrt(total_segs)
    block_tiles = jnp.full((q_block,), block, jnp.int32)
    partial_value = traction_terms(quad_pos, block_tiles, seg_pos, seg_tile, burgers)
    whole = lax.psum(partial_value, "seg")
    mine = lax.dynamic_slice_in_dim(whole, column * q_dev, q_dev, 1) * scale_t
    load = jnp.zeros((3, wide * tall * deep), jnp.float32).at[:, my_nodes].add(mine)
    load = load.reshape(3, wide, tall, deep)
    correction = jnp.zeros_like(load)
    residual = load
    direction = load
    norm_now = squares(residual)
    for step in range(ITERS):
        image = operate(direction, stiffness)
        alpha = norm_now / lax.psum(jnp.sum(direction * image), ("seg", "fe"))
        correction = correction + alpha * direction
        residual = residual - alpha * image
        norm_next = squares(residual)
        direction = residual + norm_next / norm_now * direction
        norm_now = norm_next
    motion = correction.reshape(3, wide * tall * deep)[:, my_nodes]
    piece = lax.all_gather(motion, "seg", axis=1, tiled=True)
    length = piece.shape[1]
    tiles = jnp.full((length,), block, jnp.int32)
    partial_stress = stress_terms(
        jnp.zeros((3, s_dev), jnp.float32), quad_pos, tiles, piece, seg_pos, seg_tile
    )
    stress = lax.psum(partial_stress, "fe") * (4.0 / math.sqrt(total_points))
    return (correction, stress)


def solution(mesh):
    placed = (
        P(None, "seg"),
        P(None, "seg"),
        P("seg"),
        P(None, "fe"),
        P("fe"),
        P("seg", None, "fe"),
    )
    return jax.shard_map(
        shards,
        mesh=mesh,
        in_specs=placed,
        out_specs=(P(None, "seg", None, "fe"), P(None, "seg")),
        check_vma=False,
    )
```

profile of v0, /device:TPU:1, one launch (start us, length us, event | category | flops | bytes accessed | tf_op | source)
XLA Modules:
  0.0 830.9 jit_solution(5003524660675801442)
XLA Ops:
  7.3 120.1 %while.21 = (s32[]{:T(128)}, f32[16,3,4096]{2,1,0:T(4,128)}, s32[16,4096]{1,0:T(8,128)S(1)}, s32[128]{0:T(128)}, f32[16,3,4096]{2,1,0:T(4,128)}, /*index=5*/f32[...) while((s32[]{:T(128)}, f32[16,3,4096]{2,1,0:T(4,128)}, ...), condition=%wide.region_1.2_spmd, body=%wide.region_0.1_spmd.sunk | while | flops 27262980 | bytes 269973 | solution.py:53
  9.1 5.7 fusion.94
  24.1 5.7 fusion.94
  39.1 5.7 fusion.94
  54.1 5.7 fusion.94
  61.6 5.7 fusion.94
  91.7 5.7 fusion.94
  99.2 5.7 fusion.94
  106.7 5.7 fusion.94
  121.7 5.7 fusion.94
  128.1 118.2 %all-reduce.5.cloned.1.call-done = f32[3,65536]{1,0:T(4,128)} async-done(((f32[3,65536]{1,0:T(4,128)}), f32[3,65536]{1,0:T(4,128)}) %all-reduce.5.cloned.1.call-update) | async-done | bytes 786448 | tf_op jit(solution)/shard_map/psum | solution.py:100
  247.4 24.6 %scatter_custom_fusion = f32[3,65536]{0,1:T(8,128)} fusion(s32[2048]{0:T(1024)S(1)} %get-tuple-element.137, f32[2048,3]{1,0:T(8,128)S(1)} %copy.51, f32[]{:T(128)} %constant.34.clone.1), kind=kCustom, calls=%fused_computation.84 | custom fusion | flops 6144 | bytes 786436 | tf_op jit(solution)/shard_map/scatter-add | solution.py:102
  272.1 10.8 %fusion.83 = (f32[3,1,128,128]{0,3,2,1:T(8,128)}, f32[3,1,128,128]{0,3,2,1:T(8,128)}) fusion(f32[3,4,128,128]{0,3,2,1:T(8,128)} %bitcast.75), kind=kLoop, calls=%fused_computation.136 | loop fusion | bytes 786432 | tf_op jit(solution)/shard_map/slice | solution.py:21
  299.1 19.6 %copy.64 = f32[3,4,128,128]{2,1,3,0:T(4,128)S(1)} copy(f32[3,4,128,128]{0,3,2,1:T(8,128)} %bitcast.76) | data formatting | bytes 1572864 | tf_op jit(solution)/shard_map/reshape | solution.py:103
  324.5 15.6 %multiply_reduce_fusion = f32[]{:T(128)} fusion(f32[3,65536]{0,1:T(8,128)} %scatter_custom_fusion), kind=kLoop, calls=%fused_computation.83 | loop fusion | flops 393215 | bytes 786436 | tf_op jit(solution)/shard_map/reduce_sum | solution.py:83
  343.3 77.9 %all-reduce.2 = (f32[]{:T(128)}, f32[]{:T(128)}) all-reduce(f32[]{:T(128)} %multiply_reduce_fusion, f32[]{:T(128)} %get-tuple-element.138), channel_id=1, replica_groups=mesh['seg'=32,'fe'=8] {'seg','fe'}, use_global_device_ids=true, to_apply=%region_5.6 | all-reduce | flops 2 | bytes 16 | tf_op jit(solution)/shard_map/psum | solution.py:83
  423.5 73.4 %psum.45 = f32[]{:T(128)} all-reduce(f32[]{:T(128)} %multiply_reduce_fusion.1), channel_id=1, replica_groups=mesh['seg'=32,'fe'=8] {'seg','fe'}, use_global_device_ids=true, to_apply=%region_9.10 | all-reduce | flops 1 | bytes 8 | tf_op jit(solution)/shard_map/psum | solution.py:83
  516.6 80.2 %psum.46 = f32[]{:T(128)} all-reduce(f32[]{:T(128)} %fusion.81), channel_id=1, replica_groups=mesh['seg'=32,'fe'=8] {'seg','fe'}, use_global_device_ids=true, to_apply=%region_11.12 | all-reduce | flops 1 | bytes 8 | tf_op jit(solution)/shard_map/psum | solution.py:110
  598.2 16.7 %copy.74 = f32[3,4,128,128]{0,3,2,1:T(8,128)} copy(f32[3,4,128,128]{2,1,3,0:T(4,128)S(1)} %bitcast.85) | data formatting | bytes 1572864 | tf_op jit(solution)/shard_map/add | solution.py:111
  616.1 16.0 %gather_fusion = f32[2048,3]{1,0:T(8,128)S(1)} fusion(f32[3,65536]{0,1:T(8,128)} %bitcast.78, s32[2048]{0:T(1024)S(1)} %get-tuple-element.136), kind=kCustom, calls=%fused_computation | custom fusion | bytes 57344 | tf_op jit(solution)/shard_map/gather | solution.py:116
  632.1 94.6 %all-gather = f32[3,65536]{0,1:T(8,128)} all-gather(f32[3,2048]{0,1:T(8,128)S(1)} %bitcast.87), channel_id=2, replica_groups=mesh['seg'=32,'fe'=8] {'seg'}, dimensions={1}, use_global_device_ids=true | all-gather | bytes 811008 | tf_op jit(solution)/shard_map/all_gather | solution.py:117
  726.8 17.7 %copy.75 = f32[3,16,4096]{2,0,1:T(4,128)S(1)} copy(f32[3,16,4096]{0,2,1:T(8,128)} %bitcast.77) | data formatting | bytes 1572864 | tf_op jit(solution)/shard_map/reshape | solution.py:63
  744.5 65.7 %while.22 = (s32[]{:T(128)}, f32[3,128]{1,0:T(4,128)S(1)}, f32[16,3,4096]{2,1,0:T(4,128)S(1)}, s32[16,4096]{1,0:T(8,128)S(1)}, s32[128]{0:T(128)S(1)}, /*index=5...) while((s32[]{:T(128)}, f32[3,128]{1,0:T(4,128)S(1)}, ...), condition=%wide.region_13.14_spmd.clone, body=%wide.region_12.13_spmd.clone.sunk | while | flops 27263748 | bytes 271011 | solution.py:69
  810.2 13.2 %psum.47 = f32[3,128]{1,0:T(4,128)S(1)} all-reduce(f32[3,128]{1,0:T(4,128)S(1)} %get-tuple-element.77), channel_id=1, replica_groups=mesh['seg'=32,'fe'=8] {'fe'}, use_global_device_ids=true, to_apply=%region_14.15 | all-reduce | flops 384 | bytes 3072 | tf_op jit(solution)/shard_map/psum | solution.py:123
  (169 shorter events, 182.2 us)
Async XLA Ops:
  7.2 239.1 %all-reduce.5.cloned.1.call-start = ((), (), s32[]{:S(2)}) async-start(), calls=%async_computation | async-start | bytes 2097152 | tf_op jit(solution)/shard_map/psum | solution.py:100
  288.1 30.6 %collective-permute-start = (f32[3,1,128,128]{3,2,1,0:T(8,128)S(1)}, f32[3,1,128,128]{3,2,1,0:T(8,128)S(1)}, u32[]{:S(2)}, u32[]{:S(2)}) collective-permute-start(f32[3,1,128,128]{3,2,1,0:T(8,128)S(1)} %copy.77), channel_id=1, source_target_pairs={{8,0},{16,8},{24,16},{32,24},{40,32},{48,40},{56,48},{64,56},{72,6... | collective-permute-start | bytes 589832 | tf_op jit(solution)/shard_map/ppermute | solution.py:24
  290.8 8.2 copy-start
  296.0 22.8 %collective-permute-start.1 = (f32[3,1,128,128]{3,2,1,0:T(8,128)S(1)}, f32[3,1,128,128]{3,2,1,0:T(8,128)S(1)}, u32[]{:S(2)}, u32[]{:S(2)}) collective-permute-start(f32[3,1,128,128]{3,2,1,0:T(8,128)S(1)} %copy.78), channel_id=1, source_target_pairs={{0,8},{8,16},{16,24},{24,32},{32,40},{40,48},{48,56},{56,64},{64,7... | collective-permute-start | bytes 589832 | tf_op jit(solution)/shard_map/ppermute | solution.py:23
  319.0 21.1 %collective-permute-start.2 = (f32[3,6,128,1]{2,1,3,0:T(8,128)S(1)}, f32[3,6,128,1]{2,1,3,0:T(8,128)S(1)}, u32[]{:S(2)}, u32[]{:S(2)}) collective-permute-start(f32[3,6,128,1]{2,1,3,0:T(8,128)S(1)} %get-tuple-element.156), channel_id=1, source_target_pairs={{1,0},{2,1},{3,2},{4,3},{5,4},{6,5},{7,6},{9,8},{10,9},{11,10},{12... | collective-permute-start | bytes 27656 | tf_op jit(solution)/shard_map/ppermute | solution.py:24
  320.3 19.8 %collective-permute-start.3 = (f32[3,6,128,1]{2,1,3,0:T(8,128)S(1)}, f32[3,6,128,1]{2,1,3,0:T(8,128)S(1)}, u32[]{:S(2)}, u32[]{:S(2)}) collective-permute-start(f32[3,6,128,1]{2,1,3,0:T(8,128)S(1)} %get-tuple-element.157), channel_id=1, source_target_pairs={{0,1},{1,2},{2,3},{3,4},{4,5},{5,6},{6,7},{8,9},{9,10},{10,11},{11... | collective-permute-start | bytes 27656 | tf_op jit(solution)/shard_map/ppermute | solution.py:23
  498.8 7.0 collective-permute-start.4
  501.5 5.6 collective-permute-start.5
  507.2 5.3 collective-permute-start.6
  508.5 4.8 collective-permute-start.7
  726.7 17.7 %copy-start.1 = (f32[3,128]{1,0:T(4,128)S(1)}, f32[3,128]{1,0:T(4,128)}, u32[]{:S(2)}) copy-start(f32[3,128]{1,0:T(4,128)} %get-tuple-element.349) | copy-start | bytes 4612
  726.7 17.7 %copy-start.2 = (s32[128]{0:T(128)S(1)}, s32[128]{0:T(128)}, u32[]{:S(2)}) copy-start(s32[128]{0:T(128)} %get-tuple-element.359) | copy-start | bytes 1540
Sparse Core Ops, SparseCore 0:
  127.5 118.7 all-reduce.4
where the time goes:
time: 836 us; the launch traced here: 831 us
  blocking collectives  339 us (41%)
  local copies, waits for them, and re-layouts  140 us (17%)
  matrix products  140 us (17%)
  waiting for transfers between devices  121 us (14%)
  other arithmetic  50 us (6%)
  starting transfers between devices  21.9 us (3%)
  between operations  18.3 us (2%)
    psum x2, blocking collectives, squares(): return lax.psum(jnp.sum(residual * residual), ('seg', 'fe'))  151 us
    psum x1, waiting for transfers between devices, shards(): whole = lax.psum(partial_value, 'seg')  118 us
    all_gather x1, blocking collectives, shards(): piece = lax.all_gather(motion, 'seg', axis=1, tiled=True)  94.6 us
    dot_general x16, matrix products, traction_one_group(): return jnp.einsum('gs,cs->cg', weights, vectors, precision=HIGH)  90.9 us
    psum x1, blocking collectives, shards(): alpha = norm_now / lax.psum(jnp.sum(direction * image), ('seg', 'fe'))  80.2 us
    dot_general x16, matrix products, stress_one_group(): jnp.einsum('gs,cg->cs', weights, item[2], precision=HIGH)  48.7 us
    slice x32, local copies, waits for them, and re-layouts, near_weights(): dist = (q_pos[0][:, None] - s_pos[0][None, :]) ** 2  32 us
    scatter-add x1, other arithmetic, shards(): jnp.zeros((3, wide * tall * deep), jnp.float32).at[:, my_nodes].add(mine)  24.6 us
  transfers between devices with their start and end apart: 9, of which 4 were waited for; matrix products, arithmetic and copies ran while one was open for 5% of the time, Pallas kernels for 0%

commit v1 on v0

v1 whole, which is shorter than its diff:
```python
import math

import jax
import jax.numpy as jnp
from jax import lax
from jax.experimental import pallas as pl
from jax.experimental.pallas import tpu as pltpu
from jax.sharding import PartitionSpec as P

CORE = 0.0001
STRENGTH = 0.001
HIGH = lax.Precision.HIGHEST
F32 = jnp.float32
BF16 = jnp.bfloat16
ROWS = 8
LANES = 128
CHUNK = 256
NT = (((1,), (1,)), ((), ()))
VMEM_LIMIT = 48 * 1024 * 1024


def iota(shape, dim):
    return lax.broadcasted_iota(jnp.int32, shape, dim)


def split(x):
    hi = x.astype(BF16)
    return hi, (x - hi.astype(F32)).astype(BF16)


def near_rank(tile, block):
    near = jnp.abs(tile - block) <= 1
    mask = jnp.where(near, 1.0, 0.0)
    n = tile.shape[1]
    before = jnp.where(iota((n, n), 0) < iota((n, n), 1), 1.0, 0.0)
    rank = jnp.dot(jnp.broadcast_to(mask, (ROWS, n)), before, preferred_element_type=F32)[:1]
    place = jnp.where(iota((n, n), 0) == rank.astype(jnp.int32), mask, 0.0)
    return mask, place


def pack_kernel(where_ref, pos_ref, burgers_ref, tile_ref, out_ref, vals):
    mask, place = near_rank(tile_ref[...], where_ref[1])
    vals[0:3, :] = pos_ref[...]
    vals[3:6, :] = burgers_ref[...]
    vals[6:8, :] = jnp.broadcast_to(mask, (2, mask.shape[1]))
    packed = lax.dot_general(vals[...], place, NT, precision=HIGH, preferred_element_type=F32)
    out_ref[...] = jnp.broadcast_to(packed[None], out_ref.shape)


def assemble(groups_ref, sbuf):
    n_groups, _, width = groups_ref.shape
    offset = jnp.int32(0)
    places = []
    for r in range(n_groups):
        group = groups_ref[r]
        count = jnp.sum(group[6:7, :]).astype(jnp.int32)
        sbuf[pl.ds(pl.multiple_of(offset, ROWS), width), 0:ROWS] = group.T
        places.append((offset, count))
        offset = offset + (count + (ROWS - 1)) // ROWS * ROWS
    sbuf[pl.ds(pl.multiple_of(offset, ROWS), CHUNK), 0:ROWS] = jnp.zeros((CHUNK, ROWS), F32)
    return places, (offset + (CHUNK - 1)) // CHUNK


def spread(sbuf, wide, start):
    for d in range(3):
        wide[d] = jnp.broadcast_to(sbuf[pl.ds(start, CHUNK), d : d + 1], (CHUNK, LANES))


def cubes(wide, q_ref, start, width):
    his, los = [], []
    for j in range(width // LANES):
        at = pl.ds(pl.multiple_of(start + j * LANES, LANES), LANES)
        dx = wide[0] - q_ref[0:1, at]
        dy = wide[1] - q_ref[1:2, at]
        dz = wide[2] - q_ref[2:3, at]
        inverse = lax.rsqrt((dx * dx + CORE) + (dy * dy + dz * dz))
        hi, lo = split(inverse * inverse * inverse)
        his.append(hi)
        los.append(lo)
    return jnp.concatenate(his, axis=1), jnp.concatenate(los, axis=1)


def traction_kernel(scale, groups_ref, q_ref, out_ref, sbuf, wide, total):
    q_dev = q_ref.shape[1]
    _, n_chunks = assemble(groups_ref, sbuf)
    total[...] = jnp.zeros_like(total)

    def chunk(i, carry):
        start = pl.multiple_of(i * CHUNK, CHUNK)
        spread(sbuf, wide, start)
        vectors = jnp.concatenate(split(sbuf[pl.ds(start, CHUNK), 0:ROWS].T), axis=0)
        vectors = jnp.concatenate([vectors, vectors], axis=1)

        def block(j, c):
            at = pl.multiple_of(j * CHUNK, CHUNK)
            hi, lo = cubes(wide, q_ref, at, CHUNK)
            weights = jnp.concatenate([hi, lo], axis=0)
            total[:, pl.ds(at, CHUNK)] += jnp.dot(vectors, weights, preferred_element_type=F32)
            return c

        return lax.fori_loop(0, q_dev // CHUNK, block, carry, unroll=2)

    lax.fori_loop(0, n_chunks, chunk, jnp.int32(0))
    both = (total[0:ROWS, :] + total[ROWS : 2 * ROWS, :]) * scale
    out_ref[...] = jnp.zeros_like(out_ref)
    out_ref[0:3, :] = both[3:6, :]


def row_hot(nodes, k, rows, first):
    row = nodes[k : k + 1, :] // LANES - first
    return jnp.where(iota((rows, LANES), 0) == row, 1.0, 0.0).astype(BF16)


def layers(nodes, t_ref, rows, first, hot, cols):
    n = nodes.shape[0]
    for k in range(n):
        at = slice(k * LANES, (k + 1) * LANES)
        hot[0:rows, at] = row_hot(nodes, k, rows, first)
        here = iota((LANES, LANES), 0) == nodes[k : k + 1, :] % LANES
        for c in range(3):
            value = t_ref[c : c + 1, at]
            hi = value.astype(BF16).astype(F32)
            for p, part in enumerate((hi, value - hi)):
                to = (p * 3 + c) * LANES
                cols[to : to + LANES, at] = jnp.where(here, part, 0.0).astype(BF16)
    out = lax.dot_general(hot[0:rows, :], cols[...], NT, preferred_element_type=F32)
    half = 3 * LANES
    return out[:, :half] + out[:, half:]


def scatter_kernel(where_ref, nodes_ref, t_ref, b_ref, low_ref, high_ref, hot, cols, ends):
    n = t_ref.shape[1] // LANES
    rows = b_ref.shape[1]
    nodes = nodes_ref[pl.ds(pl.multiple_of(where_ref[0] * n, n), n), :]
    load = layers(nodes, t_ref, rows, 0, hot, cols)
    for c in range(3):
        b_ref[c] = load[:, c * LANES : (c + 1) * LANES]
    for k in range(n):
        at = slice(k * LANES, (k + 1) * LANES)
        last = nodes[k : k + 1, :] % LANES
        value = t_ref[:, at]
        hi = value.astype(BF16).astype(F32)
        for p, part in enumerate((hi, value - hi)):
            ends[p * 16 : p * 16 + 8, at] = jnp.where(last == 0, part, 0.0)
            ends[p * 16 + 8 : p * 16 + 16, at] = jnp.where(last == LANES - 1, part, 0.0)
    faces = lax.dot_general(ends[...].astype(BF16), hot[...], NT, preferred_element_type=F32)
    low_ref[...] = faces[0:8] + faces[16:24]
    high_ref[...] = faces[8:16] + faces[24:32]


def beside_in_layer(f):
    i, j = iota(f.shape, 0), iota(f.shape, 1)
    n, m = f.shape
    up = jnp.where(i == 0, 0.0, pltpu.roll(f, 1, 0)) + jnp.where(i == n - 1, 0.0, pltpu.roll(f, n - 1, 0))
    return up + (jnp.where(j == 0, 0.0, pltpu.roll(f, 1, 1)) + jnp.where(j == m - 1, 0.0, pltpu.roll(f, m - 1, 1)))


def operate_kernel(
    n_seg, where_ref, nodes_ref, b_ref, left_ref, right_ref, below_ref, above_ref, k_ref, kr_ref,
    u_ref, g_ref, low_ref, high_ref, corner_ref, sums_ref, hot, cols, parts,
):
    n = left_ref.shape[1] // LANES
    rows = b_ref.shape[1]
    wide = rows // LANES
    me = where_ref[0]

    def nodes_of(r):
        return nodes_ref[pl.ds(pl.multiple_of(r * n, n), n), :]

    left = layers(nodes_of(jnp.maximum(me - 1, 0)), left_ref, LANES, rows - LANES, hot, cols)
    right = layers(nodes_of(jnp.minimum(me + 1, n_seg - 1)), right_ref, 2 * LANES, 0, hot, cols)
    below, above = below_ref[...].T, above_ref[...].T
    lane = iota((LANES, LANES), 1)
    zero = jnp.zeros((LANES, LANES), F32)
    bb, bu, uu, uau = zero, zero, zero, zero
    not_last = jnp.where(me < n_seg - 1, 1.0, 0.0)
    low_ref[...] = jnp.zeros_like(low_ref)
    high_ref[...] = jnp.zeros_like(high_ref)
    corner_ref[...] = jnp.zeros_like(corner_ref)
    for c in range(3):
        comp = slice(c * LANES, (c + 1) * LANES)
        b4, b5 = right[0:LANES, comp], right[LANES : 2 * LANES, comp]
        field = [left[:, comp]] + [b_ref[c, x * LANES : (x + 1) * LANES, :] for x in range(wide)] + [b4]
        us = []
        for x in range(wide):
            at = slice(x * LANES, (x + 1) * LANES)
            f = field[x + 1]
            beside = beside_in_layer(f) + (field[x] + field[x + 2])
            beside = beside + jnp.where(lane == 0, below[at, c : c + 1], 0.0)
            beside = beside + jnp.where(lane == LANES - 1, above[at, c : c + 1], 0.0)
            u = (6.0 + k_ref[at, :]) * f - beside
            u_ref[c, at, :] = u
            us.append(u)
            bb = bb + f * f
            bu = bu + f * u
            uu = uu + u * u
            b_hi, b_lo = split(f.T)
            u_t = u.T
            u_hi, u_lo = split(u_t)
            low_ref[c : c + 1, at] = u_t[0:1, :]
            high_ref[c : c + 1, at] = u_t[LANES - 1 : LANES, :]
            for place, hi, lo in ((c, b_hi, b_lo), (c + 3, u_hi, u_lo)):
                to = slice(place * LANES, (place + 1) * LANES)
                parts[to, at] = hi
                parts[to, rows + x * LANES : rows + (x + 1) * LANES] = lo
        ur = (6.0 + kr_ref[...]) * b4 - (field[wide] + b5 + beside_in_layer(b4))
        for x in range(wide):
            at = slice(x * LANES, (x + 1) * LANES)
            au = (6.0 + k_ref[at, :]) * us[x] - beside_in_layer(us[x])
            if x + 1 < wide:
                au = au - 2.0 * us[x + 1]
            else:
                au = au - (2.0 * not_last) * ur
            uau = uau + us[x] * au
        b4_t = b4.T
        corner_ref[c : c + 1, 0:LANES] = b4_t[0:1, :]
        corner_ref[c : c + 1, LANES : 2 * LANES] = b4_t[LANES - 1 : LANES, :]
    line = iota((1, LANES), 1)
    sums = jnp.zeros((1, LANES), F32)
    for i, part in enumerate((bb, bu, uu, uau)):
        sums = sums + jnp.where(line == i, jnp.sum(part), 0.0)
    sums_ref[...] = jnp.broadcast_to(sums, sums_ref.shape)

    nodes = nodes_of(me)
    g_ref[...] = jnp.zeros_like(g_ref)
    for k in range(0, n, 2):
        here = jnp.concatenate([row_hot(nodes, k, rows, 0), row_hot(nodes, k + 1, rows, 0)], axis=1)
        here = jnp.concatenate([here, here], axis=0)
        found = jnp.dot(parts[...], here, preferred_element_type=F32)
        last = jnp.concatenate([nodes[k : k + 1, :], nodes[k + 1 : k + 2, :]], axis=1) % LANES
        pick = iota((LANES, 2 * LANES), 0) == last
        for v in range(6):
            value = jnp.where(pick, found[v * LANES : (v + 1) * LANES, :], 0.0)
            g_ref[v : v + 1, k * LANES : (k + 2) * LANES] = jnp.sum(value, axis=0, keepdims=True)


def stress_kernel(groups_ref, q_ref, g_ref, out_ref, sbuf, wide, results, motion):
    q_dev = q_ref.shape[1]
    places, n_chunks = assemble(groups_ref, sbuf)
    hi, lo = split(g_ref[...])
    motion[...] = jnp.concatenate([hi, lo], axis=0)

    def chunk(i, carry):
        start = pl.multiple_of(i * CHUNK, CHUNK)
        spread(sbuf, wide, start)

        def block(j, total):
            at = pl.multiple_of(j * CHUNK, CHUNK)
            hi, lo = cubes(wide, q_ref, at, CHUNK)
            weights = jnp.concatenate([hi, lo], axis=1)
            m = motion[:, pl.ds(at, CHUNK)]
            m = jnp.concatenate([m, m], axis=1)
            return total + lax.dot_general(weights, m, NT, preferred_element_type=F32)

        results[pl.ds(start, CHUNK), 0 : 2 * ROWS] = lax.fori_loop(
            0, q_dev // CHUNK, block, jnp.zeros((CHUNK, 2 * ROWS), F32), unroll=2
        )
        return carry

    lax.fori_loop(0, n_chunks, chunk, jnp.int32(0))
    width = groups_ref.shape[2]
    for r, (offset, count) in enumerate(places):
        found = results[pl.ds(pl.multiple_of(offset, ROWS), width), 0 : 2 * ROWS].T
        found = found[0:ROWS] + found[ROWS : 2 * ROWS]
        out_ref[r] = jnp.where(iota((ROWS, width), 1) < count, found, 0.0)


def moments_kernel(sums_ref, high_ref, above_ref, below_ref, corner_ref, partial_ref, out_ref):
    rows = high_ref.shape[1]
    above, below = above_ref[...], below_ref[...]
    crossing = jnp.sum(high_ref[...] * above)
    last = slice(rows - LANES, rows)
    crossing = crossing - jnp.sum(above[:, last] * corner_ref[:, LANES : 2 * LANES])
    crossing = crossing - jnp.sum(below[:, last] * corner_ref[:, 0:LANES])
    lane = iota((ROWS, LANES), 1)
    sums = sums_ref[...] - jnp.where(lane == 3, 2.0 * crossing, 0.0)
    row = iota((ROWS, LANES), 0)
    out_ref[...] = jnp.where((row == 6)[None], sums[None], partial_ref[...])


def unpack_kernel(where_ref, tile_ref, partial_ref, out_ref):
    _, place = near_rank(tile_ref[...], where_ref[1])
    total = jnp.sum(partial_ref[...], axis=0)
    spreaded = jnp.dot(total, place, precision=HIGH, preferred_element_type=F32)
    total = jnp.where(iota(total.shape, 0) == 6, total, spreaded)
    out_ref[...] = jnp.broadcast_to(total[None], out_ref.shape)


def finish_kernel(scale, partial_ref, b_ref, u_ref, correction_ref, stress_ref):
    total = jnp.sum(partial_ref[...], axis=0)
    bb, bu, uu, uau = [total[6:7, i : i + 1] for i in range(4)]
    alpha = bb / bu
    later = bb - 2.0 * alpha * bu + alpha * alpha * uu
    beta = later / bb
    grow = 1.0 + beta
    alpha_next = later / (grow * grow * bu - 2.0 * alpha * grow * uu + alpha * alpha * uau)
    on_b = alpha + alpha_next * grow
    on_u = -alpha_next * alpha
    stress_ref[...] = (on_b * total[0:3] + on_u * total[3:6]) * scale
    for c in range(3):
        correction_ref[c] = on_b * b_ref[c] + on_u * u_ref[c]


def call(kernel, out, scratch=(), smem=0, inputs=0, flops=0, moved=0):
    specs = [pl.BlockSpec(memory_space=pltpu.SMEM)] * smem + [pl.BlockSpec(memory_space=pltpu.VMEM)] * inputs
    shapes = [jax.ShapeDtypeStruct(s, F32) for s in out]
    single = len(shapes) == 1
    vmem = pl.BlockSpec(memory_space=pltpu.VMEM)
    return pl.pallas_call(
        kernel,
        out_shape=shapes[0] if single else tuple(shapes),
        in_specs=specs,
        out_specs=vmem if single else (vmem,) * len(shapes),
        scratch_shapes=list(scratch),
        compiler_params=pltpu.CompilerParams(vmem_limit_bytes=VMEM_LIMIT),
        cost_estimate=pl.CostEstimate(flops=flops, bytes_accessed=moved, transcendentals=0),
    )


def shards(seg_pos, burgers, seg_tile, quad_pos, quad_node, stiffness):
    n_seg, n_fe = lax.axis_size("seg"), lax.axis_size("fe")
    column, block = lax.axis_index("seg"), lax.axis_index("fe")
    s_dev = seg_pos.shape[1]
    q_block = quad_pos.shape[1]
    q_dev = q_block // n_seg
    total_segs = s_dev * n_seg
    total_points = q_block * n_fe
    wide, tall, deep = stiffness.shape
    rows = wide * tall
    where = jnp.stack([column, block]).astype(jnp.int32)
    tile = seg_tile.reshape(1, s_dev)
    nodes = quad_node.reshape(q_block // LANES, LANES)
    points = lax.dynamic_slice_in_dim(quad_pos, column * q_dev, q_dev, 1)
    stiff = stiffness.reshape(rows, deep)

    up_seg = [(i, i + 1) for i in range(n_seg - 1)]
    down_seg = [(i + 1, i) for i in range(n_seg - 1)]
    up_fe = [(i, i + 1) for i in range(n_fe - 1)]
    down_fe = [(i + 1, i) for i in range(n_fe - 1)]

    stiff_right = lax.ppermute(stiff[0:LANES], "seg", down_seg)
    packed = call(
        pack_kernel, [(n_seg, ROWS, s_dev)], [pltpu.VMEM((ROWS, s_dev), F32)], smem=1, inputs=3
    )(where, seg_pos, burgers, tile)
    groups = lax.all_to_all(packed, "seg", 0, 0, tiled=True)

    long = total_segs + 2 * CHUNK
    sbuf = pltpu.VMEM((long, LANES), F32)
    spreaded = pltpu.VMEM((3, CHUNK, LANES), F32)

    def traction(*refs):
        traction_kernel(STRENGTH / math.sqrt(total_segs), *refs)

    t = call(
        traction, [(ROWS, q_dev)], [sbuf, spreaded, pltpu.VMEM((2 * ROWS, q_dev), F32)], inputs=2,
        flops=10**9, moved=10**6,
    )(groups, points)
    from_left = lax.ppermute(t, "seg", up_seg)
    from_right = lax.ppermute(t, "seg", down_seg)
    hot = pltpu.VMEM((rows, q_dev), BF16)
    cols = pltpu.VMEM((6 * LANES, q_dev), BF16)
    b, low, high = call(
        scatter_kernel, [(3, rows, deep), (ROWS, rows), (ROWS, rows)],
        [hot, cols, pltpu.VMEM((4 * ROWS, q_dev), F32)], smem=1, inputs=2, flops=2 * 10**9, moved=10**6,
    )(where, nodes, t)
    below = lax.ppermute(high, "fe", up_fe)
    above = lax.ppermute(low, "fe", down_fe)

    def operate(*refs):
        operate_kernel(n_seg, *refs)

    u, motion, low, high, corner, sums = call(
        operate, [(3, rows, deep), (ROWS, q_dev), (ROWS, rows), (ROWS, rows), (ROWS, 2 * LANES), (ROWS, LANES)],
        [hot, cols, pltpu.VMEM((6 * LANES, 2 * rows), BF16)], smem=1, inputs=8, flops=4 * 10**9, moved=4 * 10**6,
    )(where, nodes, b, from_left, from_right, below, above, stiff, stiff_right)
    u_below = lax.ppermute(high, "fe", up_fe)
    u_above = lax.ppermute(low, "fe", down_fe)
    partial = call(
        stress_kernel, [(n_seg, ROWS, s_dev)],
        [sbuf, spreaded, pltpu.VMEM((long, LANES), F32), pltpu.VMEM((2 * ROWS, q_dev), BF16)],
        inputs=3, flops=10**10, moved=10**6,
    )(groups, points, motion)
    partial = call(moments_kernel, [(n_seg, ROWS, s_dev)], inputs=6)(sums, high, u_above, u_below, corner, partial)
    partial = lax.all_to_all(partial, "seg", 0, 0, tiled=True)
    partial = call(unpack_kernel, [(n_fe, ROWS, s_dev)], smem=1, inputs=2)(where, tile, partial)
    partial = lax.all_to_all(partial, "fe", 0, 0, tiled=True)

    def finish(*refs):
        finish_kernel(4.0 * STRENGTH / math.sqrt(total_points), *refs)

    correction, stress = call(finish, [(3, rows, deep), (3, s_dev)], inputs=3)(partial, b, u)
    return correction.reshape(3, wide, tall, deep), stress


def solution(mesh):
    placed = (
        P(None, "seg"),
        P(None, "seg"),
        P("seg"),
        P(None, "fe"),
        P("fe"),
        P("seg", None, "fe"),
    )
    return jax.shard_map(
        shards,
        mesh=mesh,
        in_specs=placed,
        out_specs=(P(None, "seg", None, "fe"), P(None, "seg")),
        check_vma=False,
    )
```

time: 836 us -> 113 us (0.14)
  blocking collectives: 339 us -> 32.1 us
  matrix products: 140 us -> 0 us
  local copies, waits for them, and re-layouts: 140 us -> 1.63 us
  waiting for transfers between devices: 121 us -> 11 us
  other arithmetic: 50 us -> 0.08 us
  Pallas kernels: 0 us -> 36.8 us
  between operations: 18.3 us -> 0.83 us
    psum x4 -> x0, blocking collectives: 245 us -> none  [the longest x2 151 us: squares(): return lax.psum(jnp.sum(residual * residual), ('seg', 'fe'))]
    dot_general x32 -> x0, matrix products: 140 us -> none  [the longest x16 90.9 us: traction_one_group(): return jnp.einsum('gs,cs->cg', weights, vectors, precision=HIGH)]
    psum x1 -> x0, waiting for transfers between devices: 118 us -> none  [shards(): whole = lax.psum(partial_value, 'seg')]
    all_gather x1 -> x0, blocking collectives: 94.6 us -> none  [shards(): piece = lax.all_gather(motion, 'seg', axis=1, tiled=True)]
    slice x36 -> x1, local copies, waits for them, and re-layouts: 43.3 us -> 0.93 us  [shards(): stiff_right = lax.ppermute(stiff[0:LANES], 'seg', down_seg)]
    reshape x3 -> x0, local copies, waits for them, and re-layouts: 37.3 us -> none  [the longest x1 19.6 us: shards(): load = load.reshape(3, wide, tall, deep)]
    pallas_call x0 -> x8, Pallas kernels: none -> 36.8 us  [the longest x1 10.9 us: shards(): call(stress_kernel, [(n_seg, ROWS, s_dev)], [sbuf, spreaded, pltpu.VMEM((...]
    all_to_all x0 -> x2, blocking collectives: none -> 32.1 us  [the longest x1 19.7 us: shards(): partial = lax.all_to_all(partial, 'fe', 0, 0, tiled=True)]
  transfers between devices with their start and end apart: 9 -> 8, of which waited for: 4 -> 2; matrix products, arithmetic and copies ran while one was open for 5% -> 0% of each run, Pallas kernels for 0% -> 23%
where the time goes in v1:
time: 113 us
  Pallas kernels  36.8 us (33%)
  blocking collectives  32.1 us (28%)
  starting transfers between devices  30.2 us (27%)
  waiting for transfers between devices  11 us (10%)
  local copies, waits for them, and re-layouts  1.63 us (1%)
    all_to_all x1, blocking collectives, shards(): partial = lax.all_to_all(partial, 'fe', 0, 0, tiled=True)  19.7 us
    all_to_all x1, blocking collectives, shards(): partial = lax.all_to_all(partial, 'seg', 0, 0, tiled=True)  12.4 us
    pallas_call x1, Pallas kernels, shards(): call(stress_kernel, [(n_seg, ROWS, s_dev)], [sbuf, spreaded, pltpu.VMEM((...  10.9 us
    pallas_call x1, Pallas kernels, shards(): call(traction, [(ROWS, q_dev)], [sbuf, spreaded, pltpu.VMEM((2 * ROWS, q_...  9.85 us
    pallas_call x1, Pallas kernels, shards(): call(operate, [(3, rows, deep), (ROWS, q_dev), (ROWS, rows), (ROWS, rows)...  8.86 us
    all_to_all x1, waiting for transfers between devices, shards(): groups = lax.all_to_all(packed, 'seg', 0, 0, tiled=True)  7.58 us
    ppermute x1, starting transfers between devices, shards(): below = lax.ppermute(high, 'fe', up_fe)  7.13 us
    all_to_all x1, starting transfers between devices, shards(): groups = lax.all_to_all(packed, 'seg', 0, 0, tiled=True)  5.47 us
  transfers between devices with their start and end apart: 8, of which 2 were waited for; matrix products, arithmetic and copies ran while one was open for 0% of the time, Pallas kernels for 23%

profile of v1, /device:TPU:1, one launch (start us, length us, event | category | flops | bytes accessed | tf_op | source)
XLA Modules:
  0.0 112.6 jit_solution(5673045549308086502)
XLA Ops:
  0.6 0.9 slice_bitcast_fusion
  1.6 5.1 %collective-permute-start.4 = (f32[128,128]{1,0:T(8,128)S(1)}, f32[128,128]{1,0:T(8,128)S(1)}, u32[]{:S(2)}, u32[]{:S(2)}) collective-permute-start(f32[128,128]{1,0:T(8,128)S(1)} %slice_bitcast_fusion), channel_id=1, source_target_pairs={{8,0},{16,8},{24,16},{32,24},{40,32},{48,40},{56,48},{64,56},{72,6... | collective-permute-start | bytes 196616 | tf_op jit(solution)/shard_map/ppermute | solution.py:341
  6.8 0.1 pad_add_fusion.where_ref.refs_0_
  6.8 0.6 copy-done.3
  7.4 0.1 copy-done.4
  7.5 1.6 %shard_map.77 = f32[32,8,128]{2,1,0:T(8,128)} custom-call(s32[2]{0:T(128)S(1)} %pad_add_fusion.where_ref.refs_0_, f32[3,128]{1,0:T(4,128)S(1)} %copy-done.2, f32[3,128]{1,0:T(4,128)S(1)} %copy-done.3, s32[1,128]{1,0:T(1,128)S(1)} %bitcast.9), custom_call_target="tpu_custom_call" | custom-call | tf_op jit(solution)/shard_map/pallas_call | solution.py:342
  9.0 5.5 %all-to-all-start = ((f32[32,8,128]{2,1,0:T(8,128)}), f32[32,8,128]{2,1,0:T(8,128)S(1)}, u32[]{:S(2)}, u32[]{:S(2)}) async-start(f32[32,8,128]{2,1,0:T(8,128)} %shard_map.77), calls=%async_computation | async-start | bytes 262144 | tf_op jit(solution)/shard_map/all_to_all | solution.py:345
  14.6 7.6 %all-to-all-done.refs_0_.groups_ref = f32[32,8,128]{2,1,0:T(8,128)S(1)} async-done(((f32[32,8,128]{2,1,0:T(8,128)}), f32[32,8,128]{2,1,0:T(8,128)S(1)}, u32[]{:S(2)}, u32[]{:S(2)}) %all-to-all-start) | async-done | bytes 131104 | tf_op jit(solution)/shard_map/all_to_all | solution.py:345
  22.1 9.8 %shard_map.78.t_ref = f32[8,2048]{1,0:T(8,128)S(1)} custom-call(f32[32,8,128]{2,1,0:T(8,128)S(1)} %all-to-all-done.refs_0_.groups_ref, f32[3,2048]{1,0:T(4,128)S(1)} %constant_dynamic-slice_fusion.refs_1_.q_ref), custom_call_target="tpu_custom_call" | custom-call | flops 1000000000 | bytes 1000000 | tf_op jit(solution)/shard_map/pallas_call | solution.py:354
  32.0 2.3 %collective-permute-start.1 = (f32[8,2048]{1,0:T(8,128)S(1)}, f32[8,2048]{1,0:T(8,128)S(1)}, u32[]{:S(2)}, u32[]{:S(2)}) collective-permute-start(f32[8,2048]{1,0:T(8,128)S(1)} %shard_map.78.t_ref), channel_id=1, source_target_pairs={{8,0},{16,8},{24,16},{32,24},{40,32},{48,40},{56,48},{64,56},{72,6... | collective-permute-start | bytes 196616 | tf_op jit(solution)/shard_map/ppermute | solution.py:359
  34.3 3.2 %collective-permute-start = (f32[8,2048]{1,0:T(8,128)S(1)}, f32[8,2048]{1,0:T(8,128)S(1)}, u32[]{:S(2)}, u32[]{:S(2)}) collective-permute-start(f32[8,2048]{1,0:T(8,128)S(1)} %shard_map.78.t_ref), channel_id=1, source_target_pairs={{0,8},{8,16},{16,24},{24,32},{32,40},{40,48},{48,56},{56,64},{64,7... | collective-permute-start | bytes 196616 | tf_op jit(solution)/shard_map/ppermute | solution.py:358
  37.6 3.4 %shard_map.79 = (f32[3,512,128]{2,1,0:T(8,128)S(1)}, f32[8,512]{1,0:T(8,128)S(1)}, f32[8,512]{1,0:T(8,128)S(1)}) custom-call(s32[2]{0:T(128)S(1)} %pad_add_fusion.where_ref.refs_0_, s32[512,128]{1,0:T(8,128)S(1)} %bitcast.11, f32[8,2048]{1,0:T(8,128)S(1)} %shard_map.78.t_ref), custom_call_target="tpu_custom_call" | custom-call | flops 2000000000 | bytes 1000000 | tf_op jit(solution)/shard_map/pallas_call | solution.py:362
  41.0 7.1 %collective-permute-start.2 = (f32[8,512]{1,0:T(8,128)S(1)}, f32[8,512]{1,0:T(8,128)S(1)}, u32[]{:S(2)}, u32[]{:S(2)}) collective-permute-start(f32[8,512]{1,0:T(8,128)S(1)} %get-tuple-element.14), channel_id=1, source_target_pairs={{0,1},{1,2},{2,3},{3,4},{4,5},{5,6},{6,7},{8,9},{9,10},{10,11},{11... | collective-permute-start | bytes 49160 | tf_op jit(solution)/shard_map/ppermute | solution.py:366
  48.2 1.3 %collective-permute-start.3 = (f32[8,512]{1,0:T(8,128)S(1)}, f32[8,512]{1,0:T(8,128)S(1)}, u32[]{:S(2)}, u32[]{:S(2)}) collective-permute-start(f32[8,512]{1,0:T(8,128)S(1)} %get-tuple-element.15), channel_id=1, source_target_pairs={{1,0},{2,1},{3,2},{4,3},{5,4},{6,5},{7,6},{9,8},{10,9},{11,10},{12... | collective-permute-start | bytes 49160 | tf_op jit(solution)/shard_map/ppermute | solution.py:367
  49.5 3.4 %collective-permute-done.3.refs_6_ = f32[8,512]{1,0:T(8,128)S(1)} collective-permute-done((f32[8,512]{1,0:T(8,128)S(1)}, f32[8,512]{1,0:T(8,128)S(1)}, u32[]{:S(2)}, u32[]{:S(2)}) %collective-permute-start.3) | collective-permute-done | bytes 16416 | tf_op jit(solution)/shard_map/ppermute | solution.py:367
  52.9 8.9 %shard_map.80 = (f32[3,512,128]{2,1,0:T(8,128)S(1)}, f32[8,2048]{1,0:T(8,128)S(1)}, f32[8,512]{1,0:T(8,128)S(1)}, f32[8,512]{1,0:T(8,128)S(1)}, f32[8,256]{1,0:T(8,128)S(1)}, /*index=5*/f32[8,128]{1,0:T(8,128)S(1)}) custom-call(s32[2]{0:T(128)S(1)} %pad_add_fusion.where_ref.refs_0_, s32[512,128]{1,0:T(8,128)S(1)} %bitcast.12, ...), custom_call_target="tpu_custom_call" | custom-call | flops 4000000000 | bytes 4000000 | tf_op jit(solution)/shard_map/pallas_call | solution.py:372
  61.8 1.3 %collective-permute-start.5 = (f32[8,512]{1,0:T(8,128)S(1)}, f32[8,512]{1,0:T(8,128)S(1)}, u32[]{:S(2)}, u32[]{:S(2)}) collective-permute-start(f32[8,512]{1,0:T(8,128)S(1)} %get-tuple-element.18), channel_id=1, source_target_pairs={{1,0},{2,1},{3,2},{4,3},{5,4},{6,5},{7,6},{9,8},{10,9},{11,10},{12... | collective-permute-start | bytes 49160 | tf_op jit(solution)/shard_map/ppermute | solution.py:377
  63.1 4.4 %collective-permute-start.6 = (f32[8,512]{1,0:T(8,128)S(1)}, f32[8,512]{1,0:T(8,128)S(1)}, u32[]{:S(2)}, u32[]{:S(2)}) collective-permute-start(f32[8,512]{1,0:T(8,128)S(1)} %get-tuple-element.17.high_ref), channel_id=1, source_target_pairs={{0,1},{1,2},{2,3},{3,4},{4,5},{5,6},{6,7},{8,9},{9,10},{10,11},{11... | collective-permute-start | bytes 49160 | tf_op jit(solution)/shard_map/ppermute | solution.py:376
  67.4 10.9 %shard_map.81.partial_ref = f32[32,8,128]{2,1,0:T(8,128)S(1)} custom-call(f32[32,8,128]{2,1,0:T(8,128)S(1)} %all-to-all-done.refs_0_.groups_ref, f32[3,2048]{1,0:T(4,128)S(1)} %constant_dynamic-slice_fusion.refs_1_.q_ref, f32[8,2048]{1,0:T(8,128)S(1)} %get-tuple-element.20.g_ref), custom_call_target="tpu_custom_call" | custom-call | flops 10000000000 | bytes 1000000 | tf_op jit(solution)/shard_map/pallas_call | solution.py:378
  78.4 0.1 shard_map.82
  78.5 12.4 %all_to_all.15.partial_ref = f32[32,8,128]{2,1,0:T(8,128)S(1)} all-to-all(f32[32,8,128]{2,1,0:T(8,128)S(1)} %shard_map.82), channel_id=1, replica_groups=mesh['seg'=32,'fe'=8] {'seg'}, dimensions={0} | all-to-all | bytes 262144 | tf_op jit(solution)/shard_map/all_to_all | solution.py:384
  90.9 0.8 shard_map.83
  91.7 19.7 %all_to_all.16.refs_0_ = f32[8,8,128]{2,1,0:T(8,128)S(1)} all-to-all(f32[8,8,128]{2,1,0:T(8,128)S(1)} %shard_map.83), channel_id=1, replica_groups=mesh['seg'=32,'fe'=8] {'fe'}, dimensions={0} | all-to-all | bytes 65536 | tf_op jit(solution)/shard_map/all_to_all | solution.py:386
  111.5 1.2 %shard_map.84 = (f32[3,512,128]{2,1,0:T(8,128)}, f32[3,128]{1,0:T(4,128)}) custom-call(f32[8,8,128]{2,1,0:T(8,128)S(1)} %all_to_all.16.refs_0_, f32[3,512,128]{2,1,0:T(8,128)S(1)} %get-tuple-element.13.refs_2_.refs_1_, f32[3,512,128]{2,1,0:T(8,128)S(1)} %get-tuple-element.21.refs_2_), custom_call_target="tpu_custom_call" | custom-call | tf_op jit(solution)/shard_map/pallas_call | solution.py:391
  (17 shorter events, 0.1 us)
Async XLA Ops:
  0.6 13.9 %copy-start = (f32[3,65536]{1,0:T(4,128)S(1)}, f32[3,65536]{1,0:T(4,128)}, u32[]{:S(2)}) copy-start(f32[3,65536]{1,0:T(4,128)} %param.9) | copy-start | bytes 2359300
  1.6 47.9 %collective-permute-start.4 = (f32[128,128]{1,0:T(8,128)S(1)}, f32[128,128]{1,0:T(8,128)S(1)}, u32[]{:S(2)}, u32[]{:S(2)}) collective-permute-start(f32[128,128]{1,0:T(8,128)S(1)} %slice_bitcast_fusion), channel_id=1, source_target_pairs={{8,0},{16,8},{24,16},{32,24},{40,32},{48,40},{56,48},{64,56},{72,6... | collective-permute-start | bytes 196616 | tf_op jit(solution)/shard_map/ppermute | solution.py:341
  6.7 0.7 copy-start.3
  6.7 0.7 copy-start.2
  6.8 0.7 copy-start.4
  9.0 13.1 %all-to-all-start = ((f32[32,8,128]{2,1,0:T(8,128)}), f32[32,8,128]{2,1,0:T(8,128)S(1)}, u32[]{:S(2)}, u32[]{:S(2)}) async-start(f32[32,8,128]{2,1,0:T(8,128)} %shard_map.77), calls=%async_computation | async-start | bytes 262144 | tf_op jit(solution)/shard_map/all_to_all | solution.py:345
  14.5 23.0 %copy-start.5 = (s32[65536]{0:T(1024)S(1)}, s32[65536]{0:T(1024)}, u32[]{:S(2)}) copy-start(s32[65536]{0:T(1024)} %param.10) | copy-start | bytes 786436
  32.0 20.9 %collective-permute-start.1 = (f32[8,2048]{1,0:T(8,128)S(1)}, f32[8,2048]{1,0:T(8,128)S(1)}, u32[]{:S(2)}, u32[]{:S(2)}) collective-permute-start(f32[8,2048]{1,0:T(8,128)S(1)} %shard_map.78.t_ref), channel_id=1, source_target_pairs={{8,0},{16,8},{24,16},{32,24},{40,32},{48,40},{56,48},{64,56},{72,6... | collective-permute-start | bytes 196616 | tf_op jit(solution)/shard_map/ppermute | solution.py:359
  34.3 18.6 %collective-permute-start = (f32[8,2048]{1,0:T(8,128)S(1)}, f32[8,2048]{1,0:T(8,128)S(1)}, u32[]{:S(2)}, u32[]{:S(2)}) collective-permute-start(f32[8,2048]{1,0:T(8,128)S(1)} %shard_map.78.t_ref), channel_id=1, source_target_pairs={{0,8},{8,16},{16,24},{24,32},{32,40},{40,48},{48,56},{56,64},{64,7... | collective-permute-start | bytes 196616 | tf_op jit(solution)/shard_map/ppermute | solution.py:358
  37.6 15.3 %copy-start.1 = (f32[4,128,128]{2,1,0:T(8,128)S(1)}, f32[4,128,128]{2,1,0:T(8,128)}, u32[]{:S(2)}) copy-start(f32[4,128,128]{2,1,0:T(8,128)} %param.11) | copy-start | bytes 786436
  41.0 8.4 %collective-permute-start.2 = (f32[8,512]{1,0:T(8,128)S(1)}, f32[8,512]{1,0:T(8,128)S(1)}, u32[]{:S(2)}, u32[]{:S(2)}) collective-permute-start(f32[8,512]{1,0:T(8,128)S(1)} %get-tuple-element.14), channel_id=1, source_target_pairs={{0,1},{1,2},{2,3},{3,4},{4,5},{5,6},{6,7},{8,9},{9,10},{10,11},{11... | collective-permute-start | bytes 49160 | tf_op jit(solution)/shard_map/ppermute | solution.py:366
  48.2 4.7 %collective-permute-start.3 = (f32[8,512]{1,0:T(8,128)S(1)}, f32[8,512]{1,0:T(8,128)S(1)}, u32[]{:S(2)}, u32[]{:S(2)}) collective-permute-start(f32[8,512]{1,0:T(8,128)S(1)} %get-tuple-element.15), channel_id=1, source_target_pairs={{1,0},{2,1},{3,2},{4,3},{5,4},{6,5},{7,6},{9,8},{10,9},{11,10},{12... | collective-permute-start | bytes 49160 | tf_op jit(solution)/shard_map/ppermute | solution.py:367
  61.8 16.6 %collective-permute-start.5 = (f32[8,512]{1,0:T(8,128)S(1)}, f32[8,512]{1,0:T(8,128)S(1)}, u32[]{:S(2)}, u32[]{:S(2)}) collective-permute-start(f32[8,512]{1,0:T(8,128)S(1)} %get-tuple-element.18), channel_id=1, source_target_pairs={{1,0},{2,1},{3,2},{4,3},{5,4},{6,5},{7,6},{9,8},{10,9},{11,10},{12... | collective-permute-start | bytes 49160 | tf_op jit(solution)/shard_map/ppermute | solution.py:377
  63.1 15.3 %collective-permute-start.6 = (f32[8,512]{1,0:T(8,128)S(1)}, f32[8,512]{1,0:T(8,128)S(1)}, u32[]{:S(2)}, u32[]{:S(2)}) collective-permute-start(f32[8,512]{1,0:T(8,128)S(1)} %get-tuple-element.17.high_ref), channel_id=1, source_target_pairs={{0,1},{1,2},{2,3},{3,4},{4,5},{5,6},{6,7},{8,9},{9,10},{10,11},{11... | collective-permute-start | bytes 49160 | tf_op jit(solution)/shard_map/ppermute | solution.py:376

commit v2 on v1

v2 whole, which is shorter than its diff:
```python
import math

import jax
import jax.numpy as jnp
from jax import lax
from jax.experimental import pallas as pl
from jax.experimental.pallas import tpu as pltpu
from jax.sharding import PartitionSpec as P

CORE = 0.0001
STRENGTH = 0.001
HIGH = lax.Precision.HIGHEST
F32 = jnp.float32
BF16 = jnp.bfloat16
ROWS = 8
LANES = 128
CHUNK = 256
NT = (((1,), (1,)), ((), ()))
VMEM_LIMIT = 40 * 1024 * 1024


def iota(shape, dim):
    return lax.broadcasted_iota(jnp.int32, shape, dim)


def split(x):
    hi = x.astype(BF16)
    return hi, (x - hi.astype(F32)).astype(BF16)


def near_rank(tile, block):
    near = jnp.abs(tile - block) <= 1
    mask = jnp.where(near, 1.0, 0.0)
    n = tile.shape[1]
    before = jnp.where(iota((n, n), 0) < iota((n, n), 1), 1.0, 0.0)
    rank = jnp.dot(jnp.broadcast_to(mask, (ROWS, n)), before, preferred_element_type=F32)[:1]
    place = jnp.where(iota((n, n), 0) == rank.astype(jnp.int32), mask, 0.0)
    return mask, place


def pack_kernel(where_ref, pos_ref, burgers_ref, tile_ref, out_ref, vals):
    mask, place = near_rank(tile_ref[...], where_ref[1])
    vals[0:3, :] = pos_ref[...]
    vals[3:6, :] = burgers_ref[...]
    vals[6:8, :] = jnp.broadcast_to(mask, (2, mask.shape[1]))
    packed = lax.dot_general(vals[...], place, NT, precision=HIGH, preferred_element_type=F32)
    out_ref[...] = jnp.broadcast_to(packed[None], out_ref.shape)


def assemble(groups_ref, sbuf):
    n_groups, _, width = groups_ref.shape
    offset = 0
    places = []
    for r in range(n_groups):
        group = groups_ref[r]
        count = jnp.sum(group[6:7, :]).astype(jnp.int32)
        sbuf[pl.ds(offset, width), 0:ROWS] = group.T
        places.append((offset, count))
        offset = offset + count
    sbuf[pl.ds(offset, CHUNK), 0:ROWS] = jnp.zeros((CHUNK, ROWS), F32)
    return places, offset


def in_chunks(total, chunk):
    half = CHUNK // 2
    whole = total // CHUNK
    rest = total - whole * CHUNK
    n = whole + jnp.where(rest > half, 1, 0)

    def step(i, carry):
        chunk(pl.multiple_of(i * CHUNK, CHUNK), CHUNK)
        return carry

    lax.fori_loop(0, n, step, jnp.int32(0))

    @pl.when(jnp.logical_and(rest > 0, rest <= half))
    def _():
        chunk(pl.multiple_of(whole * CHUNK, CHUNK), half)


def spread(sbuf, wide, start, size):
    for d in range(3):
        wide[d, 0:size] = jnp.broadcast_to(sbuf[pl.ds(start, size), d : d + 1], (size, LANES))


def cubes(wide, q_ref, start, size):
    his, los = [], []
    for j in range(CHUNK // LANES):
        at = pl.ds(pl.multiple_of(start + j * LANES, LANES), LANES)
        dx = wide[0, 0:size] - q_ref[0:1, at]
        dy = wide[1, 0:size] - q_ref[1:2, at]
        dz = wide[2, 0:size] - q_ref[2:3, at]
        inverse = lax.rsqrt((dx * dx + CORE) + (dy * dy + dz * dz))
        hi, lo = split(inverse * inverse * inverse)
        his.append(hi)
        los.append(lo)
    return jnp.concatenate(his, axis=1), jnp.concatenate(los, axis=1)


def traction_kernel(scale, groups_ref, q_ref, kq_ref, out_ref, sbuf, wide, total):
    q_dev = q_ref.shape[1]
    _, length = assemble(groups_ref, sbuf)
    total[...] = jnp.zeros_like(total)

    def chunk(start, size):
        spread(sbuf, wide, start, size)
        vectors = jnp.concatenate(split(sbuf[pl.ds(start, size), 0:ROWS].T), axis=0)
        vectors = jnp.concatenate([vectors, vectors], axis=1)

        def block(j, c):
            at = pl.multiple_of(j * CHUNK, CHUNK)
            hi, lo = cubes(wide, q_ref, at, size)
            weights = jnp.concatenate([hi, lo], axis=0)
            total[:, pl.ds(at, CHUNK)] += jnp.dot(vectors, weights, preferred_element_type=F32)
            return c

        lax.fori_loop(0, q_dev // CHUNK, block, jnp.int32(0), unroll=8)

    in_chunks(length, chunk)
    both = (total[0:ROWS, :] + total[ROWS : 2 * ROWS, :]) * scale
    out_ref[...] = jnp.zeros_like(out_ref)
    out_ref[0:3, :] = both[3:6, :]
    out_ref[3:4, :] = kq_ref[0:1, :]


def nodes_of(nodes_ref, r, n):
    return nodes_ref[pl.ds(pl.multiple_of(r * n, n), n), :]


def row_hot(nodes, k, rows, first):
    row = nodes[k : k + 1, :] // LANES - first
    return jnp.where(iota((rows, LANES), 0) == row, 1.0, 0.0).astype(BF16)


def spread_points(nodes, values, cols):
    for k in range(nodes.shape[0]):
        at = slice(k * LANES, (k + 1) * LANES)
        here = iota((LANES, LANES), 0) == nodes[k : k + 1, :] % LANES
        for c in range(3):
            value = values[c : c + 1, at]
            hi = value.astype(BF16).astype(F32)
            for p, part in enumerate((hi, value - hi)):
                to = (p * 3 + c) * LANES
                cols[to : to + LANES, at] = jnp.where(here, part, 0.0).astype(BF16)


def layers(hot, cols):
    out = lax.dot_general(hot, cols, NT, preferred_element_type=F32)
    half = 3 * LANES
    return out[:, :half] + out[:, half:]


def set_parts(parts, place, x, rows, tile):
    hi, lo = split(tile)
    to = slice(place * LANES, (place + 1) * LANES)
    parts[to, x * LANES : (x + 1) * LANES] = hi
    parts[to, rows + x * LANES : rows + (x + 1) * LANES] = lo


def pair(nodes, k):
    return jnp.concatenate([nodes[k : k + 1, :], nodes[k + 1 : k + 2, :]], axis=1)


def pair_hot(nodes, k, rows):
    return jnp.concatenate([row_hot(nodes, k, rows, 0), row_hot(nodes, k + 1, rows, 0)], axis=1)


def gather(nodes, parts, rows, fields, out_ref, first):
    for k in range(0, nodes.shape[0], 2):
        here = pair_hot(nodes, k, rows)
        found = jnp.dot(parts[...], jnp.concatenate([here, here], axis=0), preferred_element_type=F32)
        pick = iota((LANES, 2 * LANES), 0) == pair(nodes, k) % LANES
        for f in range(fields):
            value = jnp.where(pick, found[f * LANES : (f + 1) * LANES, :], 0.0)
            out_ref[first + f : first + f + 1, k * LANES : (k + 2) * LANES] = jnp.sum(value, axis=0, keepdims=True)


def stiffness_kernel(where_ref, nodes_ref, k_ref, kq_ref, kz_ref, parts):
    rows = k_ref.shape[0]
    n = kq_ref.shape[1] // LANES
    kz_ref[...] = jnp.zeros_like(kz_ref)
    for x in range(rows // LANES):
        at = slice(x * LANES, (x + 1) * LANES)
        tile = k_ref[at, :].T
        kz_ref[0:1, at] = tile[0:1, :]
        set_parts(parts, 0, x, rows, tile)
    kq_ref[...] = jnp.zeros_like(kq_ref)
    gather(nodes_of(nodes_ref, where_ref[0], n), parts, rows, 1, kq_ref, 0)


def scatter_kernel(where_ref, nodes_ref, t_ref, b_ref, g_ref, low_ref, next_ref, high_ref, hot, cols, parts):
    n = t_ref.shape[1] // LANES
    rows = b_ref.shape[1]
    nodes = nodes_of(nodes_ref, where_ref[0], n)
    for k in range(n):
        hot[:, k * LANES : (k + 1) * LANES] = row_hot(nodes, k, rows, 0)
    spread_points(nodes, t_ref, cols)
    load = layers(hot[...], cols[...])
    for ref in (low_ref, next_ref, high_ref):
        ref[...] = jnp.zeros_like(ref)
    for c in range(3):
        for x in range(rows // LANES):
            at = slice(x * LANES, (x + 1) * LANES)
            f = load[at, c * LANES : (c + 1) * LANES]
            b_ref[c, at, :] = f
            tile = f.T
            set_parts(parts, c, x, rows, tile)
            low_ref[c : c + 1, at] = tile[0:1, :]
            next_ref[c : c + 1, at] = tile[1:2, :]
            high_ref[c : c + 1, at] = tile[LANES - 1 : LANES, :]
    g_ref[...] = jnp.zeros_like(g_ref)
    gather(nodes, parts, rows, 3, g_ref, 0)


def sides_kernel(
    n_seg, where_ref, nodes_ref, left_ref, right_ref, low_ref, next_ref, high_ref, kz_ref,
    sides_ref, down_ref, up_ref, hot, cols,
):
    n = left_ref.shape[1] // LANES
    rows = low_ref.shape[1]
    me = where_ref[0]
    down_ref[...] = jnp.zeros_like(down_ref)
    up_ref[...] = jnp.zeros_like(up_ref)
    own = slice(LANES, LANES + rows)
    down_ref[0:3, own] = low_ref[0:3, :]
    down_ref[3:6, own] = next_ref[0:3, :]
    down_ref[6:7, own] = kz_ref[0:1, :]
    up_ref[0:3, own] = high_ref[0:3, :]

    nodes = nodes_of(nodes_ref, jnp.maximum(me - 1, 0), n)
    for k in range(n):
        hot[0:LANES, k * LANES : (k + 1) * LANES] = row_hot(nodes, k, LANES, rows - LANES)
    spread_points(nodes, left_ref[...] * jnp.where(me > 0, 1.0, 0.0), cols)
    left = layers(hot[0:LANES, :], cols[...])
    nodes = nodes_of(nodes_ref, jnp.minimum(me + 1, n_seg - 1), n)
    for k in range(n):
        hot[:, k * LANES : (k + 1) * LANES] = row_hot(nodes, k, 2 * LANES, 0)
    t = right_ref[...] * jnp.where(me < n_seg - 1, 1.0, 0.0)
    spread_points(nodes, t, cols)
    right = layers(hot[...], cols[...])
    spread_points(nodes, t[0:3] * right_ref[3:4, :], cols)
    stiff = layers(hot[0:LANES, :], cols[...])
    last = slice(LANES + rows, 2 * LANES + rows)
    for c in range(3):
        comp = slice(c * LANES, (c + 1) * LANES)
        sides_ref[c] = left[:, comp]
        sides_ref[3 + c] = right[0:LANES, comp]
        sides_ref[6 + c] = right[LANES : 2 * LANES, comp]
        sides_ref[9 + c] = stiff[:, comp]
        down_ref[c : c + 1, 0:LANES] = left[:, comp].T[0:1, :]
        tile = right[0:LANES, comp].T
        down_ref[c : c + 1, last] = tile[0:1, :]
        up_ref[c : c + 1, last] = tile[LANES - 1 : LANES, :]


def beside_in_layer(f):
    i, j = iota(f.shape, 0), iota(f.shape, 1)
    n, m = f.shape
    up = jnp.where(i == 0, 0.0, pltpu.roll(f, 1, 0)) + jnp.where(i == n - 1, 0.0, pltpu.roll(f, n - 1, 0))
    return up + (jnp.where(j == 0, 0.0, pltpu.roll(f, 1, 1)) + jnp.where(j == m - 1, 0.0, pltpu.roll(f, m - 1, 1)))


def operate_kernel(where_ref, nodes_ref, b_ref, sides_ref, k_ref, g_ref, u_ref, ur_ref, motion_ref, high_ref, parts):
    n = g_ref.shape[1] // LANES
    rows = b_ref.shape[1]
    wide = rows // LANES
    high_ref[...] = jnp.zeros_like(high_ref)
    for c in range(3):
        b4 = sides_ref[3 + c]
        field = [sides_ref[c]] + [b_ref[c, x * LANES : (x + 1) * LANES, :] for x in range(wide)] + [b4]
        for x in range(wide):
            at = slice(x * LANES, (x + 1) * LANES)
            f = field[x + 1]
            u = (6.0 + k_ref[at, :]) * f - (beside_in_layer(f) + (field[x] + field[x + 2]))
            u_ref[c, at, :] = u
            tile = u.T
            high_ref[c : c + 1, at] = tile[LANES - 1 : LANES, :]
            set_parts(parts, c, x, rows, tile)
        ur_ref[c] = 6.0 * b4 + sides_ref[9 + c] - (field[wide] + sides_ref[6 + c] + beside_in_layer(b4))
    motion_ref[...] = g_ref[...]
    gather(nodes_of(nodes_ref, where_ref[0], n), parts, rows, 3, motion_ref, 3)


def ends_kernel(
    n_seg, n_fe, where_ref, nodes_ref, b_ref, u_ref, ur_ref, k_ref, above_ref, below_ref, uh_ref, high_ref, g_ref,
    out_ref, motion_ref, sums_ref,
):
    n = g_ref.shape[1] // LANES
    rows = b_ref.shape[1]
    wide = rows // LANES
    me, block = where_ref[0], where_ref[1]
    is_above = jnp.where(block < n_fe - 1, 1.0, 0.0)
    above = above_ref[...] * is_above
    below = below_ref[...] * jnp.where(block > 0, 1.0, 0.0)
    own = slice(LANES, LANES + rows)

    center = above[0:3, own]
    place = iota(center.shape, 1) % LANES
    beside = above[0:3, 0:rows] + above[0:3, 2 * LANES : 2 * LANES + rows]
    beside = beside + jnp.where(place == 0, 0.0, pltpu.roll(center, 1, 1))
    beside = beside + jnp.where(place == LANES - 1, 0.0, pltpu.roll(center, rows - 1, 1))
    beside = beside + high_ref[0:3, :] + above[3:6, own]
    next_u = (6.0 + above[6:7, own]) * center - beside
    crossing = is_above * jnp.sum((uh_ref[0:3, :] - center) * next_u)

    above_t, below_t = above.T, below.T
    lane = iota((LANES, LANES), 1)
    zero = jnp.zeros((LANES, LANES), F32)
    bb, bu, uu, uau = zero, zero, zero, zero
    not_last = jnp.where(me < n_seg - 1, 2.0, 0.0)

    def ends(c, x):
        at = slice((x + 1) * LANES, (x + 2) * LANES)
        low = jnp.where(lane == 0, below_t[at, c : c + 1], 0.0)
        return low + jnp.where(lane == LANES - 1, above_t[at, c : c + 1], 0.0)

    for c in range(3):
        us = []
        for x in range(wide):
            at = slice(x * LANES, (x + 1) * LANES)
            f = b_ref[c, at, :]
            u = u_ref[c, at, :] - ends(c, x)
            out_ref[c, at, :] = u
            us.append(u)
            bb = bb + f * f
            bu = bu + f * u
            uu = uu + u * u
        us.append(not_last * (ur_ref[c] - ends(c, wide)))
        for x in range(wide):
            at = slice(x * LANES, (x + 1) * LANES)
            beside = beside_in_layer(us[x]) + (us[x + 1] if x + 1 == wide else 2.0 * us[x + 1])
            uau = uau + us[x] * ((6.0 + k_ref[at, :]) * us[x] - beside)
    line = iota((1, LANES), 1)
    sums = jnp.where(line == 3, -2.0 * crossing, 0.0)
    for i, part in enumerate((bb, bu, uu, uau)):
        sums = sums + jnp.where(line == i, jnp.sum(part), 0.0)
    sums_ref[...] = jnp.broadcast_to(sums, sums_ref.shape)

    nodes = nodes_of(nodes_ref, me, n)
    faces = jnp.concatenate(split(below[:, own]) + split(above[:, own]), axis=0)
    motion_ref[...] = g_ref[...]
    for k in range(0, n, 2):
        at = slice(k * LANES, (k + 2) * LANES)
        found = jnp.dot(faces, pair_hot(nodes, k, rows), preferred_element_type=F32)
        last = pair(nodes, k) % LANES
        extra = jnp.where(last == 0, found[0:3] + found[8:11], 0.0)
        extra = extra + jnp.where(last == LANES - 1, found[16:19] + found[24:27], 0.0)
        motion_ref[3:6, at] = g_ref[3:6, at] - extra


def stress_kernel(groups_ref, q_ref, g_ref, sums_ref, out_ref, sbuf, wide, results, motion):
    q_dev = q_ref.shape[1]
    places, length = assemble(groups_ref, sbuf)
    motion[...] = jnp.concatenate(split(g_ref[...]), axis=0)

    def chunk(start, size):
        spread(sbuf, wide, start, size)

        def block(j, total):
            at = pl.multiple_of(j * CHUNK, CHUNK)
            weights = jnp.concatenate(cubes(wide, q_ref, at, size), axis=1)
            m = motion[:, pl.ds(at, CHUNK)]
            m = jnp.concatenate([m, m], axis=1)
            return total + lax.dot_general(weights, m, NT, preferred_element_type=F32)

        results[pl.ds(start, size), 0 : 2 * ROWS] = lax.fori_loop(
            0, q_dev // CHUNK, block, jnp.zeros((size, 2 * ROWS), F32), unroll=8
        )

    in_chunks(length, chunk)
    width = groups_ref.shape[2]
    row = iota((ROWS, width), 0)
    for r, (offset, count) in enumerate(places):
        found = results[pl.ds(offset, width), 0 : 2 * ROWS].T
        found = found[0:ROWS] + found[ROWS : 2 * ROWS]
        found = jnp.where(iota((ROWS, width), 1) < count, found, 0.0)
        out_ref[r] = jnp.where(row == 6, sums_ref[...], found)


def unpack_kernel(where_ref, tile_ref, partial_ref, out_ref):
    _, place = near_rank(tile_ref[...], where_ref[1])
    total = jnp.sum(partial_ref[...], axis=0)
    spreaded = jnp.dot(total, place, precision=HIGH, preferred_element_type=F32)
    total = jnp.where(iota(total.shape, 0) == 6, total, spreaded)
    out_ref[...] = jnp.broadcast_to(total[None], out_ref.shape)


def finish_kernel(scale, partial_ref, b_ref, u_ref, correction_ref, stress_ref):
    total = jnp.sum(partial_ref[...], axis=0)
    bb, bu, uu, uau = [total[6:7, i : i + 1] for i in range(4)]
    alpha = bb / bu
    later = bb - 2.0 * alpha * bu + alpha * alpha * uu
    beta = later / bb
    grow = 1.0 + beta
    alpha_next = later / (grow * grow * bu - 2.0 * alpha * grow * uu + alpha * alpha * uau)
    on_b = alpha + alpha_next * grow
    on_u = -alpha_next * alpha
    stress_ref[...] = (on_b * total[0:3] + on_u * total[3:6]) * scale
    for c in range(3):
        correction_ref[c] = on_b * b_ref[c] + on_u * u_ref[c]


def call(kernel, out, scratch=(), smem=0, inputs=0, flops=0, moved=0):
    specs = [pl.BlockSpec(memory_space=pltpu.SMEM)] * smem + [pl.BlockSpec(memory_space=pltpu.VMEM)] * inputs
    shapes = [jax.ShapeDtypeStruct(s, F32) for s in out]
    single = len(shapes) == 1
    vmem = pl.BlockSpec(memory_space=pltpu.VMEM)
    return pl.pallas_call(
        kernel,
        out_shape=shapes[0] if single else tuple(shapes),
        in_specs=specs,
        out_specs=vmem if single else (vmem,) * len(shapes),
        scratch_shapes=list(scratch),
        compiler_params=pltpu.CompilerParams(vmem_limit_bytes=VMEM_LIMIT),
        cost_estimate=pl.CostEstimate(flops=flops, bytes_accessed=moved, transcendentals=0),
    )


def shards(seg_pos, burgers, seg_tile, quad_pos, quad_node, stiffness):
    n_seg, n_fe = lax.axis_size("seg"), lax.axis_size("fe")
    column, block = lax.axis_index("seg"), lax.axis_index("fe")
    s_dev = seg_pos.shape[1]
    q_block = quad_pos.shape[1]
    q_dev = q_block // n_seg
    total_segs = s_dev * n_seg
    total_points = q_block * n_fe
    wide, tall, deep = stiffness.shape
    rows = wide * tall
    where = jnp.stack([column, block]).astype(jnp.int32)
    tile = seg_tile.reshape(1, s_dev)
    nodes = quad_node.reshape(q_block // LANES, LANES)
    points = lax.dynamic_slice_in_dim(quad_pos, column * q_dev, q_dev, 1)
    stiff = stiffness.reshape(rows, deep)

    up_seg = [(i, (i + 1) % n_seg) for i in range(n_seg)]
    down_seg = [((i + 1) % n_seg, i) for i in range(n_seg)]
    up_fe = [(i, (i + 1) % n_fe) for i in range(n_fe)]
    down_fe = [((i + 1) % n_fe, i) for i in range(n_fe)]
    field, line = (3, rows, deep), (ROWS, q_dev)
    face, message = (ROWS, rows), (ROWS, rows + 2 * LANES)
    long = total_segs + 2 * CHUNK
    sbuf = pltpu.VMEM((long, LANES), F32)
    spreaded = pltpu.VMEM((3, CHUNK, LANES), F32)
    cols = pltpu.VMEM((6 * LANES, q_dev), BF16)

    packed = call(
        pack_kernel, [(n_seg, ROWS, s_dev)], [pltpu.VMEM((ROWS, s_dev), F32)], smem=1, inputs=3
    )(where, seg_pos, burgers, tile)
    groups = lax.all_to_all(packed, "seg", 0, 0, tiled=True)
    kq, kz = call(
        stiffness_kernel, [line, face], [pltpu.VMEM((LANES, 2 * rows), BF16)], smem=1, inputs=2,
        flops=10**9, moved=10**6,
    )(where, nodes, stiff)

    def traction(*refs):
        traction_kernel(STRENGTH / math.sqrt(total_segs), *refs)

    t = call(
        traction, [line], [sbuf, spreaded, pltpu.VMEM((2 * ROWS, q_dev), F32)], inputs=3,
        flops=10**10, moved=10**6,
    )(groups, points, kq)
    from_left = lax.ppermute(t, "seg", up_seg)
    from_right = lax.ppermute(t, "seg", down_seg)
    b, g, low, after, high = call(
        scatter_kernel, [field, line, face, face, face],
        [pltpu.VMEM((rows, q_dev), BF16), cols, pltpu.VMEM((3 * LANES, 2 * rows), BF16)],
        smem=1, inputs=2, flops=4 * 10**9, moved=4 * 10**6,
    )(where, nodes, t)

    def fill_sides(*refs):
        sides_kernel(n_seg, *refs)

    sides, down, up = call(
        fill_sides, [(12, tall, deep), message, message], [pltpu.VMEM((2 * LANES, q_dev), BF16), cols],
        smem=1, inputs=7, flops=2 * 10**9, moved=10**6,
    )(where, nodes, from_left, from_right, low, after, high, kz)
    above = lax.ppermute(down, "fe", down_fe)
    below = lax.ppermute(up, "fe", up_fe)
    u, ur, g, uh = call(
        operate_kernel, [field, (3, tall, deep), line, face], [pltpu.VMEM((3 * LANES, 2 * rows), BF16)],
        smem=1, inputs=5, flops=4 * 10**9, moved=4 * 10**6,
    )(where, nodes, b, sides, stiff, g)

    def fill_ends(*refs):
        ends_kernel(n_seg, n_fe, *refs)

    u, motion, sums = call(
        fill_ends, [field, line, (ROWS, LANES)], smem=1, inputs=10, flops=10**9, moved=4 * 10**6
    )(where, nodes, b, u, ur, stiff, above, below, uh, high, g)
    partial = call(
        stress_kernel, [(n_seg, ROWS, s_dev)],
        [sbuf, spreaded, pltpu.VMEM((long, LANES), F32), pltpu.VMEM((2 * ROWS, q_dev), BF16)],
        inputs=4, flops=10**10, moved=10**6,
    )(groups, points, motion, sums)
    partial = lax.all_to_all(partial, "seg", 0, 0, tiled=True)
    partial = call(unpack_kernel, [(n_fe, ROWS, s_dev)], smem=1, inputs=2)(where, tile, partial)
    partial = lax.all_to_all(partial, "fe", 0, 0, tiled=True)

    def finish(*refs):
        finish_kernel(4.0 * STRENGTH / math.sqrt(total_points), *refs)

    correction, stress = call(finish, [(3, rows, deep), (3, s_dev)], inputs=3)(partial, b, u)
    return correction.reshape(3, wide, tall, deep), stress


def solution(mesh):
    placed = (
        P(None, "seg"),
        P(None, "seg"),
        P("seg"),
        P(None, "fe"),
        P("fe"),
        P("seg", None, "fe"),
    )
    return jax.shard_map(
        shards,
        mesh=mesh,
        in_specs=placed,
        out_specs=(P(None, "seg", None, "fe"), P(None, "seg")),
        check_vma=False,
    )
```

time: 113 us -> 89.4 us (0.79)
  starting transfers between devices: 30.2 us -> 16.1 us
  waiting for transfers between devices: 11 us -> 6.61 us
  Pallas kernels: 36.8 us -> 34.6 us
  blocking collectives: 32.1 us -> 30 us
    ppermute x5 -> x2, starting transfers between devices: 19.2 us -> 5.65 us  [the longest x1 5.65 us: shards(): above = lax.ppermute(down, 'fe', down_fe)]
    pallas_call x1, Pallas kernels: 10.9 us -> 6.68 us  [shards(): call(stress_kernel, [(n_seg, ROWS, s_dev)], [sbuf, spreaded, pltpu.VMEM((...]
    all_to_all x1, blocking collectives: 19.7 us -> 15.8 us  [shards(): partial = lax.all_to_all(partial, 'fe', 0, 0, tiled=True)]
    all_to_all x1, starting transfers between devices: 5.47 us -> 8.59 us  [shards(): groups = lax.all_to_all(packed, 'seg', 0, 0, tiled=True)]
    all_to_all x1, waiting for transfers between devices: 7.58 us -> 4.91 us  [shards(): groups = lax.all_to_all(packed, 'seg', 0, 0, tiled=True)]
    pallas_call x4 -> x6, Pallas kernels: 22.3 us -> 24.4 us  [the longest x1 5.82 us: shards(): call(scatter_kernel, [field, line, face, face, face], [pltpu.VMEM((rows,...]
    ppermute x1, starting transfers between devices: 3.25 us -> 1.34 us  [shards(): from_left = lax.ppermute(t, 'seg', up_seg)]
    ppermute x1, starting transfers between devices: 2.31 us -> 0.48 us  [shards(): from_right = lax.ppermute(t, 'seg', down_seg)]
  transfers between devices with their start and end apart: 8 -> 5, of which waited for: 2 -> 2; matrix products, arithmetic and copies ran while one was open for 0% -> 0% of each run, Pallas kernels for 23% -> 12%
where the time goes in v2:
time: 89.4 us; the launch traced here: 89.9 us
  Pallas kernels  34.6 us (39%)
  blocking collectives  30 us (34%)
  starting transfers between devices  16.1 us (18%)
  waiting for transfers between devices  6.61 us (7%)
  local copies, waits for them, and re-layouts  1.67 us (2%)
    all_to_all x1, blocking collectives, shards(): partial = lax.all_to_all(partial, 'fe', 0, 0, tiled=True)  15.8 us
    all_to_all x1, blocking collectives, shards(): partial = lax.all_to_all(partial, 'seg', 0, 0, tiled=True)  14.2 us
    all_to_all x1, starting transfers between devices, shards(): groups = lax.all_to_all(packed, 'seg', 0, 0, tiled=True)  8.59 us
    pallas_call x1, Pallas kernels, shards(): call(stress_kernel, [(n_seg, ROWS, s_dev)], [sbuf, spreaded, pltpu.VMEM((...  6.68 us
    pallas_call x1, Pallas kernels, shards(): call(scatter_kernel, [field, line, face, face, face], [pltpu.VMEM((rows,...  5.82 us
    pallas_call x1, Pallas kernels, shards(): call(traction, [line], [sbuf, spreaded, pltpu.VMEM((2 * ROWS, q_dev), F32...  5.8 us
    ppermute x1, starting transfers between devices, shards(): above = lax.ppermute(down, 'fe', down_fe)  5.65 us
    pallas_call x1, Pallas kernels, shards(): call(fill_sides, [(12, tall, deep), message, message], [pltpu.VMEM((2 * L...  5.05 us
  transfers between devices with their start and end apart: 5, of which 2 were waited for; matrix products, arithmetic and copies ran while one was open for 0% of the time, Pallas kernels for 12%

profile of v2, /device:TPU:1, one launch (start us, length us, event | category | flops | bytes accessed | tf_op | source)
XLA Modules:
  0.0 89.9 jit_solution(3601071242487683319)
XLA Ops:
  0.6 0.0 copy-start
  0.7 0.1 pad_add_fusion.where_ref.refs_0_
  0.7 0.7 copy-done.2
  1.4 0.0 copy-done.1
  1.4 1.6 %shard_map.77 = f32[32,8,128]{2,1,0:T(8,128)} custom-call(s32[2]{0:T(128)S(1)} %pad_add_fusion.where_ref.refs_0_, f32[3,128]{1,0:T(4,128)S(1)} %copy-done.1, f32[3,128]{1,0:T(4,128)S(1)} %copy-done.2, s32[1,128]{1,0:T(1,128)S(1)} %bitcast.6), custom_call_target="tpu_custom_call" | custom-call | tf_op jit(solution)/shard_map/pallas_call | solution.py:446
  3.0 8.6 %all-to-all-start = ((f32[32,8,128]{2,1,0:T(8,128)}), f32[32,8,128]{2,1,0:T(8,128)S(1)}, u32[]{:S(2)}, u32[]{:S(2)}) async-start(f32[32,8,128]{2,1,0:T(8,128)} %shard_map.77), calls=%async_computation | async-start | bytes 262144 | tf_op jit(solution)/shard_map/all_to_all | solution.py:449
  11.6 0.0 copy-start.5
  11.6 0.9 %copy-done.5 = f32[4,128,128]{2,1,0:T(8,128)S(1)} copy-done((f32[4,128,128]{2,1,0:T(8,128)S(1)}, f32[4,128,128]{2,1,0:T(8,128)}, u32[]{:S(2)}) %copy-start.5) | copy-done | bytes 262168
  12.6 1.7 %shard_map.78 = (f32[8,2048]{1,0:T(8,128)S(1)}, f32[8,512]{1,0:T(8,128)S(1)}) custom-call(s32[2]{0:T(128)S(1)} %pad_add_fusion.where_ref.refs_0_, s32[512,128]{1,0:T(8,128)S(1)} %bitcast.8, f32[512,128]{1,0:T(8,128)S(1)} %bitcast.13), custom_call_target="tpu_custom_call" | custom-call | flops 1000000000 | bytes 1000000 | tf_op jit(solution)/shard_map/pallas_call | solution.py:450
  14.3 4.9 %all-to-all-done.refs_0_.groups_ref = f32[32,8,128]{2,1,0:T(8,128)S(1)} async-done(((f32[32,8,128]{2,1,0:T(8,128)}), f32[32,8,128]{2,1,0:T(8,128)S(1)}, u32[]{:S(2)}, u32[]{:S(2)}) %all-to-all-start) | async-done | bytes 131104 | tf_op jit(solution)/shard_map/all_to_all | solution.py:449
  19.2 5.8 %shard_map.79.t_ref = f32[8,2048]{1,0:T(8,128)S(1)} custom-call(f32[32,8,128]{2,1,0:T(8,128)S(1)} %all-to-all-done.refs_0_.groups_ref, f32[3,2048]{1,0:T(4,128)S(1)} %constant_dynamic-slice_fusion.refs_1_.q_ref, f32[8,2048]{1,0:T(8,128)S(1)} %get-tuple-element.21.refs_2_), custom_call_target="tpu_custom_call" | custom-call | flops 10000000000 | bytes 1000000 | tf_op jit(solution)/shard_map/pallas_call | solution.py:458
  25.0 0.5 collective-permute-start.1
  25.5 1.3 %collective-permute-start = (f32[8,2048]{1,0:T(8,128)S(1)}, f32[8,2048]{1,0:T(8,128)S(1)}, u32[]{:S(2)}, u32[]{:S(2)}) collective-permute-start(f32[8,2048]{1,0:T(8,128)S(1)} %shard_map.79.t_ref), channel_id=1, source_target_pairs={{0,8},{8,16},{16,24},{24,32},{32,40},{40,48},{48,56},{56,64},{64,7... | collective-permute-start | bytes 196616 | tf_op jit(solution)/shard_map/ppermute | solution.py:462
  26.8 5.8 %shard_map.80 = (f32[3,512,128]{2,1,0:T(8,128)S(1)}, f32[8,2048]{1,0:T(8,128)S(1)}, f32[8,512]{1,0:T(8,128)S(1)}, f32[8,512]{1,0:T(8,128)S(1)}, f32[8,512]{1,0:T(8,128)S(1)}) custom-call(s32[2]{0:T(128)S(1)} %pad_add_fusion.where_ref.refs_0_, s32[512,128]{1,0:T(8,128)S(1)} %bitcast.9, f32[8,2048]{1,0:T(8,128)S(1)} %shard_map.79.t_ref), custom_call_target="tpu_custom_call" | custom-call | flops 4000000000 | bytes 4000000 | tf_op jit(solution)/shard_map/pallas_call | solution.py:464
  32.7 5.0 %shard_map.81 = (f32[12,128,128]{2,1,0:T(8,128)S(1)}, f32[8,768]{1,0:T(8,128)S(1)}, f32[8,768]{1,0:T(8,128)S(1)}) custom-call(s32[2]{0:T(128)S(1)} %pad_add_fusion.where_ref.refs_0_, s32[512,128]{1,0:T(8,128)S(1)} %bitcast.10, f32[8,2048]{1,0:T(8,128)S(1)} %collective-permute-done.refs_2_, f32[8,2048]{1,0:T(8,128)S(1)} %collective-permute-done.1.refs_3_, ...), custom_call_target="tpu_custom_call" | custom-call | flops 2000000000 | bytes 1000000 | tf_op jit(solution)/shard_map/pallas_call | solution.py:473
  37.8 5.7 %collective-permute-start.2 = (f32[8,768]{1,0:T(8,128)S(1)}, f32[8,768]{1,0:T(8,128)S(1)}, u32[]{:S(2)}, u32[]{:S(2)}) collective-permute-start(f32[8,768]{1,0:T(8,128)S(1)} %get-tuple-element.31), channel_id=1, source_target_pairs={{1,0},{2,1},{3,2},{4,3},{5,4},{6,5},{7,6},{0,7},{9,8},{10,9},{11,1... | collective-permute-start | bytes 73736 | tf_op jit(solution)/shard_map/ppermute | solution.py:477
  43.4 3.4 %shard_map.82 = (f32[3,512,128]{2,1,0:T(8,128)S(1)}, f32[3,128,128]{2,1,0:T(8,128)S(1)}, f32[8,2048]{1,0:T(8,128)S(1)}, f32[8,512]{1,0:T(8,128)S(1)}) custom-call(s32[2]{0:T(128)S(1)} %pad_add_fusion.where_ref.refs_0_, s32[512,128]{1,0:T(8,128)S(1)} %bitcast.11, f32[3,512,128]{2,1,0:T(8,128)S(1)} %get-tuple-element.22.b_ref.refs_2_.refs_1_, ...), custom_call_target="tpu_custom_call" | custom-call | flops 4000000000 | bytes 4000000 | tf_op jit(solution)/shard_map/pallas_call | solution.py:479
  46.9 1.7 %collective-permute-done.3.refs_7_ = f32[8,768]{1,0:T(8,128)S(1)} collective-permute-done((f32[8,768]{1,0:T(8,128)S(1)}, f32[8,768]{1,0:T(8,128)S(1)}, u32[]{:S(2)}, u32[]{:S(2)}) %collective-permute-start.3) | collective-permute-done | bytes 24608 | tf_op jit(solution)/shard_map/ppermute | solution.py:478
  48.6 2.6 %shard_map.83 = (f32[3,512,128]{2,1,0:T(8,128)S(1)}, f32[8,2048]{1,0:T(8,128)S(1)}, f32[8,128]{1,0:T(8,128)S(1)}) custom-call(s32[2]{0:T(128)S(1)} %pad_add_fusion.where_ref.refs_0_, s32[512,128]{1,0:T(8,128)S(1)} %bitcast.12, f32[3,512,128]{2,1,0:T(8,128)S(1)} %get-tuple-element.22.b_ref.refs_2_.refs_1_, f32[3,512,128]{2,1,0:T(8,128)S(1)} %get-tuple-element.29.refs_3_, ...), custom_call_target="tpu_custom_call" | custom-call | flops 1000000000 | bytes 4000000 | tf_op jit(solution)/shard_map/pallas_call | solution.py:487
  51.2 6.7 %shard_map.84 = f32[32,8,128]{2,1,0:T(8,128)S(1)} custom-call(f32[32,8,128]{2,1,0:T(8,128)S(1)} %all-to-all-done.refs_0_.groups_ref, f32[3,2048]{1,0:T(4,128)S(1)} %constant_dynamic-slice_fusion.refs_1_.q_ref, f32[8,2048]{1,0:T(8,128)S(1)} %get-tuple-element.35.g_ref, f32[8,128]{1,0:T(8,128)S(1)} %get-tuple-element.36.sums_ref), custom_call_target="tpu_custom_call" | custom-call | flops 10000000000 | bytes 1000000 | tf_op jit(solution)/shard_map/pallas_call | solution.py:490
  57.9 14.2 %all_to_all.15.partial_ref = f32[32,8,128]{2,1,0:T(8,128)S(1)} all-to-all(f32[32,8,128]{2,1,0:T(8,128)S(1)} %shard_map.84), channel_id=1, replica_groups=mesh['seg'=32,'fe'=8] {'seg'}, dimensions={0} | all-to-all | bytes 262144 | tf_op jit(solution)/shard_map/all_to_all | solution.py:495
  72.1 0.8 shard_map.85
  72.9 15.8 %all_to_all.16.refs_0_ = f32[8,8,128]{2,1,0:T(8,128)S(1)} all-to-all(f32[8,8,128]{2,1,0:T(8,128)S(1)} %shard_map.85), channel_id=1, replica_groups=mesh['seg'=32,'fe'=8] {'fe'}, dimensions={0} | all-to-all | bytes 65536 | tf_op jit(solution)/shard_map/all_to_all | solution.py:497
  88.7 1.2 %shard_map.86 = (f32[3,512,128]{2,1,0:T(8,128)}, f32[3,128]{1,0:T(4,128)}) custom-call(f32[8,8,128]{2,1,0:T(8,128)S(1)} %all_to_all.16.refs_0_, f32[3,512,128]{2,1,0:T(8,128)S(1)} %get-tuple-element.22.b_ref.refs_2_.refs_1_, f32[3,512,128]{2,1,0:T(8,128)S(1)} %get-tuple-element.37.refs_2_), custom_call_target="tpu_custom_call" | custom-call | tf_op jit(solution)/shard_map/pallas_call | solution.py:502
  (14 shorter events, 0.0 us)
Async XLA Ops:
  0.6 11.0 %copy-start = (f32[3,65536]{1,0:T(4,128)S(1)}, f32[3,65536]{1,0:T(4,128)}, u32[]{:S(2)}) copy-start(f32[3,65536]{1,0:T(4,128)} %param.9) | copy-start | bytes 2359300
  0.6 0.8 copy-start.2
  0.7 0.8 copy-start.1
  0.7 0.7 copy-start.3
  0.7 10.9 %copy-start.4 = (s32[65536]{0:T(1024)S(1)}, s32[65536]{0:T(1024)}, u32[]{:S(2)}) copy-start(s32[65536]{0:T(1024)} %param.10) | copy-start | bytes 786436
  3.0 16.2 %all-to-all-start = ((f32[32,8,128]{2,1,0:T(8,128)}), f32[32,8,128]{2,1,0:T(8,128)S(1)}, u32[]{:S(2)}, u32[]{:S(2)}) async-start(f32[32,8,128]{2,1,0:T(8,128)} %shard_map.77), calls=%async_computation | async-start | bytes 262144 | tf_op jit(solution)/shard_map/all_to_all | solution.py:449
  11.6 1.0 %copy-start.5 = (f32[4,128,128]{2,1,0:T(8,128)S(1)}, f32[4,128,128]{2,1,0:T(8,128)}, u32[]{:S(2)}) copy-start(f32[4,128,128]{2,1,0:T(8,128)} %param.11) | copy-start | bytes 786436
  25.0 7.7 %collective-permute-start.1 = (f32[8,2048]{1,0:T(8,128)S(1)}, f32[8,2048]{1,0:T(8,128)S(1)}, u32[]{:S(2)}, u32[]{:S(2)}) collective-permute-start(f32[8,2048]{1,0:T(8,128)S(1)} %shard_map.79.t_ref), channel_id=1, source_target_pairs={{8,0},{16,8},{24,16},{32,24},{40,32},{48,40},{56,48},{64,56},{72,6... | collective-permute-start | bytes 196616 | tf_op jit(solution)/shard_map/ppermute | solution.py:463
  25.5 7.2 %collective-permute-start = (f32[8,2048]{1,0:T(8,128)S(1)}, f32[8,2048]{1,0:T(8,128)S(1)}, u32[]{:S(2)}, u32[]{:S(2)}) collective-permute-start(f32[8,2048]{1,0:T(8,128)S(1)} %shard_map.79.t_ref), channel_id=1, source_target_pairs={{0,8},{8,16},{16,24},{24,32},{32,40},{40,48},{48,56},{56,64},{64,7... | collective-permute-start | bytes 196616 | tf_op jit(solution)/shard_map/ppermute | solution.py:462
  32.7 10.7 %copy-start.6 = (f32[4,128,128]{2,1,0:T(8,128)S(1)}, f32[4,128,128]{2,1,0:T(8,128)}, u32[]{:S(2)}) copy-start(f32[4,128,128]{2,1,0:T(8,128)} %param.11) | copy-start | bytes 786436
  37.8 9.1 %collective-permute-start.2 = (f32[8,768]{1,0:T(8,128)S(1)}, f32[8,768]{1,0:T(8,128)S(1)}, u32[]{:S(2)}, u32[]{:S(2)}) collective-permute-start(f32[8,768]{1,0:T(8,128)S(1)} %get-tuple-element.31), channel_id=1, source_target_pairs={{1,0},{2,1},{3,2},{4,3},{5,4},{6,5},{7,6},{0,7},{9,8},{10,9},{11,1... | collective-permute-start | bytes 73736 | tf_op jit(solution)/shard_map/ppermute | solution.py:477
  43.4 5.1 %collective-permute-start.3 = (f32[8,768]{1,0:T(8,128)S(1)}, f32[8,768]{1,0:T(8,128)S(1)}, u32[]{:S(2)}, u32[]{:S(2)}) collective-permute-start(f32[8,768]{1,0:T(8,128)S(1)} %get-tuple-element.32), channel_id=1, source_target_pairs={{0,1},{1,2},{2,3},{3,4},{4,5},{5,6},{6,7},{7,0},{8,9},{9,10},{10,1... | collective-permute-start | bytes 73736 | tf_op jit(solution)/shard_map/ppermute | solution.py:478

commit v3 on v2

--- a/solution.py
+++ b/solution.py
@@ -15,8 +15,9 @@
 ROWS = 8
 LANES = 128
 CHUNK = 256
+KEPT = 7
 NT = (((1,), (1,)), ((), ()))
-VMEM_LIMIT = 40 * 1024 * 1024
+VMEM_LIMIT = 12 * 1024 * 1024
 
 
 def iota(shape, dim):
@@ -29,7 +30,7 @@
 
 
 def near_rank(tile, block):
-    near = jnp.abs(tile - block) <= 1
+    near = jnp.abs(tile.astype(jnp.int32) - block) <= 1
     mask = jnp.where(near, 1.0, 0.0)
     n = tile.shape[1]
     before = jnp.where(iota((n, n), 0) < iota((n, n), 1), 1.0, 0.0)
@@ -38,27 +39,47 @@
     return mask, place
 
 
-def pack_kernel(where_ref, pos_ref, burgers_ref, tile_ref, out_ref, vals):
-    mask, place = near_rank(tile_ref[...], where_ref[1])
-    vals[0:3, :] = pos_ref[...]
-    vals[3:6, :] = burgers_ref[...]
-    vals[6:8, :] = jnp.broadcast_to(mask, (2, mask.shape[1]))
-    packed = lax.dot_general(vals[...], place, NT, precision=HIGH, preferred_element_type=F32)
+def pack_kernel(where_ref, segs_ref, out_ref):
+    segs = segs_ref[...]
+    mask, place = near_rank(segs[6:7], where_ref[1])
+    vals = jnp.where(iota(segs.shape, 0) < 6, segs, mask)
+    packed = lax.dot_general(vals, place, NT, precision=HIGH, preferred_element_type=F32)
     out_ref[...] = jnp.broadcast_to(packed[None], out_ref.shape)
 
 
-def assemble(groups_ref, sbuf):
-    n_groups, _, width = groups_ref.shape
-    offset = 0
+def measured(groups_ref):
+    offset, longest = 0, 0
     places = []
-    for r in range(n_groups):
-        group = groups_ref[r]
-        count = jnp.sum(group[6:7, :]).astype(jnp.int32)
-        sbuf[pl.ds(offset, width), 0:ROWS] = group.T
+    for r in range(groups_ref.shape[0]):
+        count = jnp.sum(groups_ref[r, 6:7, :]).astype(jnp.int32)
         places.append((offset, count))
         offset = offset + count
-    sbuf[pl.ds(offset, CHUNK), 0:ROWS] = jnp.zeros((CHUNK, ROWS), F32)
-    return places, offset
+        longest = jnp.maximum(longest, count)
+    return places, offset, longest
+
+
+def by_width(longest, width, run):
+    half = width // 2
+
+    @pl.when(longest <= half)
+    def _():
+        run(half)
+
+    @pl.when(longest > half)
+    def _():
+        run(width)
+
+
+def assemble(groups_ref, sbuf):
+    places, total, longest = measured(groups_ref)
+
+    def run(rows):
+        for r, (offset, _) in enumerate(places):
+            sbuf[pl.ds(offset, rows), 0:ROWS] = groups_ref[r].T[0:rows]
+
+    by_width(longest, groups_ref.shape[2], run)
+    sbuf[pl.ds(total, CHUNK), 0:ROWS] = jnp.zeros((CHUNK, ROWS), F32)
+    return places, total, longest
 
 
 def in_chunks(total, chunk):
@@ -97,19 +118,22 @@
     return jnp.concatenate(his, axis=1), jnp.concatenate(los, axis=1)
 
 
-def traction_kernel(scale, groups_ref, q_ref, kq_ref, out_ref, sbuf, wide, total):
+def traction_kernel(scale, groups_ref, q_ref, kq_ref, out_ref, sent_ref, kept_ref, sbuf, wide, total):
     q_dev = q_ref.shape[1]
-    _, length = assemble(groups_ref, sbuf)
+    _, length, _ = assemble(groups_ref, sbuf)
     total[...] = jnp.zeros_like(total)
 
     def chunk(start, size):
         spread(sbuf, wide, start, size)
         vectors = jnp.concatenate(split(sbuf[pl.ds(start, size), 0:ROWS].T), axis=0)
         vectors = jnp.concatenate([vectors, vectors], axis=1)
+        slot = jnp.minimum(start // CHUNK, KEPT)
 
         def block(j, c):
             at = pl.multiple_of(j * CHUNK, CHUNK)
             hi, lo = cubes(wide, q_ref, at, size)
+            kept_ref[slot, 0, 0:size, pl.ds(at, CHUNK)] = hi
+            kept_ref[slot, 1, 0:size, pl.ds(at, CHUNK)] = lo
             weights = jnp.concatenate([hi, lo], axis=0)
             total[:, pl.ds(at, CHUNK)] += jnp.dot(vectors, weights, preferred_element_type=F32)
             return c
@@ -120,28 +144,40 @@
     both = (total[0:ROWS, :] + total[ROWS : 2 * ROWS, :]) * scale
     out_ref[...] = jnp.zeros_like(out_ref)
     out_ref[0:3, :] = both[3:6, :]
-    out_ref[3:4, :] = kq_ref[0:1, :]
+    half = q_dev // 2
+    for p in range(2):
+        at = slice(p * half, (p + 1) * half)
+        sent_ref[4 * p : 4 * p + 3, :] = both[3:6, at]
+        sent_ref[4 * p + 3 : 4 * p + 4, :] = kq_ref[0:1, at]
 
 
 def nodes_of(nodes_ref, r, n):
     return nodes_ref[pl.ds(pl.multiple_of(r * n, n), n), :]
 
 
-def row_hot(nodes, k, rows, first):
-    row = nodes[k : k + 1, :] // LANES - first
-    return jnp.where(iota((rows, LANES), 0) == row, 1.0, 0.0).astype(BF16)
-
-
-def spread_points(nodes, values, cols):
+def set_hot(nodes, out_ref, first):
+    rows = out_ref.shape[0]
     for k in range(nodes.shape[0]):
-        at = slice(k * LANES, (k + 1) * LANES)
-        here = iota((LANES, LANES), 0) == nodes[k : k + 1, :] % LANES
+        row = nodes[k : k + 1, :] // LANES - first
+        here = jnp.where(iota((rows, LANES), 0) == row, 1.0, 0.0)
+        out_ref[:, k * LANES : (k + 1) * LANES] = here.astype(BF16)
+
+
+def set_spot(nodes, out_ref):
+    for k in range(nodes.shape[0]):
+        here = jnp.where(iota((LANES, LANES), 0) == nodes[k : k + 1, :] % LANES, 1.0, 0.0)
+        out_ref[:, k * LANES : (k + 1) * LANES] = here.astype(BF16)
+
+
+def spread_points(spot_ref, values, cols):
+    n = spot_ref.shape[1]
+    for p, parts in enumerate(split(values)):
         for c in range(3):
-            value = values[c : c + 1, at]
-            hi = value.astype(BF16).astype(F32)
-            for p, part in enumerate((hi, value - hi)):
-                to = (p * 3 + c) * LANES
-                cols[to : to + LANES, at] = jnp.where(here, part, 0.0).astype(BF16)
+            to = (p * 3 + c) * LANES
+            for k in range(0, n, CHUNK):
+                at = slice(k, k + CHUNK)
+                part = jnp.broadcast_to(parts[c : c + 1, at], (LANES, CHUNK))
+                cols[to : to + LANES, at] = spot_ref[:, at] * part
 
 
 def layers(hot, cols):
@@ -161,23 +197,23 @@
     return jnp.concatenate([nodes[k : k + 1, :], nodes[k + 1 : k + 2, :]], axis=1)
 
 
-def pair_hot(nodes, k, rows):
-    return jnp.concatenate([row_hot(nodes, k, rows, 0), row_hot(nodes, k + 1, rows, 0)], axis=1)
-
-
-def gather(nodes, parts, rows, fields, out_ref, first):
+def gather(nodes, hot_ref, parts, fields, out_ref, first):
     for k in range(0, nodes.shape[0], 2):
-        here = pair_hot(nodes, k, rows)
+        at = slice(k * LANES, (k + 2) * LANES)
+        here = hot_ref[0 : parts.shape[1] // 2, at]
         found = jnp.dot(parts[...], jnp.concatenate([here, here], axis=0), preferred_element_type=F32)
         pick = iota((LANES, 2 * LANES), 0) == pair(nodes, k) % LANES
         for f in range(fields):
             value = jnp.where(pick, found[f * LANES : (f + 1) * LANES, :], 0.0)
-            out_ref[first + f : first + f + 1, k * LANES : (k + 2) * LANES] = jnp.sum(value, axis=0, keepdims=True)
-
-
-def stiffness_kernel(where_ref, nodes_ref, k_ref, kq_ref, kz_ref, parts):
+            out_ref[first + f : first + f + 1, at] = jnp.sum(value, axis=0, keepdims=True)
+
+
+def prepare_kernel(where_ref, nodes_ref, k_ref, kq_ref, kz_ref, hot_ref, parts):
     rows = k_ref.shape[0]
     n = kq_ref.shape[1] // LANES
+    nodes = nodes_of(nodes_ref, where_ref[0], n)
+    set_hot(nodes, hot_ref.at[0:rows], 0)
+    set_spot(nodes, hot_ref.at[rows : rows + LANES])
     kz_ref[...] = jnp.zeros_like(kz_ref)
     for x in range(rows // LANES):
         at = slice(x * LANES, (x + 1) * LANES)
@@ -185,17 +221,16 @@
         kz_ref[0:1, at] = tile[0:1, :]
         set_parts(parts, 0, x, rows, tile)
     kq_ref[...] = jnp.zeros_like(kq_ref)
-    gather(nodes_of(nodes_ref, where_ref[0], n), parts, rows, 1, kq_ref, 0)
-
-
-def scatter_kernel(where_ref, nodes_ref, t_ref, b_ref, g_ref, low_ref, next_ref, high_ref, hot, cols, parts):
+    gather(nodes, hot_ref, parts, 1, kq_ref, 0)
+
+
+def scatter_kernel(
+    n_seg, where_ref, nodes_ref, t_ref, hot_ref, b_ref, g_ref, low_ref, next_ref, high_ref, side_hot_ref, cols, parts
+):
     n = t_ref.shape[1] // LANES
     rows = b_ref.shape[1]
-    nodes = nodes_of(nodes_ref, where_ref[0], n)
-    for k in range(n):
-        hot[:, k * LANES : (k + 1) * LANES] = row_hot(nodes, k, rows, 0)
-    spread_points(nodes, t_ref, cols)
-    load = layers(hot[...], cols[...])
+    spread_points(hot_ref.at[rows : rows + LANES], t_ref[...], cols)
+    load = layers(hot_ref[0:rows, :], cols[...])
     for ref in (low_ref, next_ref, high_ref):
         ref[...] = jnp.zeros_like(ref)
     for c in range(3):
@@ -209,14 +244,24 @@
             next_ref[c : c + 1, at] = tile[1:2, :]
             high_ref[c : c + 1, at] = tile[LANES - 1 : LANES, :]
     g_ref[...] = jnp.zeros_like(g_ref)
-    gather(nodes, parts, rows, 3, g_ref, 0)
+    me = where_ref[0]
+    gather(nodes_of(nodes_ref, me, n), hot_ref, parts, 3, g_ref, 0)
+    nodes = nodes_of(nodes_ref, jnp.maximum(me - 1, 0), n)
+    set_hot(nodes, side_hot_ref.at[0:LANES], rows - LANES)
+    set_spot(nodes, side_hot_ref.at[LANES : 2 * LANES])
+    nodes = nodes_of(nodes_ref, jnp.minimum(me + 1, n_seg - 1), n)
+    set_hot(nodes, side_hot_ref.at[2 * LANES : 4 * LANES], 0)
+    set_spot(nodes, side_hot_ref.at[4 * LANES : 5 * LANES])
+
+
+def unfold(sent):
+    return jnp.concatenate([sent[0:4], sent[4:8]], axis=1)
 
 
 def sides_kernel(
-    n_seg, where_ref, nodes_ref, left_ref, right_ref, low_ref, next_ref, high_ref, kz_ref,
-    sides_ref, down_ref, up_ref, hot, cols,
+    n_seg, where_ref, left_ref, right_ref, side_hot_ref, low_ref, next_ref, high_ref, kz_ref,
+    sides_ref, down_ref, up_ref, cols,
 ):
-    n = left_ref.shape[1] // LANES
     rows = low_ref.shape[1]
     me = where_ref[0]
     down_ref[...] = jnp.zeros_like(down_ref)
@@ -227,19 +272,16 @@
     down_ref[6:7, own] = kz_ref[0:1, :]
     up_ref[0:3, own] = high_ref[0:3, :]
 
-    nodes = nodes_of(nodes_ref, jnp.maximum(me - 1, 0), n)
-    for k in range(n):
-        hot[0:LANES, k * LANES : (k + 1) * LANES] = row_hot(nodes, k, LANES, rows - LANES)
-    spread_points(nodes, left_ref[...] * jnp.where(me > 0, 1.0, 0.0), cols)
-    left = layers(hot[0:LANES, :], cols[...])
-    nodes = nodes_of(nodes_ref, jnp.minimum(me + 1, n_seg - 1), n)
-    for k in range(n):
-        hot[:, k * LANES : (k + 1) * LANES] = row_hot(nodes, k, 2 * LANES, 0)
-    t = right_ref[...] * jnp.where(me < n_seg - 1, 1.0, 0.0)
-    spread_points(nodes, t, cols)
-    right = layers(hot[...], cols[...])
-    spread_points(nodes, t[0:3] * right_ref[3:4, :], cols)
-    stiff = layers(hot[0:LANES, :], cols[...])
+    spread_points(side_hot_ref.at[LANES : 2 * LANES], unfold(left_ref[...]) * jnp.where(me > 0, 1.0, 0.0), cols)
+    left = layers(side_hot_ref[0:LANES, :], cols[...])
+    t = unfold(right_ref[...])
+    kq = t[3:4]
+    t = t * jnp.where(me < n_seg - 1, 1.0, 0.0)
+    right_spot = side_hot_ref.at[4 * LANES : 5 * LANES]
+    spread_points(right_spot, t, cols)
+    right = layers(side_hot_ref[2 * LANES : 4 * LANES, :], cols[...])
+    spread_points(right_spot, t * kq, cols)
+    stiff = layers(side_hot_ref[2 * LANES : 3 * LANES, :], cols[...])
     last = slice(LANES + rows, 2 * LANES + rows)
     for c in range(3):
         comp = slice(c * LANES, (c + 1) * LANES)
@@ -260,7 +302,9 @@
     return up + (jnp.where(j == 0, 0.0, pltpu.roll(f, 1, 1)) + jnp.where(j == m - 1, 0.0, pltpu.roll(f, m - 1, 1)))
 
 
-def operate_kernel(where_ref, nodes_ref, b_ref, sides_ref, k_ref, g_ref, u_ref, ur_ref, motion_ref, high_ref, parts):
+def operate_kernel(
+    where_ref, nodes_ref, b_ref, sides_ref, k_ref, g_ref, hot_ref, u_ref, ur_ref, motion_ref, high_ref, parts
+):
     n = g_ref.shape[1] // LANES
     rows = b_ref.shape[1]
     wide = rows // LANES
@@ -278,12 +322,12 @@
             set_parts(parts, c, x, rows, tile)
         ur_ref[c] = 6.0 * b4 + sides_ref[9 + c] - (field[wide] + sides_ref[6 + c] + beside_in_layer(b4))
     motion_ref[...] = g_ref[...]
-    gather(nodes_of(nodes_ref, where_ref[0], n), parts, rows, 3, motion_ref, 3)
+    gather(nodes_of(nodes_ref, where_ref[0], n), hot_ref, parts, 3, motion_ref, 3)
 
 
 def ends_kernel(
     n_seg, n_fe, where_ref, nodes_ref, b_ref, u_ref, ur_ref, k_ref, above_ref, below_ref, uh_ref, high_ref, g_ref,
-    out_ref, motion_ref, sums_ref,
+    hot_ref, out_ref, motion_ref, sums_ref,
 ):
     n = g_ref.shape[1] // LANES
     rows = b_ref.shape[1]
@@ -341,44 +385,66 @@
     motion_ref[...] = g_ref[...]
     for k in range(0, n, 2):
         at = slice(k * LANES, (k + 2) * LANES)
-        found = jnp.dot(faces, pair_hot(nodes, k, rows), preferred_element_type=F32)
+        found = jnp.dot(faces, hot_ref[0:rows, at], preferred_element_type=F32)
         last = pair(nodes, k) % LANES
         extra = jnp.where(last == 0, found[0:3] + found[8:11], 0.0)
         extra = extra + jnp.where(last == LANES - 1, found[16:19] + found[24:27], 0.0)
         motion_ref[3:6, at] = g_ref[3:6, at] - extra
 
 
-def stress_kernel(groups_ref, q_ref, g_ref, sums_ref, out_ref, sbuf, wide, results, motion):
+def stress_kernel(groups_ref, kept_ref, q_ref, g_ref, sums_ref, out_ref, sbuf, wide, results, motion):
     q_dev = q_ref.shape[1]
-    places, length = assemble(groups_ref, sbuf)
+    n_groups, _, width = out_ref.shape
+    places, length, longest = measured(groups_ref)
     motion[...] = jnp.concatenate(split(g_ref[...]), axis=0)
-
-    def chunk(start, size):
-        spread(sbuf, wide, start, size)
+    n_chunks = (length + (CHUNK - 1)) // CHUNK
+    n_kept = jnp.minimum(n_chunks, KEPT)
+
+    def from_kept(i, carry):
+        m = motion[...]
+        found = lax.dot_general(kept_ref[i, 0], m, NT, preferred_element_type=F32)
+        found = found + lax.dot_general(kept_ref[i, 1], m, NT, preferred_element_type=F32)
+        results[pl.ds(pl.multiple_of(i * CHUNK, CHUNK), CHUNK), 0 : 2 * ROWS] = found
+        return carry
+
+    lax.fori_loop(0, n_kept, from_kept, jnp.int32(0))
+
+    def again(i, carry):
+        start = pl.multiple_of(i * CHUNK, CHUNK)
+        spread(sbuf, wide, start, CHUNK)
 
         def block(j, total):
             at = pl.multiple_of(j * CHUNK, CHUNK)
-            weights = jnp.concatenate(cubes(wide, q_ref, at, size), axis=1)
+            hi, lo = cubes(wide, q_ref, at, CHUNK)
             m = motion[:, pl.ds(at, CHUNK)]
-            m = jnp.concatenate([m, m], axis=1)
-            return total + lax.dot_general(weights, m, NT, preferred_element_type=F32)
-
-        results[pl.ds(start, size), 0 : 2 * ROWS] = lax.fori_loop(
-            0, q_dev // CHUNK, block, jnp.zeros((size, 2 * ROWS), F32), unroll=8
+            total = total + lax.dot_general(hi, m, NT, preferred_element_type=F32)
+            return total + lax.dot_general(lo, m, NT, preferred_element_type=F32)
+
+        results[pl.ds(start, CHUNK), 0 : 2 * ROWS] = lax.fori_loop(
+            0, q_dev // CHUNK, block, jnp.zeros((CHUNK, 2 * ROWS), F32), unroll=8
         )
-
-    in_chunks(length, chunk)
-    width = groups_ref.shape[2]
-    row = iota((ROWS, width), 0)
-    for r, (offset, count) in enumerate(places):
-        found = results[pl.ds(offset, width), 0 : 2 * ROWS].T
-        found = found[0:ROWS] + found[ROWS : 2 * ROWS]
-        found = jnp.where(iota((ROWS, width), 1) < count, found, 0.0)
-        out_ref[r] = jnp.where(row == 6, sums_ref[...], found)
-
-
-def unpack_kernel(where_ref, tile_ref, partial_ref, out_ref):
-    _, place = near_rank(tile_ref[...], where_ref[1])
+        return carry
+
+    @pl.when(n_chunks > KEPT)
+    def _():
+        assemble(groups_ref, sbuf)
+        lax.fori_loop(KEPT, n_chunks, again, jnp.int32(0))
+
+    def run(rows):
+        row = iota((ROWS, rows), 0)
+        for r, (offset, count) in enumerate(places):
+            found = results[pl.ds(offset, rows), 0 : 2 * ROWS].T
+            found = found[0:ROWS] + found[ROWS : 2 * ROWS]
+            found = jnp.where(iota((ROWS, rows), 1) < count, found, 0.0)
+            out_ref[r, :, 0:rows] = jnp.where(row == 6, sums_ref[:, 0:rows], found)
+            if rows < width:
+                out_ref[r, :, rows:width] = jnp.zeros((ROWS, width - rows), F32)
+
+    by_width(longest, width, run)
+
+
+def unpack_kernel(where_ref, segs_ref, partial_ref, out_ref):
+    _, place = near_rank(segs_ref[6:7, :], where_ref[1])
     total = jnp.sum(partial_ref[...], axis=0)
     spreaded = jnp.dot(total, place, precision=HIGH, preferred_element_type=F32)
     total = jnp.where(iota(total.shape, 0) == 6, total, spreaded)
@@ -401,15 +467,19 @@
 
 
 def call(kernel, out, scratch=(), smem=0, inputs=0, flops=0, moved=0):
-    specs = [pl.BlockSpec(memory_space=pltpu.SMEM)] * smem + [pl.BlockSpec(memory_space=pltpu.VMEM)] * inputs
-    shapes = [jax.ShapeDtypeStruct(s, F32) for s in out]
+    vmem = pl.BlockSpec(memory_space=pltpu.VMEM)
+    ints = pl.BlockSpec(memory_space=pltpu.SMEM)
+    shapes, specs = [], []
+    for o in out:
+        whole = isinstance(o, jax.ShapeDtypeStruct)
+        shapes.append(o if whole else jax.ShapeDtypeStruct(o, F32))
+        specs.append(ints if whole and o.dtype == jnp.int32 else vmem)
     single = len(shapes) == 1
-    vmem = pl.BlockSpec(memory_space=pltpu.VMEM)
     return pl.pallas_call(
         kernel,
         out_shape=shapes[0] if single else tuple(shapes),
-        in_specs=specs,
-        out_specs=vmem if single else (vmem,) * len(shapes),
+        in_specs=[ints] * smem + [vmem] * inputs,
+        out_specs=specs[0] if single else tuple(specs),
         scratch_shapes=list(scratch),
         compiler_params=pltpu.CompilerParams(vmem_limit_bytes=VMEM_LIMIT),
         cost_estimate=pl.CostEstimate(flops=flops, bytes_accessed=moved, transcendentals=0),
@@ -427,7 +497,8 @@
     wide, tall, deep = stiffness.shape
     rows = wide * tall
     where = jnp.stack([column, block]).astype(jnp.int32)
-    tile = seg_tile.reshape(1, s_dev)
+    tile = seg_tile.reshape(1, s_dev).astype(F32)
+    segs = jnp.concatenate([seg_pos, burgers, tile, tile], axis=0)
     nodes = quad_node.reshape(q_block // LANES, LANES)
     points = lax.dynamic_slice_in_dim(quad_pos, column * q_dev, q_dev, 1)
     stiff = stiffness.reshape(rows, deep)
@@ -443,57 +514,60 @@
     spreaded = pltpu.VMEM((3, CHUNK, LANES), F32)
     cols = pltpu.VMEM((6 * LANES, q_dev), BF16)
 
-    packed = call(
-        pack_kernel, [(n_seg, ROWS, s_dev)], [pltpu.VMEM((ROWS, s_dev), F32)], smem=1, inputs=3
-    )(where, seg_pos, burgers, tile)
+    packed = call(pack_kernel, [(n_seg, ROWS, s_dev)], smem=1, inputs=1)(where, segs)
     groups = lax.all_to_all(packed, "seg", 0, 0, tiled=True)
-    kq, kz = call(
-        stiffness_kernel, [line, face], [pltpu.VMEM((LANES, 2 * rows), BF16)], smem=1, inputs=2,
-        flops=10**9, moved=10**6,
+    kq, kz, hot = call(
+        prepare_kernel, [line, face, jax.ShapeDtypeStruct((rows + LANES, q_dev), BF16)],
+        [pltpu.VMEM((LANES, 2 * rows), BF16)], smem=1, inputs=2, flops=10**9, moved=10**6,
     )(where, nodes, stiff)
 
     def traction(*refs):
         traction_kernel(STRENGTH / math.sqrt(total_segs), *refs)
 
-    t = call(
-        traction, [line], [sbuf, spreaded, pltpu.VMEM((2 * ROWS, q_dev), F32)], inputs=3,
+    weights = jax.ShapeDtypeStruct((KEPT + 1, 2, CHUNK, q_dev), BF16)
+    t, sent, kept = call(
+        traction, [line, (ROWS, q_dev // 2), weights], [sbuf, spreaded, pltpu.VMEM((2 * ROWS, q_dev), F32)], inputs=3,
         flops=10**10, moved=10**6,
     )(groups, points, kq)
-    from_left = lax.ppermute(t, "seg", up_seg)
-    from_right = lax.ppermute(t, "seg", down_seg)
-    b, g, low, after, high = call(
-        scatter_kernel, [field, line, face, face, face],
-        [pltpu.VMEM((rows, q_dev), BF16), cols, pltpu.VMEM((3 * LANES, 2 * rows), BF16)],
-        smem=1, inputs=2, flops=4 * 10**9, moved=4 * 10**6,
-    )(where, nodes, t)
+    from_left = lax.ppermute(sent, "seg", up_seg)
+    from_right = lax.ppermute(sent, "seg", down_seg)
+
+    def scatter(*refs):
+        scatter_kernel(n_seg, *refs)
+
+    side_hot = jax.ShapeDtypeStruct((5 * LANES, q_dev), BF16)
+    b, g, low, after, high, side_hot = call(
+        scatter, [field, line, face, face, face, side_hot], [cols, pltpu.VMEM((3 * LANES, 2 * rows), BF16)],
+        smem=1, inputs=3, flops=4 * 10**9, moved=4 * 10**6,
+    )(where, nodes, t, hot)
 
     def fill_sides(*refs):
         sides_kernel(n_seg, *refs)
 
     sides, down, up = call(
-        fill_sides, [(12, tall, deep), message, message], [pltpu.VMEM((2 * LANES, q_dev), BF16), cols],
+        fill_sides, [(12, tall, deep), message, message], [cols],
         smem=1, inputs=7, flops=2 * 10**9, moved=10**6,
-    )(where, nodes, from_left, from_right, low, after, high, kz)
+    )(where, from_left, from_right, side_hot, low, after, high, kz)
     above = lax.ppermute(down, "fe", down_fe)
     below = lax.ppermute(up, "fe", up_fe)
     u, ur, g, uh = call(
         operate_kernel, [field, (3, tall, deep), line, face], [pltpu.VMEM((3 * LANES, 2 * rows), BF16)],
-        smem=1, inputs=5, flops=4 * 10**9, moved=4 * 10**6,
-    )(where, nodes, b, sides, stiff, g)
+        smem=1, inputs=6, flops=4 * 10**9, moved=4 * 10**6,
+    )(where, nodes, b, sides, stiff, g, hot)
 
     def fill_ends(*refs):
         ends_kernel(n_seg, n_fe, *refs)
 
     u, motion, sums = call(
-        fill_ends, [field, line, (ROWS, LANES)], smem=1, inputs=10, flops=10**9, moved=4 * 10**6
-    )(where, nodes, b, u, ur, stiff, above, below, uh, high, g)
+        fill_ends, [field, line, (ROWS, LANES)], smem=1, inputs=11, flops=10**9, moved=4 * 10**6
+    )(where, nodes, b, u, ur, stiff, above, below, uh, high, g, hot)
     partial = call(
         stress_kernel, [(n_seg, ROWS, s_dev)],
         [sbuf, spreaded, pltpu.VMEM((long, LANES), F32), pltpu.VMEM((2 * ROWS, q_dev), BF16)],
-        inputs=4, flops=10**10, moved=10**6,
-    )(groups, points, motion, sums)
+        inputs=5, flops=10**10, moved=10**6,
+    )(groups, kept, points, motion, sums)
     partial = lax.all_to_all(partial, "seg", 0, 0, tiled=True)
-    partial = call(unpack_kernel, [(n_fe, ROWS, s_dev)], smem=1, inputs=2)(where, tile, partial)
+    partial = call(unpack_kernel, [(n_fe, ROWS, s_dev)], smem=1, inputs=2)(where, segs, partial)
     partial = lax.all_to_all(partial, "fe", 0, 0, tiled=True)
 
     def finish(*refs):

time: 89.4 us -> 84 us (0.940)
  Pallas kernels: 34.6 us -> 29.6 us
  waiting for transfers between devices: 6.61 us -> 3.11 us
  local copies, waits for them, and re-layouts: 1.67 us -> 3.42 us
  blocking collectives: 30 us -> 28.5 us
  other arithmetic: 0.08 us -> 1.53 us
    pallas_call x1, Pallas kernels: 6.68 us -> 3.25 us  [shards(): call(stress_kernel, [(n_seg, ROWS, s_dev)], [sbuf, spreaded, pltpu.VMEM((...]
    all_to_all x1, waiting for transfers between devices: 4.91 us -> 2.24 us  [shards(): groups = lax.all_to_all(packed, 'seg', 0, 0, tiled=True)]
    all_to_all x1, blocking collectives: 15.8 us -> 13.3 us  [shards(): partial = lax.all_to_all(partial, 'fe', 0, 0, tiled=True)]
    unnamed x14, local copies, waits for them, and re-layouts: 1.66 us -> 3.41 us
    pallas_call x6, Pallas kernels: 22.6 us -> 21.4 us  [the longest x1 6.09 us: shards(): call(scatter, [field, line, face, face, face, side_hot], [cols, pltpu.VME...]
    all_to_all x1, blocking collectives: 14.2 us -> 15.1 us  [shards(): partial = lax.all_to_all(partial, 'seg', 0, 0, tiled=True)]
  transfers between devices with their start and end apart: 5 -> 5, of which waited for: 2 -> 2; matrix products, arithmetic and copies ran while one was open for 0% -> 0% of each run, Pallas kernels for 12% -> 13%
where the time goes in v3:
time: 84 us; the launch traced here: 83.7 us
  Pallas kernels  29.6 us (35%)
  blocking collectives  28.5 us (34%)
  starting transfers between devices  16.8 us (20%)
  local copies, waits for them, and re-layouts  3.42 us (4%)
  waiting for transfers between devices  3.11 us (4%)
  other arithmetic  1.53 us (2%)
    all_to_all x1, blocking collectives, shards(): partial = lax.all_to_all(partial, 'seg', 0, 0, tiled=True)  15.1 us
    all_to_all x1, blocking collectives, shards(): partial = lax.all_to_all(partial, 'fe', 0, 0, tiled=True)  13.3 us
    all_to_all x1, starting transfers between devices, shards(): groups = lax.all_to_all(packed, 'seg', 0, 0, tiled=True)  8.59 us
    ppermute x1, starting transfers between devices, shards(): above = lax.ppermute(down, 'fe', down_fe)  6.39 us
    pallas_call x1, Pallas kernels, shards(): call(scatter, [field, line, face, face, face, side_hot], [cols, pltpu.VME...  6.09 us
    pallas_call x1, Pallas kernels, shards(): call(traction, [line, (ROWS, q_dev // 2), weights], [sbuf, spreaded, pltp...  5.86 us
    pallas_call x1, Pallas kernels, shards(): call(fill_sides, [(12, tall, deep), message, message], [cols], smem=1, in...  3.52 us
    unnamed x14, local copies, waits for them, and re-layouts  3.41 us
  transfers between devices with their start and end apart: 5, of which 2 were waited for; matrix products, arithmetic and copies ran while one was open for 0% of the time, Pallas kernels for 13%

profile of v3, /device:TPU:1, one launch (start us, length us, event | category | flops | bytes accessed | tf_op | source)
XLA Modules:
  0.0 83.7 jit_solution(3581025102034033544)
XLA Ops:
  0.7 0.7 convert_bitcast_fusion
  1.4 0.1 pad_add_fusion.where_ref.refs_0_
  1.5 0.7 pad_maximum_fusion.segs_ref
  2.2 1.6 %shard_map.77 = f32[32,8,128]{2,1,0:T(8,128)} custom-call(s32[2]{0:T(128)S(1)} %pad_add_fusion.where_ref.refs_0_, f32[8,128]{1,0:T(8,128)S(1)} %pad_maximum_fusion.segs_ref), custom_call_target="tpu_custom_call" | custom-call | tf_op jit(solution)/shard_map/pallas_call | solution.py:517
  3.7 8.6 %all-to-all-start = ((f32[32,8,128]{2,1,0:T(8,128)}), f32[32,8,128]{2,1,0:T(8,128)S(1)}, u32[]{:S(2)}, u32[]{:S(2)}) async-start(f32[32,8,128]{2,1,0:T(8,128)} %shard_map.77), calls=%async_computation | async-start | bytes 262144 | tf_op jit(solution)/shard_map/all_to_all | solution.py:518
  12.4 0.9 %copy-done.3 = s32[65536]{0:T(1024)S(1)} copy-done((s32[65536]{0:T(1024)S(1)}, s32[65536]{0:T(1024)}, u32[]{:S(2)}) %copy-start.3) | copy-done | bytes 262168
  13.3 0.9 %copy-done.5 = f32[4,128,128]{2,1,0:T(8,128)S(1)} copy-done((f32[4,128,128]{2,1,0:T(8,128)S(1)}, f32[4,128,128]{2,1,0:T(8,128)}, u32[]{:S(2)}) %copy-start.5) | copy-done | bytes 262168
  14.3 1.9 %shard_map.78 = (f32[8,2048]{1,0:T(8,128)S(1)}, f32[8,512]{1,0:T(8,128)S(1)}, bf16[640,2048]{1,0:T(8,128)(2,1)S(1)}) custom-call(s32[2]{0:T(128)S(1)} %pad_add_fusion.where_ref.refs_0_, s32[512,128]{1,0:T(8,128)S(1)} %bitcast.7, f32[512,128]{1,0:T(8,128)S(1)} %bitcast.11), custom_call_target="tpu_custom_call" | custom-call | flops 1000000000 | bytes 1000000 | tf_op jit(solution)/shard_map/pallas_call | solution.py:519
  16.2 1.5 %copy-done.1 = bf16[640,2048]{1,0:T(8,128)(2,1)} copy-done((bf16[640,2048]{1,0:T(8,128)(2,1)}, bf16[640,2048]{1,0:T(8,128)(2,1)S(1)}, u32[]{:S(2)}) %copy-start.1) | copy-done | bytes 2621464
  17.7 2.2 %all-to-all-done.refs_0_.groups_ref = f32[32,8,128]{2,1,0:T(8,128)S(1)} async-done(((f32[32,8,128]{2,1,0:T(8,128)}), f32[32,8,128]{2,1,0:T(8,128)S(1)}, u32[]{:S(2)}, u32[]{:S(2)}) %all-to-all-start) | async-done | bytes 131104 | tf_op jit(solution)/shard_map/all_to_all | solution.py:518
  20.0 5.9 %shard_map.79 = (f32[8,2048]{1,0:T(8,128)S(1)}, f32[8,1024]{1,0:T(8,128)S(1)}, bf16[8,2,256,2048]{3,2,1,0:T(8,128)(2,1)S(1)}) custom-call(f32[32,8,128]{2,1,0:T(8,128)S(1)} %all-to-all-done.refs_0_.groups_ref, f32[3,2048]{1,0:T(4,128)S(1)} %constant_dynamic-slice_fusion.refs_1_.q_ref, f32[8,2048]{1,0:T(8,128)S(1)} %get-tuple-element.26.refs_2_), custom_call_target="tpu_custom_call" | custom-call | flops 10000000000 | bytes 1000000 | tf_op jit(solution)/shard_map/pallas_call | solution.py:528
  25.8 0.5 collective-permute-start.1
  26.3 1.3 %collective-permute-start = (f32[8,1024]{1,0:T(8,128)S(1)}, f32[8,1024]{1,0:T(8,128)S(1)}, u32[]{:S(2)}, u32[]{:S(2)}) collective-permute-start(f32[8,1024]{1,0:T(8,128)S(1)} %get-tuple-element.31), channel_id=1, source_target_pairs={{0,8},{8,16},{16,24},{24,32},{32,40},{40,48},{48,56},{56,64},{64,7... | collective-permute-start | bytes 98312 | tf_op jit(solution)/shard_map/ppermute | solution.py:532
  27.7 6.1 %shard_map.80 = (f32[3,512,128]{2,1,0:T(8,128)S(1)}, f32[8,2048]{1,0:T(8,128)S(1)}, f32[8,512]{1,0:T(8,128)S(1)}, f32[8,512]{1,0:T(8,128)S(1)}, f32[8,512]{1,0:T(8,128)S(1)}, /*index=5*/bf16[640,2048]{1,0:T(8,128)(2,1)S(1)}) custom-call(s32[2]{0:T(128)S(1)} %pad_add_fusion.where_ref.refs_0_, s32[512,128]{1,0:T(8,128)S(1)} %bitcast.8, ...), custom_call_target="tpu_custom_call" | custom-call | flops 4000000000 | bytes 4000000 | tf_op jit(solution)/shard_map/pallas_call | solution.py:539
  33.8 3.5 %shard_map.81 = (f32[12,128,128]{2,1,0:T(8,128)S(1)}, f32[8,768]{1,0:T(8,128)S(1)}, f32[8,768]{1,0:T(8,128)S(1)}) custom-call(s32[2]{0:T(128)S(1)} %pad_add_fusion.where_ref.refs_0_, f32[8,1024]{1,0:T(8,128)S(1)} %collective-permute-done.refs_1_, f32[8,1024]{1,0:T(8,128)S(1)} %collective-permute-done.1.refs_2_, ...), custom_call_target="tpu_custom_call" | custom-call | flops 2000000000 | bytes 1000000 | tf_op jit(solution)/shard_map/pallas_call | solution.py:547
  37.3 6.4 %collective-permute-start.2 = (f32[8,768]{1,0:T(8,128)S(1)}, f32[8,768]{1,0:T(8,128)S(1)}, u32[]{:S(2)}, u32[]{:S(2)}) collective-permute-start(f32[8,768]{1,0:T(8,128)S(1)} %get-tuple-element.41), channel_id=1, source_target_pairs={{1,0},{2,1},{3,2},{4,3},{5,4},{6,5},{7,6},{0,7},{9,8},{10,9},{11,1... | collective-permute-start | bytes 73736 | tf_op jit(solution)/shard_map/ppermute | solution.py:551
  43.7 3.0 %shard_map.82 = (f32[3,512,128]{2,1,0:T(8,128)S(1)}, f32[3,128,128]{2,1,0:T(8,128)S(1)}, f32[8,2048]{1,0:T(8,128)S(1)}, f32[8,512]{1,0:T(8,128)S(1)}) custom-call(s32[2]{0:T(128)S(1)} %pad_add_fusion.where_ref.refs_0_, s32[512,128]{1,0:T(8,128)S(1)} %bitcast.9, f32[3,512,128]{2,1,0:T(8,128)S(1)} %get-tuple-element.30.b_ref.refs_2_.refs_1_, ...), custom_call_target="tpu_custom_call" | custom-call | flops 4000000000 | bytes 4000000 | tf_op jit(solution)/shard_map/pallas_call | solution.py:553
  46.7 0.9 %collective-permute-done.3.refs_7_ = f32[8,768]{1,0:T(8,128)S(1)} collective-permute-done((f32[8,768]{1,0:T(8,128)S(1)}, f32[8,768]{1,0:T(8,128)S(1)}, u32[]{:S(2)}, u32[]{:S(2)}) %collective-permute-start.3) | collective-permute-done | bytes 24608 | tf_op jit(solution)/shard_map/ppermute | solution.py:552
  47.6 2.4 %shard_map.83 = (f32[3,512,128]{2,1,0:T(8,128)S(1)}, f32[8,2048]{1,0:T(8,128)S(1)}, f32[8,128]{1,0:T(8,128)S(1)}) custom-call(s32[2]{0:T(128)S(1)} %pad_add_fusion.where_ref.refs_0_, s32[512,128]{1,0:T(8,128)S(1)} %bitcast.10, f32[3,512,128]{2,1,0:T(8,128)S(1)} %get-tuple-element.30.b_ref.refs_2_.refs_1_, f32[3,512,128]{2,1,0:T(8,128)S(1)} %get-tuple-element.39.refs_3_, ...), custom_call_target="tpu_custom_call" | custom-call | flops 1000000000 | bytes 4000000 | tf_op jit(solution)/shard_map/pallas_call | solution.py:561
  50.0 3.2 %shard_map.84 = f32[32,8,128]{2,1,0:T(8,128)S(1)} custom-call(f32[32,8,128]{2,1,0:T(8,128)S(1)} %all-to-all-done.refs_0_.groups_ref, bf16[8,2,256,2048]{3,2,1,0:T(8,128)(2,1)S(1)} %get-tuple-element.27.kept_ref, f32[3,2048]{1,0:T(4,128)S(1)} %constant_dynamic-slice_fusion.refs_1_.q_ref, f32[8,2048]{1,0:T(8,128)S(1)} %get-tuple-element.45.g_ref, ...), custom_call_target="tpu_custom_call" | custom-call | flops 10000000000 | bytes 1000000 | tf_op jit(solution)/shard_map/pallas_call | solution.py:564
  53.3 15.1 %all_to_all.15.partial_ref = f32[32,8,128]{2,1,0:T(8,128)S(1)} all-to-all(f32[32,8,128]{2,1,0:T(8,128)S(1)} %shard_map.84), channel_id=1, replica_groups=mesh['seg'=32,'fe'=8] {'seg'}, dimensions={0} | all-to-all | bytes 262144 | tf_op jit(solution)/shard_map/all_to_all | solution.py:569
  68.4 0.8 shard_map.85
  69.2 13.3 %all_to_all.16.refs_0_ = f32[8,8,128]{2,1,0:T(8,128)S(1)} all-to-all(f32[8,8,128]{2,1,0:T(8,128)S(1)} %shard_map.85), channel_id=1, replica_groups=mesh['seg'=32,'fe'=8] {'fe'}, dimensions={0} | all-to-all | bytes 65536 | tf_op jit(solution)/shard_map/all_to_all | solution.py:571
  82.6 1.2 %shard_map.86 = (f32[3,512,128]{2,1,0:T(8,128)}, f32[3,128]{1,0:T(4,128)}) custom-call(f32[8,8,128]{2,1,0:T(8,128)S(1)} %all_to_all.16.refs_0_, f32[3,512,128]{2,1,0:T(8,128)S(1)} %get-tuple-element.30.b_ref.refs_2_.refs_1_, f32[3,512,128]{2,1,0:T(8,128)S(1)} %get-tuple-element.47.refs_2_), custom_call_target="tpu_custom_call" | custom-call | tf_op jit(solution)/shard_map/pallas_call | solution.py:576
  (16 shorter events, 0.1 us)
Async XLA Ops:
  0.6 11.7 %copy-start = (f32[3,65536]{1,0:T(4,128)S(1)}, f32[3,65536]{1,0:T(4,128)}, u32[]{:S(2)}) copy-start(f32[3,65536]{1,0:T(4,128)} %param.9) | copy-start | bytes 2359300
  3.7 16.2 %all-to-all-start = ((f32[32,8,128]{2,1,0:T(8,128)}), f32[32,8,128]{2,1,0:T(8,128)S(1)}, u32[]{:S(2)}, u32[]{:S(2)}) async-start(f32[32,8,128]{2,1,0:T(8,128)} %shard_map.77), calls=%async_computation | async-start | bytes 262144 | tf_op jit(solution)/shard_map/all_to_all | solution.py:518
  12.4 1.0 %copy-start.3 = (s32[65536]{0:T(1024)S(1)}, s32[65536]{0:T(1024)}, u32[]{:S(2)}) copy-start(s32[65536]{0:T(1024)} %param.10) | copy-start | bytes 786436
  13.3 0.9 %copy-start.5 = (f32[4,128,128]{2,1,0:T(8,128)S(1)}, f32[4,128,128]{2,1,0:T(8,128)}, u32[]{:S(2)}) copy-start(f32[4,128,128]{2,1,0:T(8,128)} %param.11) | copy-start | bytes 786436
  16.2 1.5 %copy-start.1 = (bf16[640,2048]{1,0:T(8,128)(2,1)}, bf16[640,2048]{1,0:T(8,128)(2,1)S(1)}, u32[]{:S(2)}) copy-start(bf16[640,2048]{1,0:T(8,128)(2,1)S(1)} %get-tuple-element.29.refs_3_.hot_ref.refs_11_) | copy-start | bytes 7864324
  20.0 7.7 %copy-start.2 = (bf16[640,2048]{1,0:T(8,128)(2,1)S(1)}, bf16[640,2048]{1,0:T(8,128)(2,1)}, u32[]{:S(2)}) copy-start(bf16[640,2048]{1,0:T(8,128)(2,1)} %copy-done.1) | copy-start | bytes 7864324
  20.0 7.7 %copy-start.4 = (s32[65536]{0:T(1024)S(1)}, s32[65536]{0:T(1024)}, u32[]{:S(2)}) copy-start(s32[65536]{0:T(1024)} %param.10) | copy-start | bytes 786436
  25.8 7.9 %collective-permute-start.1 = (f32[8,1024]{1,0:T(8,128)S(1)}, f32[8,1024]{1,0:T(8,128)S(1)}, u32[]{:S(2)}, u32[]{:S(2)}) collective-permute-start(f32[8,1024]{1,0:T(8,128)S(1)} %get-tuple-element.31), channel_id=1, source_target_pairs={{8,0},{16,8},{24,16},{32,24},{40,32},{48,40},{56,48},{64,56},{72,6... | collective-permute-start | bytes 98312 | tf_op jit(solution)/shard_map/ppermute | solution.py:533
  26.3 7.5 %collective-permute-start = (f32[8,1024]{1,0:T(8,128)S(1)}, f32[8,1024]{1,0:T(8,128)S(1)}, u32[]{:S(2)}, u32[]{:S(2)}) collective-permute-start(f32[8,1024]{1,0:T(8,128)S(1)} %get-tuple-element.31), channel_id=1, source_target_pairs={{0,8},{8,16},{16,24},{24,32},{32,40},{40,48},{48,56},{56,64},{64,7... | collective-permute-start | bytes 98312 | tf_op jit(solution)/shard_map/ppermute | solution.py:532
  33.8 9.9 %copy-start.6 = (f32[4,128,128]{2,1,0:T(8,128)S(1)}, f32[4,128,128]{2,1,0:T(8,128)}, u32[]{:S(2)}) copy-start(f32[4,128,128]{2,1,0:T(8,128)} %param.11) | copy-start | bytes 786436
  37.3 9.4 %collective-permute-start.2 = (f32[8,768]{1,0:T(8,128)S(1)}, f32[8,768]{1,0:T(8,128)S(1)}, u32[]{:S(2)}, u32[]{:S(2)}) collective-permute-start(f32[8,768]{1,0:T(8,128)S(1)} %get-tuple-element.41), channel_id=1, source_target_pairs={{1,0},{2,1},{3,2},{4,3},{5,4},{6,5},{7,6},{0,7},{9,8},{10,9},{11,1... | collective-permute-start | bytes 73736 | tf_op jit(solution)/shard_map/ppermute | solution.py:551
  43.7 3.9 %collective-permute-start.3 = (f32[8,768]{1,0:T(8,128)S(1)}, f32[8,768]{1,0:T(8,128)S(1)}, u32[]{:S(2)}, u32[]{:S(2)}) collective-permute-start(f32[8,768]{1,0:T(8,128)S(1)} %get-tuple-element.42), channel_id=1, source_target_pairs={{0,1},{1,2},{2,3},{3,4},{4,5},{5,6},{6,7},{7,0},{8,9},{9,10},{10,1... | collective-permute-start | bytes 73736 | tf_op jit(solution)/shard_map/ppermute | solution.py:552

commit v4 on v3

--- a/solution.py
+++ b/solution.py
@@ -30,7 +30,7 @@
 
 
 def near_rank(tile, block):
-    near = jnp.abs(tile.astype(jnp.int32) - block) <= 1
+    near = jnp.abs(tile - block) <= 1
     mask = jnp.where(near, 1.0, 0.0)
     n = tile.shape[1]
     before = jnp.where(iota((n, n), 0) < iota((n, n), 1), 1.0, 0.0)
@@ -39,11 +39,11 @@
     return mask, place
 
 
-def pack_kernel(where_ref, segs_ref, out_ref):
-    segs = segs_ref[...]
-    mask, place = near_rank(segs[6:7], where_ref[1])
-    vals = jnp.where(iota(segs.shape, 0) < 6, segs, mask)
-    packed = lax.dot_general(vals, place, NT, precision=HIGH, preferred_element_type=F32)
+def pack_kernel(where_ref, segs_ref, tile_ref, out_ref):
+    mask, place = near_rank(tile_ref[...], where_ref[1])
+    rest = jnp.broadcast_to(mask, (2, mask.shape[1]))
+    segs = jnp.concatenate([segs_ref[...], rest], axis=0)
+    packed = lax.dot_general(segs, place, NT, precision=HIGH, preferred_element_type=F32)
     out_ref[...] = jnp.broadcast_to(packed[None], out_ref.shape)
 
 
@@ -83,7 +83,7 @@
 
 
 def in_chunks(total, chunk):
-    half = CHUNK // 2
+    quarter, half = CHUNK // 4, CHUNK // 2
     whole = total // CHUNK
     rest = total - whole * CHUNK
     n = whole + jnp.where(rest > half, 1, 0)
@@ -93,10 +93,11 @@
         return carry
 
     lax.fori_loop(0, n, step, jnp.int32(0))
-
-    @pl.when(jnp.logical_and(rest > 0, rest <= half))
-    def _():
-        chunk(pl.multiple_of(whole * CHUNK, CHUNK), half)
+    for least, most in ((0, quarter), (quarter, half)):
+
+        @pl.when(jnp.logical_and(rest > least, rest <= most))
+        def _():
+            chunk(pl.multiple_of(whole * CHUNK, CHUNK), most)
 
 
 def spread(sbuf, wide, start, size):
@@ -225,7 +226,7 @@
 
 
 def scatter_kernel(
-    n_seg, where_ref, nodes_ref, t_ref, hot_ref, b_ref, g_ref, low_ref, next_ref, high_ref, side_hot_ref, cols, parts
+    where_ref, nodes_ref, t_ref, hot_ref, b_ref, g_ref, low_ref, next_ref, high_ref, cols, parts
 ):
     n = t_ref.shape[1] // LANES
     rows = b_ref.shape[1]
@@ -244,14 +245,7 @@
             next_ref[c : c + 1, at] = tile[1:2, :]
             high_ref[c : c + 1, at] = tile[LANES - 1 : LANES, :]
     g_ref[...] = jnp.zeros_like(g_ref)
-    me = where_ref[0]
-    gather(nodes_of(nodes_ref, me, n), hot_ref, parts, 3, g_ref, 0)
-    nodes = nodes_of(nodes_ref, jnp.maximum(me - 1, 0), n)
-    set_hot(nodes, side_hot_ref.at[0:LANES], rows - LANES)
-    set_spot(nodes, side_hot_ref.at[LANES : 2 * LANES])
-    nodes = nodes_of(nodes_ref, jnp.minimum(me + 1, n_seg - 1), n)
-    set_hot(nodes, side_hot_ref.at[2 * LANES : 4 * LANES], 0)
-    set_spot(nodes, side_hot_ref.at[4 * LANES : 5 * LANES])
+    gather(nodes_of(nodes_ref, where_ref[0], n), hot_ref, parts, 3, g_ref, 0)
 
 
 def unfold(sent):
@@ -259,9 +253,10 @@
 
 
 def sides_kernel(
-    n_seg, where_ref, left_ref, right_ref, side_hot_ref, low_ref, next_ref, high_ref, kz_ref,
-    sides_ref, down_ref, up_ref, cols,
+    n_seg, where_ref, nodes_ref, left_ref, right_ref, low_ref, next_ref, high_ref, kz_ref,
+    sides_ref, down_ref, up_ref, hot, spot, cols,
 ):
+    n = hot.shape[1] // LANES
     rows = low_ref.shape[1]
     me = where_ref[0]
     down_ref[...] = jnp.zeros_like(down_ref)
@@ -272,16 +267,21 @@
     down_ref[6:7, own] = kz_ref[0:1, :]
     up_ref[0:3, own] = high_ref[0:3, :]
 
-    spread_points(side_hot_ref.at[LANES : 2 * LANES], unfold(left_ref[...]) * jnp.where(me > 0, 1.0, 0.0), cols)
-    left = layers(side_hot_ref[0:LANES, :], cols[...])
+    nodes = nodes_of(nodes_ref, jnp.maximum(me - 1, 0), n)
+    set_hot(nodes, hot.at[0:LANES], rows - LANES)
+    set_spot(nodes, spot)
+    spread_points(spot, unfold(left_ref[...]) * jnp.where(me > 0, 1.0, 0.0), cols)
+    left = layers(hot[0:LANES, :], cols[...])
+    nodes = nodes_of(nodes_ref, jnp.minimum(me + 1, n_seg - 1), n)
+    set_hot(nodes, hot, 0)
+    set_spot(nodes, spot)
     t = unfold(right_ref[...])
     kq = t[3:4]
     t = t * jnp.where(me < n_seg - 1, 1.0, 0.0)
-    right_spot = side_hot_ref.at[4 * LANES : 5 * LANES]
-    spread_points(right_spot, t, cols)
-    right = layers(side_hot_ref[2 * LANES : 4 * LANES, :], cols[...])
-    spread_points(right_spot, t * kq, cols)
-    stiff = layers(side_hot_ref[2 * LANES : 3 * LANES, :], cols[...])
+    spread_points(spot, t, cols)
+    right = layers(hot[...], cols[...])
+    spread_points(spot, t * kq, cols)
+    stiff = layers(hot[0:LANES, :], cols[...])
     last = slice(LANES + rows, 2 * LANES + rows)
     for c in range(3):
         comp = slice(c * LANES, (c + 1) * LANES)
@@ -398,16 +398,15 @@
     places, length, longest = measured(groups_ref)
     motion[...] = jnp.concatenate(split(g_ref[...]), axis=0)
     n_chunks = (length + (CHUNK - 1)) // CHUNK
-    n_kept = jnp.minimum(n_chunks, KEPT)
-
-    def from_kept(i, carry):
+
+    def from_kept(start, size):
+        i = start // CHUNK
         m = motion[...]
-        found = lax.dot_general(kept_ref[i, 0], m, NT, preferred_element_type=F32)
-        found = found + lax.dot_general(kept_ref[i, 1], m, NT, preferred_element_type=F32)
-        results[pl.ds(pl.multiple_of(i * CHUNK, CHUNK), CHUNK), 0 : 2 * ROWS] = found
-        return carry
-
-    lax.fori_loop(0, n_kept, from_kept, jnp.int32(0))
+        found = lax.dot_general(kept_ref[i, 0, 0:size], m, NT, preferred_element_type=F32)
+        found = found + lax.dot_general(kept_ref[i, 1, 0:size], m, NT, preferred_element_type=F32)
+        results[pl.ds(start, size), 0 : 2 * ROWS] = found
+
+    in_chunks(jnp.minimum(length, KEPT * CHUNK), from_kept)
 
     def again(i, carry):
         start = pl.multiple_of(i * CHUNK, CHUNK)
@@ -443,8 +442,8 @@
     by_width(longest, width, run)
 
 
-def unpack_kernel(where_ref, segs_ref, partial_ref, out_ref):
-    _, place = near_rank(segs_ref[6:7, :], where_ref[1])
+def unpack_kernel(where_ref, tile_ref, partial_ref, out_ref):
+    _, place = near_rank(tile_ref[...], where_ref[1])
     total = jnp.sum(partial_ref[...], axis=0)
     spreaded = jnp.dot(total, place, precision=HIGH, preferred_element_type=F32)
     total = jnp.where(iota(total.shape, 0) == 6, total, spreaded)
@@ -469,17 +468,15 @@
 def call(kernel, out, scratch=(), smem=0, inputs=0, flops=0, moved=0):
     vmem = pl.BlockSpec(memory_space=pltpu.VMEM)
     ints = pl.BlockSpec(memory_space=pltpu.SMEM)
-    shapes, specs = [], []
+    shapes = []
     for o in out:
-        whole = isinstance(o, jax.ShapeDtypeStruct)
-        shapes.append(o if whole else jax.ShapeDtypeStruct(o, F32))
-        specs.append(ints if whole and o.dtype == jnp.int32 else vmem)
+        shapes.append(o if isinstance(o, jax.ShapeDtypeStruct) else jax.ShapeDtypeStruct(o, F32))
     single = len(shapes) == 1
     return pl.pallas_call(
         kernel,
         out_shape=shapes[0] if single else tuple(shapes),
         in_specs=[ints] * smem + [vmem] * inputs,
-        out_specs=specs[0] if single else tuple(specs),
+        out_specs=vmem if single else (vmem,) * len(shapes),
         scratch_shapes=list(scratch),
         compiler_params=pltpu.CompilerParams(vmem_limit_bytes=VMEM_LIMIT),
         cost_estimate=pl.CostEstimate(flops=flops, bytes_accessed=moved, transcendentals=0),
@@ -497,8 +494,7 @@
     wide, tall, deep = stiffness.shape
     rows = wide * tall
     where = jnp.stack([column, block]).astype(jnp.int32)
-    tile = seg_tile.reshape(1, s_dev).astype(F32)
-    segs = jnp.concatenate([seg_pos, burgers, tile, tile], axis=0)
+    tile = seg_tile.reshape(1, s_dev)
     nodes = quad_node.reshape(q_block // LANES, LANES)
     points = lax.dynamic_slice_in_dim(quad_pos, column * q_dev, q_dev, 1)
     stiff = stiffness.reshape(rows, deep)
@@ -514,7 +510,8 @@
     spreaded = pltpu.VMEM((3, CHUNK, LANES), F32)
     cols = pltpu.VMEM((6 * LANES, q_dev), BF16)
 
-    packed = call(pack_kernel, [(n_seg, ROWS, s_dev)], smem=1, inputs=1)(where, segs)
+    segs = jnp.concatenate([seg_pos, burgers], axis=0)
+    packed = call(pack_kernel, [(n_seg, ROWS, s_dev)], smem=1, inputs=2)(where, segs, tile)
     groups = lax.all_to_all(packed, "seg", 0, 0, tiled=True)
     kq, kz, hot = call(
         prepare_kernel, [line, face, jax.ShapeDtypeStruct((rows + LANES, q_dev), BF16)],
@@ -532,12 +529,8 @@
     from_left = lax.ppermute(sent, "seg", up_seg)
     from_right = lax.ppermute(sent, "seg", down_seg)
 
-    def scatter(*refs):
-        scatter_kernel(n_seg, *refs)
-
-    side_hot = jax.ShapeDtypeStruct((5 * LANES, q_dev), BF16)
-    b, g, low, after, high, side_hot = call(
-        scatter, [field, line, face, face, face, side_hot], [cols, pltpu.VMEM((3 * LANES, 2 * rows), BF16)],
+    b, g, low, after, high = call(
+        scatter_kernel, [field, line, face, face, face], [cols, pltpu.VMEM((3 * LANES, 2 * rows), BF16)],
         smem=1, inputs=3, flops=4 * 10**9, moved=4 * 10**6,
     )(where, nodes, t, hot)
 
@@ -545,9 +538,10 @@
         sides_kernel(n_seg, *refs)
 
     sides, down, up = call(
-        fill_sides, [(12, tall, deep), message, message], [cols],
+        fill_sides, [(12, tall, deep), message, message],
+        [pltpu.VMEM((2 * LANES, q_dev), BF16), pltpu.VMEM((LANES, q_dev), BF16), cols],
         smem=1, inputs=7, flops=2 * 10**9, moved=10**6,
-    )(where, from_left, from_right, side_hot, low, after, high, kz)
+    )(where, nodes, from_left, from_right, low, after, high, kz)
     above = lax.ppermute(down, "fe", down_fe)
     below = lax.ppermute(up, "fe", up_fe)
     u, ur, g, uh = call(
@@ -567,7 +561,7 @@
         inputs=5, flops=10**10, moved=10**6,
     )(groups, kept, points, motion, sums)
     partial = lax.all_to_all(partial, "seg", 0, 0, tiled=True)
-    partial = call(unpack_kernel, [(n_fe, ROWS, s_dev)], smem=1, inputs=2)(where, segs, partial)
+    partial = call(unpack_kernel, [(n_fe, ROWS, s_dev)], smem=1, inputs=2)(where, tile, partial)
     partial = lax.all_to_all(partial, "fe", 0, 0, tiled=True)
 
     def finish(*refs):

time: 84 us -> 83.3 us (level)
  starting transfers between devices: 16.8 us -> 15.6 us
    ppermute x1, starting transfers between devices: 6.39 us -> 5.19 us  [shards(): above = lax.ppermute(down, 'fe', down_fe)]
    unnamed x14 -> x18, local copies, waits for them, and re-layouts: 3.41 us -> 4.07 us
  transfers between devices with their start and end apart: 5 -> 5, of which waited for: 2 -> 2; matrix products, arithmetic and copies ran while one was open for 0% -> 0% of each run, Pallas kernels for 13% -> 12%
where the time goes in v4:
time: 83.3 us; the launch traced here: 83 us
  Pallas kernels  29.7 us (36%)
  blocking collectives  28.2 us (34%)
  starting transfers between devices  15.6 us (19%)
  local copies, waits for them, and re-layouts  4.08 us (5%)
  waiting for transfers between devices  3.78 us (5%)
  other arithmetic  0.85 us (1%)
    all_to_all x1, blocking collectives, shards(): partial = lax.all_to_all(partial, 'seg', 0, 0, tiled=True)  15.1 us
    all_to_all x1, blocking collectives, shards(): partial = lax.all_to_all(partial, 'fe', 0, 0, tiled=True)  13.1 us
    all_to_all x1, starting transfers between devices, shards(): groups = lax.all_to_all(packed, 'seg', 0, 0, tiled=True)  8.59 us
    pallas_call x1, Pallas kernels, shards(): call(traction, [line, (ROWS, q_dev // 2), weights], [sbuf, spreaded, pltp...  6.29 us
    ppermute x1, starting transfers between devices, shards(): above = lax.ppermute(down, 'fe', down_fe)  5.19 us
    pallas_call x1, Pallas kernels, shards(): call(scatter_kernel, [field, line, face, face, face], [cols, pltpu.VMEM((...  5.05 us
    unnamed x18, local copies, waits for them, and re-layouts  4.07 us
    pallas_call x1, Pallas kernels, shards(): call(fill_sides, [(12, tall, deep), message, message], [pltpu.VMEM((2 * L...  3.87 us
  transfers between devices with their start and end apart: 5, of which 2 were waited for; matrix products, arithmetic and copies ran while one was open for 0% of the time, Pallas kernels for 12%

profile of v4, /device:TPU:1, one launch (start us, length us, event | category | flops | bytes accessed | tf_op | source)
XLA Modules:
  0.0 83.0 jit_solution(15102503237277499186)
XLA Ops:
  0.6 0.1 pad_add_fusion.where_ref.refs_0_
  0.7 0.8 pad_maximum_fusion.segs_ref
  1.5 0.7 copy-done.7
  2.2 1.6 %shard_map.77 = f32[32,8,128]{2,1,0:T(8,128)} custom-call(s32[2]{0:T(128)S(1)} %pad_add_fusion.where_ref.refs_0_, f32[6,128]{1,0:T(8,128)S(1)} %pad_maximum_fusion.segs_ref, s32[1,128]{1,0:T(1,128)S(1)} %bitcast.14), custom_call_target="tpu_custom_call" | custom-call | tf_op jit(solution)/shard_map/pallas_call | solution.py:514
  3.7 8.6 %all-to-all-start = ((f32[32,8,128]{2,1,0:T(8,128)}), f32[32,8,128]{2,1,0:T(8,128)S(1)}, u32[]{:S(2)}, u32[]{:S(2)}) async-start(f32[32,8,128]{2,1,0:T(8,128)} %shard_map.77), calls=%async_computation | async-start | bytes 262144 | tf_op jit(solution)/shard_map/all_to_all | solution.py:515
  12.4 0.9 %copy-done.3 = s32[65536]{0:T(1024)S(1)} copy-done((s32[65536]{0:T(1024)S(1)}, s32[65536]{0:T(1024)}, u32[]{:S(2)}) %copy-start.3) | copy-done | bytes 262168
  13.3 0.9 %copy-done.5 = f32[4,128,128]{2,1,0:T(8,128)S(1)} copy-done((f32[4,128,128]{2,1,0:T(8,128)S(1)}, f32[4,128,128]{2,1,0:T(8,128)}, u32[]{:S(2)}) %copy-start.5) | copy-done | bytes 262168
  14.2 1.9 %shard_map.78 = (f32[8,2048]{1,0:T(8,128)S(1)}, f32[8,512]{1,0:T(8,128)S(1)}, bf16[640,2048]{1,0:T(8,128)(2,1)S(1)}) custom-call(s32[2]{0:T(128)S(1)} %pad_add_fusion.where_ref.refs_0_, s32[512,128]{1,0:T(8,128)S(1)} %bitcast.6, f32[512,128]{1,0:T(8,128)S(1)} %bitcast.11), custom_call_target="tpu_custom_call" | custom-call | flops 1000000000 | bytes 1000000 | tf_op jit(solution)/shard_map/pallas_call | solution.py:516
  16.2 1.5 %copy-done.1 = bf16[640,2048]{1,0:T(8,128)(2,1)} copy-done((bf16[640,2048]{1,0:T(8,128)(2,1)}, bf16[640,2048]{1,0:T(8,128)(2,1)S(1)}, u32[]{:S(2)}) %copy-start.1) | copy-done | bytes 2621464
  17.7 2.2 %all-to-all-done.refs_0_.groups_ref = f32[32,8,128]{2,1,0:T(8,128)S(1)} async-done(((f32[32,8,128]{2,1,0:T(8,128)}), f32[32,8,128]{2,1,0:T(8,128)S(1)}, u32[]{:S(2)}, u32[]{:S(2)}) %all-to-all-start) | async-done | bytes 131104 | tf_op jit(solution)/shard_map/all_to_all | solution.py:515
  19.9 6.3 %shard_map.79 = (f32[8,2048]{1,0:T(8,128)S(1)}, f32[8,1024]{1,0:T(8,128)S(1)}, bf16[8,2,256,2048]{3,2,1,0:T(8,128)(2,1)S(1)}) custom-call(f32[32,8,128]{2,1,0:T(8,128)S(1)} %all-to-all-done.refs_0_.groups_ref, f32[3,2048]{1,0:T(4,128)S(1)} %constant_dynamic-slice_fusion.refs_1_.q_ref, f32[8,2048]{1,0:T(8,128)S(1)} %get-tuple-element.25.refs_2_), custom_call_target="tpu_custom_call" | custom-call | flops 10000000000 | bytes 1000000 | tf_op jit(solution)/shard_map/pallas_call | solution.py:525
  26.3 0.5 collective-permute-start.1
  26.7 1.3 %collective-permute-start = (f32[8,1024]{1,0:T(8,128)S(1)}, f32[8,1024]{1,0:T(8,128)S(1)}, u32[]{:S(2)}, u32[]{:S(2)}) collective-permute-start(f32[8,1024]{1,0:T(8,128)S(1)} %get-tuple-element.30), channel_id=1, source_target_pairs={{0,8},{8,16},{16,24},{24,32},{32,40},{40,48},{48,56},{56,64},{64,7... | collective-permute-start | bytes 98312 | tf_op jit(solution)/shard_map/ppermute | solution.py:529
  28.1 5.0 %shard_map.80 = (f32[3,512,128]{2,1,0:T(8,128)S(1)}, f32[8,2048]{1,0:T(8,128)S(1)}, f32[8,512]{1,0:T(8,128)S(1)}, f32[8,512]{1,0:T(8,128)S(1)}, f32[8,512]{1,0:T(8,128)S(1)}) custom-call(s32[2]{0:T(128)S(1)} %pad_add_fusion.where_ref.refs_0_, s32[512,128]{1,0:T(8,128)S(1)} %bitcast.7, f32[8,2048]{1,0:T(8,128)S(1)} %get-tuple-element.27.t_ref, ...), custom_call_target="tpu_custom_call" | custom-call | flops 4000000000 | bytes 4000000 | tf_op jit(solution)/shard_map/pallas_call | solution.py:532
  33.2 3.9 %shard_map.81 = (f32[12,128,128]{2,1,0:T(8,128)S(1)}, f32[8,768]{1,0:T(8,128)S(1)}, f32[8,768]{1,0:T(8,128)S(1)}) custom-call(s32[2]{0:T(128)S(1)} %pad_add_fusion.where_ref.refs_0_, s32[512,128]{1,0:T(8,128)S(1)} %bitcast.8, f32[8,1024]{1,0:T(8,128)S(1)} %collective-permute-done.refs_2_, f32[8,1024]{1,0:T(8,128)S(1)} %collective-permute-done.1.refs_3_, ...), custom_call_target="tpu_custom_call" | custom-call | flops 2000000000 | bytes 1000000 | tf_op jit(solution)/shard_map/pallas_call | solution.py:540
  37.0 5.2 %collective-permute-start.2 = (f32[8,768]{1,0:T(8,128)S(1)}, f32[8,768]{1,0:T(8,128)S(1)}, u32[]{:S(2)}, u32[]{:S(2)}) collective-permute-start(f32[8,768]{1,0:T(8,128)S(1)} %get-tuple-element.39), channel_id=1, source_target_pairs={{1,0},{2,1},{3,2},{4,3},{5,4},{6,5},{7,6},{0,7},{9,8},{10,9},{11,1... | collective-permute-start | bytes 73736 | tf_op jit(solution)/shard_map/ppermute | solution.py:545
  42.2 3.0 %shard_map.82 = (f32[3,512,128]{2,1,0:T(8,128)S(1)}, f32[3,128,128]{2,1,0:T(8,128)S(1)}, f32[8,2048]{1,0:T(8,128)S(1)}, f32[8,512]{1,0:T(8,128)S(1)}) custom-call(s32[2]{0:T(128)S(1)} %pad_add_fusion.where_ref.refs_0_, s32[512,128]{1,0:T(8,128)S(1)} %bitcast.9, f32[3,512,128]{2,1,0:T(8,128)S(1)} %get-tuple-element.29.b_ref.refs_2_.refs_1_, ...), custom_call_target="tpu_custom_call" | custom-call | flops 4000000000 | bytes 4000000 | tf_op jit(solution)/shard_map/pallas_call | solution.py:547
  45.3 1.5 %collective-permute-done.3.refs_7_ = f32[8,768]{1,0:T(8,128)S(1)} collective-permute-done((f32[8,768]{1,0:T(8,128)S(1)}, f32[8,768]{1,0:T(8,128)S(1)}, u32[]{:S(2)}, u32[]{:S(2)}) %collective-permute-start.3) | collective-permute-done | bytes 24608 | tf_op jit(solution)/shard_map/ppermute | solution.py:546
  46.8 2.4 %shard_map.83 = (f32[3,512,128]{2,1,0:T(8,128)S(1)}, f32[8,2048]{1,0:T(8,128)S(1)}, f32[8,128]{1,0:T(8,128)S(1)}) custom-call(s32[2]{0:T(128)S(1)} %pad_add_fusion.where_ref.refs_0_, s32[512,128]{1,0:T(8,128)S(1)} %bitcast.10, f32[3,512,128]{2,1,0:T(8,128)S(1)} %get-tuple-element.29.b_ref.refs_2_.refs_1_, f32[3,512,128]{2,1,0:T(8,128)S(1)} %get-tuple-element.37.refs_3_, ...), custom_call_target="tpu_custom_call" | custom-call | flops 1000000000 | bytes 4000000 | tf_op jit(solution)/shard_map/pallas_call | solution.py:555
  49.2 3.6 %shard_map.84 = f32[32,8,128]{2,1,0:T(8,128)S(1)} custom-call(f32[32,8,128]{2,1,0:T(8,128)S(1)} %all-to-all-done.refs_0_.groups_ref, bf16[8,2,256,2048]{3,2,1,0:T(8,128)(2,1)S(1)} %get-tuple-element.26.kept_ref, f32[3,2048]{1,0:T(4,128)S(1)} %constant_dynamic-slice_fusion.refs_1_.q_ref, f32[8,2048]{1,0:T(8,128)S(1)} %get-tuple-element.43.g_ref, ...), custom_call_target="tpu_custom_call" | custom-call | flops 10000000000 | bytes 1000000 | tf_op jit(solution)/shard_map/pallas_call | solution.py:558
  52.8 15.1 %all_to_all.15.partial_ref = f32[32,8,128]{2,1,0:T(8,128)S(1)} all-to-all(f32[32,8,128]{2,1,0:T(8,128)S(1)} %shard_map.84), channel_id=1, replica_groups=mesh['seg'=32,'fe'=8] {'seg'}, dimensions={0} | all-to-all | bytes 262144 | tf_op jit(solution)/shard_map/all_to_all | solution.py:563
  67.9 0.8 shard_map.85
  68.7 13.1 %all_to_all.16.refs_0_ = f32[8,8,128]{2,1,0:T(8,128)S(1)} all-to-all(f32[8,8,128]{2,1,0:T(8,128)S(1)} %shard_map.85), channel_id=1, replica_groups=mesh['seg'=32,'fe'=8] {'fe'}, dimensions={0} | all-to-all | bytes 65536 | tf_op jit(solution)/shard_map/all_to_all | solution.py:565
  81.8 1.2 %shard_map.86 = (f32[3,512,128]{2,1,0:T(8,128)}, f32[3,128]{1,0:T(4,128)}) custom-call(f32[8,8,128]{2,1,0:T(8,128)S(1)} %all_to_all.16.refs_0_, f32[3,512,128]{2,1,0:T(8,128)S(1)} %get-tuple-element.29.b_ref.refs_2_.refs_1_, f32[3,512,128]{2,1,0:T(8,128)S(1)} %get-tuple-element.45.refs_2_), custom_call_target="tpu_custom_call" | custom-call | tf_op jit(solution)/shard_map/pallas_call | solution.py:570
  (19 shorter events, 0.1 us)
Async XLA Ops:
  0.6 11.7 %copy-start = (f32[3,65536]{1,0:T(4,128)S(1)}, f32[3,65536]{1,0:T(4,128)}, u32[]{:S(2)}) copy-start(f32[3,65536]{1,0:T(4,128)} %param.9) | copy-start | bytes 2359300
  1.5 0.7 copy-start.7
  3.7 16.2 %all-to-all-start = ((f32[32,8,128]{2,1,0:T(8,128)}), f32[32,8,128]{2,1,0:T(8,128)S(1)}, u32[]{:S(2)}, u32[]{:S(2)}) async-start(f32[32,8,128]{2,1,0:T(8,128)} %shard_map.77), calls=%async_computation | async-start | bytes 262144 | tf_op jit(solution)/shard_map/all_to_all | solution.py:515
  12.3 1.0 %copy-start.3 = (s32[65536]{0:T(1024)S(1)}, s32[65536]{0:T(1024)}, u32[]{:S(2)}) copy-start(s32[65536]{0:T(1024)} %param.10) | copy-start | bytes 786436
  13.3 0.9 %copy-start.5 = (f32[4,128,128]{2,1,0:T(8,128)S(1)}, f32[4,128,128]{2,1,0:T(8,128)}, u32[]{:S(2)}) copy-start(f32[4,128,128]{2,1,0:T(8,128)} %param.11) | copy-start | bytes 786436
  16.2 1.5 %copy-start.1 = (bf16[640,2048]{1,0:T(8,128)(2,1)}, bf16[640,2048]{1,0:T(8,128)(2,1)S(1)}, u32[]{:S(2)}) copy-start(bf16[640,2048]{1,0:T(8,128)(2,1)S(1)} %get-tuple-element.28.hot_ref.refs_11_) | copy-start | bytes 7864324
  19.9 8.1 %copy-start.2 = (bf16[640,2048]{1,0:T(8,128)(2,1)S(1)}, bf16[640,2048]{1,0:T(8,128)(2,1)}, u32[]{:S(2)}) copy-start(bf16[640,2048]{1,0:T(8,128)(2,1)} %copy-done.1) | copy-start | bytes 7864324
  19.9 8.1 %copy-start.4 = (s32[65536]{0:T(1024)S(1)}, s32[65536]{0:T(1024)}, u32[]{:S(2)}) copy-start(s32[65536]{0:T(1024)} %param.10) | copy-start | bytes 786436
  26.2 16.0 %copy-start.6 = (f32[4,128,128]{2,1,0:T(8,128)S(1)}, f32[4,128,128]{2,1,0:T(8,128)}, u32[]{:S(2)}) copy-start(f32[4,128,128]{2,1,0:T(8,128)} %param.11) | copy-start | bytes 786436
  26.3 6.9 %collective-permute-start.1 = (f32[8,1024]{1,0:T(8,128)S(1)}, f32[8,1024]{1,0:T(8,128)S(1)}, u32[]{:S(2)}, u32[]{:S(2)}) collective-permute-start(f32[8,1024]{1,0:T(8,128)S(1)} %get-tuple-element.30), channel_id=1, source_target_pairs={{8,0},{16,8},{24,16},{32,24},{40,32},{48,40},{56,48},{64,56},{72,6... | collective-permute-start | bytes 98312 | tf_op jit(solution)/shard_map/ppermute | solution.py:530
  26.7 6.4 %collective-permute-start = (f32[8,1024]{1,0:T(8,128)S(1)}, f32[8,1024]{1,0:T(8,128)S(1)}, u32[]{:S(2)}, u32[]{:S(2)}) collective-permute-start(f32[8,1024]{1,0:T(8,128)S(1)} %get-tuple-element.30), channel_id=1, source_target_pairs={{0,8},{8,16},{16,24},{24,32},{32,40},{40,48},{48,56},{56,64},{64,7... | collective-permute-start | bytes 98312 | tf_op jit(solution)/shard_map/ppermute | solution.py:529
  37.0 8.2 %collective-permute-start.2 = (f32[8,768]{1,0:T(8,128)S(1)}, f32[8,768]{1,0:T(8,128)S(1)}, u32[]{:S(2)}, u32[]{:S(2)}) collective-permute-start(f32[8,768]{1,0:T(8,128)S(1)} %get-tuple-element.39), channel_id=1, source_target_pairs={{1,0},{2,1},{3,2},{4,3},{5,4},{6,5},{7,6},{0,7},{9,8},{10,9},{11,1... | collective-permute-start | bytes 73736 | tf_op jit(solution)/shard_map/ppermute | solution.py:545
  42.2 4.6 %collective-permute-start.3 = (f32[8,768]{1,0:T(8,128)S(1)}, f32[8,768]{1,0:T(8,128)S(1)}, u32[]{:S(2)}, u32[]{:S(2)}) collective-permute-start(f32[8,768]{1,0:T(8,128)S(1)} %get-tuple-element.40), channel_id=1, source_target_pairs={{0,1},{1,2},{2,3},{3,4},{4,5},{5,6},{6,7},{7,0},{8,9},{9,10},{10,1... | collective-permute-start | bytes 73736 | tf_op jit(solution)/shard_map/ppermute | solution.py:546
  49.2 18.7 %copy-start.8 = (s32[128]{0:T(128)S(1)}, s32[128]{0:T(128)}, u32[]{:S(2)}) copy-start(s32[128]{0:T(128)} %param.8) | copy-start | bytes 1540

commit v5 on v4

--- a/solution.py
+++ b/solution.py
@@ -18,6 +18,7 @@
 KEPT = 7
 NT = (((1,), (1,)), ((), ()))
 VMEM_LIMIT = 12 * 1024 * 1024
+PACK_LIMIT = 60 * 1024 * 1024
 
 
 def iota(shape, dim):
@@ -39,10 +40,10 @@
     return mask, place
 
 
-def pack_kernel(where_ref, segs_ref, tile_ref, out_ref):
+def pack_kernel(where_ref, pos_ref, burgers_ref, tile_ref, out_ref):
     mask, place = near_rank(tile_ref[...], where_ref[1])
     rest = jnp.broadcast_to(mask, (2, mask.shape[1]))
-    segs = jnp.concatenate([segs_ref[...], rest], axis=0)
+    segs = jnp.concatenate([pos_ref[...], burgers_ref[...], rest], axis=0)
     packed = lax.dot_general(segs, place, NT, precision=HIGH, preferred_element_type=F32)
     out_ref[...] = jnp.broadcast_to(packed[None], out_ref.shape)
 
@@ -295,6 +296,11 @@
         up_ref[c : c + 1, last] = tile[LANES - 1 : LANES, :]
 
 
+def before_in_layer(f):
+    i, j = iota(f.shape, 0), iota(f.shape, 1)
+    return jnp.where(i == 0, 0.0, pltpu.roll(f, 1, 0)) + jnp.where(j == 0, 0.0, pltpu.roll(f, 1, 1))
+
+
 def beside_in_layer(f):
     i, j = iota(f.shape, 0), iota(f.shape, 1)
     n, m = f.shape
@@ -351,7 +357,7 @@
     lane = iota((LANES, LANES), 1)
     zero = jnp.zeros((LANES, LANES), F32)
     bb, bu, uu, uau = zero, zero, zero, zero
-    not_last = jnp.where(me < n_seg - 1, 2.0, 0.0)
+    not_last = jnp.where(me < n_seg - 1, 1.0, 0.0)
 
     def ends(c, x):
         at = slice((x + 1) * LANES, (x + 2) * LANES)
@@ -372,8 +378,8 @@
         us.append(not_last * (ur_ref[c] - ends(c, wide)))
         for x in range(wide):
             at = slice(x * LANES, (x + 1) * LANES)
-            beside = beside_in_layer(us[x]) + (us[x + 1] if x + 1 == wide else 2.0 * us[x + 1])
-            uau = uau + us[x] * ((6.0 + k_ref[at, :]) * us[x] - beside)
+            beside = before_in_layer(us[x]) + us[x + 1]
+            uau = uau + us[x] * ((6.0 + k_ref[at, :]) * us[x] - 2.0 * beside)
     line = iota((1, LANES), 1)
     sums = jnp.where(line == 3, -2.0 * crossing, 0.0)
     for i, part in enumerate((bb, bu, uu, uau)):
@@ -465,7 +471,7 @@
         correction_ref[c] = on_b * b_ref[c] + on_u * u_ref[c]
 
 
-def call(kernel, out, scratch=(), smem=0, inputs=0, flops=0, moved=0):
+def call(kernel, out, scratch=(), smem=0, inputs=0, flops=0, moved=0, limit=VMEM_LIMIT):
     vmem = pl.BlockSpec(memory_space=pltpu.VMEM)
     ints = pl.BlockSpec(memory_space=pltpu.SMEM)
     shapes = []
@@ -478,7 +484,7 @@
         in_specs=[ints] * smem + [vmem] * inputs,
         out_specs=vmem if single else (vmem,) * len(shapes),
         scratch_shapes=list(scratch),
-        compiler_params=pltpu.CompilerParams(vmem_limit_bytes=VMEM_LIMIT),
+        compiler_params=pltpu.CompilerParams(vmem_limit_bytes=limit),
         cost_estimate=pl.CostEstimate(flops=flops, bytes_accessed=moved, transcendentals=0),
     )
 
@@ -510,12 +516,13 @@
     spreaded = pltpu.VMEM((3, CHUNK, LANES), F32)
     cols = pltpu.VMEM((6 * LANES, q_dev), BF16)
 
-    segs = jnp.concatenate([seg_pos, burgers], axis=0)
-    packed = call(pack_kernel, [(n_seg, ROWS, s_dev)], smem=1, inputs=2)(where, segs, tile)
+    packed = call(
+        pack_kernel, [(n_seg, ROWS, s_dev)], smem=1, inputs=3, limit=PACK_LIMIT
+    )(where, seg_pos, burgers, tile)
     groups = lax.all_to_all(packed, "seg", 0, 0, tiled=True)
     kq, kz, hot = call(
         prepare_kernel, [line, face, jax.ShapeDtypeStruct((rows + LANES, q_dev), BF16)],
-        [pltpu.VMEM((LANES, 2 * rows), BF16)], smem=1, inputs=2, flops=10**9, moved=10**6,
+        [pltpu.VMEM((LANES, 2 * rows), BF16)], smem=1, inputs=2, flops=10**9, moved=10**6, limit=PACK_LIMIT,
     )(where, nodes, stiff)
 
     def traction(*refs):
@@ -525,7 +532,7 @@
     t, sent, kept = call(
         traction, [line, (ROWS, q_dev // 2), weights], [sbuf, spreaded, pltpu.VMEM((2 * ROWS, q_dev), F32)], inputs=3,
         flops=10**10, moved=10**6,
-    )(groups, points, kq)
+    )(groups, points, kq[0:1])
     from_left = lax.ppermute(sent, "seg", up_seg)
     from_right = lax.ppermute(sent, "seg", down_seg)
 

time: 83.3 us -> 82.4 us (0.989)
  local copies, waits for them, and re-layouts: 4.08 us -> 0.89 us
  Pallas kernels: 29.7 us -> 30.8 us
  starting transfers between devices: 15.6 us -> 16.5 us
    unnamed x18 -> x14, local copies, waits for them, and re-layouts: 4.07 us -> 0.04 us
    pallas_call x1, Pallas kernels: 1.94 us -> 3.94 us  [shards(): call(prepare_kernel, [line, face, jax.ShapeDtypeStruct((rows + LANES, q_d...]
    ppermute x1, starting transfers between devices: 5.19 us -> 6.13 us  [shards(): above = lax.ppermute(down, 'fe', down_fe)]
    slice x0 -> x1, local copies, waits for them, and re-layouts: none -> 0.84 us  [shards(): kq[0:1]]
  transfers between devices with their start and end apart: 5 -> 5, of which waited for: 2 -> 2; matrix products, arithmetic and copies ran while one was open for 0% -> 1% of each run, Pallas kernels for 12% -> 15%
where the time goes in v5:
time: 82.4 us; the launch traced here: 82.1 us
  Pallas kernels  30.8 us (37%)
  blocking collectives  28.2 us (34%)
  starting transfers between devices  16.5 us (20%)
  waiting for transfers between devices  4.35 us (5%)
  local copies, waits for them, and re-layouts  0.89 us (1%)
    all_to_all x1, blocking collectives, shards(): partial = lax.all_to_all(partial, 'seg', 0, 0, tiled=True)  14.6 us
    all_to_all x1, blocking collectives, shards(): partial = lax.all_to_all(partial, 'fe', 0, 0, tiled=True)  13.6 us
    all_to_all x1, starting transfers between devices, shards(): groups = lax.all_to_all(packed, 'seg', 0, 0, tiled=True)  8.59 us
    ppermute x1, starting transfers between devices, shards(): above = lax.ppermute(down, 'fe', down_fe)  6.13 us
    pallas_call x1, Pallas kernels, shards(): call(traction, [line, (ROWS, q_dev // 2), weights], [sbuf, spreaded, pltp...  5.85 us
    pallas_call x1, Pallas kernels, shards(): call(scatter_kernel, [field, line, face, face, face], [cols, pltpu.VMEM((...  5.03 us
    pallas_call x1, Pallas kernels, shards(): call(prepare_kernel, [line, face, jax.ShapeDtypeStruct((rows + LANES, q_d...  3.94 us
    pallas_call x1, Pallas kernels, shards(): call(fill_sides, [(12, tall, deep), message, message], [pltpu.VMEM((2 * L...  3.87 us
  transfers between devices with their start and end apart: 5, of which 2 were waited for; matrix products, arithmetic and copies ran while one was open for 1% of the time, Pallas kernels for 15%

profile of v5, /device:TPU:1, one launch (start us, length us, event | category | flops | bytes accessed | tf_op | source)
XLA Modules:
  0.0 82.1 jit_solution(11699267233658334146)
XLA Ops:
  0.6 0.0 copy-start
  0.6 0.6 pad_add_fusion.where_ref.refs_0_
  1.2 1.8 %shard_map.77 = f32[32,8,128]{2,1,0:T(8,128)} custom-call(s32[2]{0:T(128)} %pad_add_fusion.where_ref.refs_0_, f32[3,128]{1,0:T(4,128)} %pos_ref.1, f32[3,128]{1,0:T(4,128)} %burgers_ref.1, s32[1,128]{1,0:T(1,128)} %bitcast.14), custom_call_target="tpu_custom_call" | custom-call | tf_op jit(solution)/shard_map/pallas_call | solution.py:519
  3.1 8.6 %all-to-all-start = ((f32[32,8,128]{2,1,0:T(8,128)}), f32[32,8,128]{2,1,0:T(8,128)S(1)}, u32[]{:S(2)}, u32[]{:S(2)}) async-start(f32[32,8,128]{2,1,0:T(8,128)} %shard_map.77), calls=%async_computation | async-start | bytes 262144 | tf_op jit(solution)/shard_map/all_to_all | solution.py:522
  11.7 3.9 %shard_map.78 = (f32[8,2048]{1,0:T(8,128)}, f32[8,512]{1,0:T(8,128)}, bf16[640,2048]{1,0:T(8,128)(2,1)}) custom-call(s32[2]{0:T(128)} %pad_add_fusion.where_ref.refs_0_, s32[512,128]{1,0:T(8,128)} %bitcast.6, f32[512,128]{1,0:T(8,128)} %bitcast.11), custom_call_target="tpu_custom_call" | custom-call | flops 1000000000 | bytes 1000000 | tf_op jit(solution)/shard_map/pallas_call | solution.py:523
  15.6 0.8 %slice.3.refs_2_ = f32[1,2048]{1,0:T(1,128)S(1)} slice(f32[8,2048]{1,0:T(8,128)} %get-tuple-element.25), slice={[0:1], [0:2048]} | slice | bytes 16384 | tf_op jit(solution)/shard_map/slice | solution.py:535
  16.5 0.0 copy-start.2
  16.5 2.8 %all-to-all-done.refs_0_.groups_ref = f32[32,8,128]{2,1,0:T(8,128)S(1)} async-done(((f32[32,8,128]{2,1,0:T(8,128)}), f32[32,8,128]{2,1,0:T(8,128)S(1)}, u32[]{:S(2)}, u32[]{:S(2)}) %all-to-all-start) | async-done | bytes 131104 | tf_op jit(solution)/shard_map/all_to_all | solution.py:522
  19.3 5.9 %shard_map.79 = (f32[8,2048]{1,0:T(8,128)S(1)}, f32[8,1024]{1,0:T(8,128)S(1)}, bf16[8,2,256,2048]{3,2,1,0:T(8,128)(2,1)S(1)}) custom-call(f32[32,8,128]{2,1,0:T(8,128)S(1)} %all-to-all-done.refs_0_.groups_ref, f32[3,2048]{1,0:T(4,128)S(1)} %constant_dynamic-slice_fusion.refs_1_.q_ref, f32[1,2048]{1,0:T(1,128)S(1)} %slice.3.refs_2_), custom_call_target="tpu_custom_call" | custom-call | flops 10000000000 | bytes 1000000 | tf_op jit(solution)/shard_map/pallas_call | solution.py:532
  25.1 0.0 copy-start.3
  25.2 0.5 collective-permute-start.1
  25.6 1.3 %collective-permute-start = (f32[8,1024]{1,0:T(8,128)S(1)}, f32[8,1024]{1,0:T(8,128)S(1)}, u32[]{:S(2)}, u32[]{:S(2)}) collective-permute-start(f32[8,1024]{1,0:T(8,128)S(1)} %get-tuple-element.30), channel_id=1, source_target_pairs={{0,8},{8,16},{16,24},{24,32},{32,40},{40,48},{48,56},{56,64},{64,7... | collective-permute-start | bytes 98312 | tf_op jit(solution)/shard_map/ppermute | solution.py:536
  27.0 5.0 %shard_map.80 = (f32[3,512,128]{2,1,0:T(8,128)S(1)}, f32[8,2048]{1,0:T(8,128)S(1)}, f32[8,512]{1,0:T(8,128)S(1)}, f32[8,512]{1,0:T(8,128)S(1)}, f32[8,512]{1,0:T(8,128)S(1)}) custom-call(s32[2]{0:T(128)S(1)} %copy-done.4, s32[512,128]{1,0:T(8,128)S(1)} %bitcast.7, f32[8,2048]{1,0:T(8,128)S(1)} %get-tuple-element.27.t_ref, bf16[640,2048]{1,0:T(8,128)(2,1)S(1)} %copy-done.1), custom_call_target="tpu_custom_call" | custom-call | flops 4000000000 | bytes 4000000 | tf_op jit(solution)/shard_map/pallas_call | solution.py:539
  32.1 3.9 %shard_map.81 = (f32[12,128,128]{2,1,0:T(8,128)S(1)}, f32[8,768]{1,0:T(8,128)S(1)}, f32[8,768]{1,0:T(8,128)S(1)}) custom-call(s32[2]{0:T(128)S(1)} %copy-done.4, s32[512,128]{1,0:T(8,128)S(1)} %bitcast.8, f32[8,1024]{1,0:T(8,128)S(1)} %collective-permute-done.refs_2_, f32[8,1024]{1,0:T(8,128)S(1)} %collective-permute-done.1.refs_3_, ...), custom_call_target="tpu_custom_call" | custom-call | flops 2000000000 | bytes 1000000 | tf_op jit(solution)/shard_map/pallas_call | solution.py:547
  35.9 6.1 %collective-permute-start.2 = (f32[8,768]{1,0:T(8,128)S(1)}, f32[8,768]{1,0:T(8,128)S(1)}, u32[]{:S(2)}, u32[]{:S(2)}) collective-permute-start(f32[8,768]{1,0:T(8,128)S(1)} %get-tuple-element.39), channel_id=1, source_target_pairs={{1,0},{2,1},{3,2},{4,3},{5,4},{6,5},{7,6},{0,7},{9,8},{10,9},{11,1... | collective-permute-start | bytes 73736 | tf_op jit(solution)/shard_map/ppermute | solution.py:552
  42.1 3.0 %shard_map.82 = (f32[3,512,128]{2,1,0:T(8,128)S(1)}, f32[3,128,128]{2,1,0:T(8,128)S(1)}, f32[8,2048]{1,0:T(8,128)S(1)}, f32[8,512]{1,0:T(8,128)S(1)}) custom-call(s32[2]{0:T(128)S(1)} %copy-done.4, s32[512,128]{1,0:T(8,128)S(1)} %bitcast.9, f32[3,512,128]{2,1,0:T(8,128)S(1)} %get-tuple-element.29.b_ref.refs_2_.refs_1_, ...), custom_call_target="tpu_custom_call" | custom-call | flops 4000000000 | bytes 4000000 | tf_op jit(solution)/shard_map/pallas_call | solution.py:554
  45.1 1.6 %collective-permute-done.3.refs_7_ = f32[8,768]{1,0:T(8,128)S(1)} collective-permute-done((f32[8,768]{1,0:T(8,128)S(1)}, f32[8,768]{1,0:T(8,128)S(1)}, u32[]{:S(2)}, u32[]{:S(2)}) %collective-permute-start.3) | collective-permute-done | bytes 24608 | tf_op jit(solution)/shard_map/ppermute | solution.py:553
  46.6 2.0 %shard_map.83 = (f32[3,512,128]{2,1,0:T(8,128)S(1)}, f32[8,2048]{1,0:T(8,128)S(1)}, f32[8,128]{1,0:T(8,128)S(1)}) custom-call(s32[2]{0:T(128)S(1)} %copy-done.4, s32[512,128]{1,0:T(8,128)S(1)} %bitcast.10, f32[3,512,128]{2,1,0:T(8,128)S(1)} %get-tuple-element.29.b_ref.refs_2_.refs_1_, f32[3,512,128]{2,1,0:T(8,128)S(1)} %get-tuple-element.37.refs_3_, ...), custom_call_target="tpu_custom_call" | custom-call | flops 1000000000 | bytes 4000000 | tf_op jit(solution)/shard_map/pallas_call | solution.py:562
  48.7 0.0 copy-start.5
  48.7 3.3 %shard_map.84 = f32[32,8,128]{2,1,0:T(8,128)S(1)} custom-call(f32[32,8,128]{2,1,0:T(8,128)S(1)} %all-to-all-done.refs_0_.groups_ref, bf16[8,2,256,2048]{3,2,1,0:T(8,128)(2,1)S(1)} %get-tuple-element.26.kept_ref, f32[3,2048]{1,0:T(4,128)S(1)} %constant_dynamic-slice_fusion.refs_1_.q_ref, f32[8,2048]{1,0:T(8,128)S(1)} %get-tuple-element.43.g_ref, ...), custom_call_target="tpu_custom_call" | custom-call | flops 10000000000 | bytes 1000000 | tf_op jit(solution)/shard_map/pallas_call | solution.py:565
  52.0 14.6 %all_to_all.15.partial_ref = f32[32,8,128]{2,1,0:T(8,128)S(1)} all-to-all(f32[32,8,128]{2,1,0:T(8,128)S(1)} %shard_map.84), channel_id=1, replica_groups=mesh['seg'=32,'fe'=8] {'seg'}, dimensions={0} | all-to-all | bytes 262144 | tf_op jit(solution)/shard_map/all_to_all | solution.py:570
  66.6 0.8 shard_map.85
  67.4 13.6 %all_to_all.16.refs_0_ = f32[8,8,128]{2,1,0:T(8,128)S(1)} all-to-all(f32[8,8,128]{2,1,0:T(8,128)S(1)} %shard_map.85), channel_id=1, replica_groups=mesh['seg'=32,'fe'=8] {'fe'}, dimensions={0} | all-to-all | bytes 65536 | tf_op jit(solution)/shard_map/all_to_all | solution.py:572
  81.0 1.2 %shard_map.86 = (f32[3,512,128]{2,1,0:T(8,128)}, f32[3,128]{1,0:T(4,128)}) custom-call(f32[8,8,128]{2,1,0:T(8,128)S(1)} %all_to_all.16.refs_0_, f32[3,512,128]{2,1,0:T(8,128)S(1)} %get-tuple-element.29.b_ref.refs_2_.refs_1_, f32[3,512,128]{2,1,0:T(8,128)S(1)} %get-tuple-element.45.refs_2_), custom_call_target="tpu_custom_call" | custom-call | tf_op jit(solution)/shard_map/pallas_call | solution.py:577
  (15 shorter events, 0.0 us)
Async XLA Ops:
  0.6 15.8 %copy-start = (f32[3,65536]{1,0:T(4,128)S(1)}, f32[3,65536]{1,0:T(4,128)}, u32[]{:S(2)}) copy-start(f32[3,65536]{1,0:T(4,128)} %param.9) | copy-start | bytes 2359300
  3.1 16.2 %all-to-all-start = ((f32[32,8,128]{2,1,0:T(8,128)}), f32[32,8,128]{2,1,0:T(8,128)S(1)}, u32[]{:S(2)}, u32[]{:S(2)}) async-start(f32[32,8,128]{2,1,0:T(8,128)} %shard_map.77), calls=%async_computation | async-start | bytes 262144 | tf_op jit(solution)/shard_map/all_to_all | solution.py:522
  16.5 10.5 %copy-start.2 = (s32[65536]{0:T(1024)S(1)}, s32[65536]{0:T(1024)}, u32[]{:S(2)}) copy-start(s32[65536]{0:T(1024)} %param.10) | copy-start | bytes 786436
  16.5 10.5 %copy-start.4 = (s32[2]{0:T(128)S(1)}, s32[2]{0:T(128)}, u32[]{:S(2)}) copy-start(s32[2]{0:T(128)} %pad_add_fusion.where_ref.refs_0_) | copy-start | bytes 28
  16.5 15.6 %copy-start.6 = (f32[8,512]{1,0:T(8,128)S(1)}, f32[8,512]{1,0:T(8,128)}, u32[]{:S(2)}) copy-start(f32[8,512]{1,0:T(8,128)} %get-tuple-element.34.refs_7_) | copy-start | bytes 49156
  19.3 7.7 %copy-start.1 = (bf16[640,2048]{1,0:T(8,128)(2,1)S(1)}, bf16[640,2048]{1,0:T(8,128)(2,1)}, u32[]{:S(2)}) copy-start(bf16[640,2048]{1,0:T(8,128)(2,1)} %get-tuple-element.28.hot_ref.refs_11_) | copy-start | bytes 7864324
  25.1 16.9 %copy-start.3 = (f32[4,128,128]{2,1,0:T(8,128)S(1)}, f32[4,128,128]{2,1,0:T(8,128)}, u32[]{:S(2)}) copy-start(f32[4,128,128]{2,1,0:T(8,128)} %param.11) | copy-start | bytes 786436
  25.2 6.9 %collective-permute-start.1 = (f32[8,1024]{1,0:T(8,128)S(1)}, f32[8,1024]{1,0:T(8,128)S(1)}, u32[]{:S(2)}, u32[]{:S(2)}) collective-permute-start(f32[8,1024]{1,0:T(8,128)S(1)} %get-tuple-element.30), channel_id=1, source_target_pairs={{8,0},{16,8},{24,16},{32,24},{40,32},{48,40},{56,48},{64,56},{72,6... | collective-permute-start | bytes 98312 | tf_op jit(solution)/shard_map/ppermute | solution.py:537
  25.6 6.4 %collective-permute-start = (f32[8,1024]{1,0:T(8,128)S(1)}, f32[8,1024]{1,0:T(8,128)S(1)}, u32[]{:S(2)}, u32[]{:S(2)}) collective-permute-start(f32[8,1024]{1,0:T(8,128)S(1)} %get-tuple-element.30), channel_id=1, source_target_pairs={{0,8},{8,16},{16,24},{24,32},{32,40},{40,48},{48,56},{56,64},{64,7... | collective-permute-start | bytes 98312 | tf_op jit(solution)/shard_map/ppermute | solution.py:536
  35.9 9.1 %collective-permute-start.2 = (f32[8,768]{1,0:T(8,128)S(1)}, f32[8,768]{1,0:T(8,128)S(1)}, u32[]{:S(2)}, u32[]{:S(2)}) collective-permute-start(f32[8,768]{1,0:T(8,128)S(1)} %get-tuple-element.39), channel_id=1, source_target_pairs={{1,0},{2,1},{3,2},{4,3},{5,4},{6,5},{7,6},{0,7},{9,8},{10,9},{11,1... | collective-permute-start | bytes 73736 | tf_op jit(solution)/shard_map/ppermute | solution.py:552
  42.1 4.6 %collective-permute-start.3 = (f32[8,768]{1,0:T(8,128)S(1)}, f32[8,768]{1,0:T(8,128)S(1)}, u32[]{:S(2)}, u32[]{:S(2)}) collective-permute-start(f32[8,768]{1,0:T(8,128)S(1)} %get-tuple-element.40), channel_id=1, source_target_pairs={{0,1},{1,2},{2,3},{3,4},{4,5},{5,6},{6,7},{7,0},{8,9},{9,10},{10,1... | collective-permute-start | bytes 73736 | tf_op jit(solution)/shard_map/ppermute | solution.py:553
  48.7 17.9 %copy-start.5 = (s32[128]{0:T(128)S(1)}, s32[128]{0:T(128)}, u32[]{:S(2)}) copy-start(s32[128]{0:T(128)} %param.8) | copy-start | bytes 1540

commit v6 on v5

--- a/solution.py
+++ b/solution.py
@@ -471,17 +471,20 @@
         correction_ref[c] = on_b * b_ref[c] + on_u * u_ref[c]
 
 
-def call(kernel, out, scratch=(), smem=0, inputs=0, flops=0, moved=0, limit=VMEM_LIMIT):
+def call(kernel, out, scratch=(), placed=False, inputs=0, flops=0, moved=0, limit=VMEM_LIMIT):
     vmem = pl.BlockSpec(memory_space=pltpu.VMEM)
-    ints = pl.BlockSpec(memory_space=pltpu.SMEM)
     shapes = []
     for o in out:
         shapes.append(o if isinstance(o, jax.ShapeDtypeStruct) else jax.ShapeDtypeStruct(o, F32))
     single = len(shapes) == 1
+
+    def with_place(*refs):
+        kernel((lax.axis_index("seg"), lax.axis_index("fe")), *refs)
+
     return pl.pallas_call(
-        kernel,
+        with_place if placed else kernel,
         out_shape=shapes[0] if single else tuple(shapes),
-        in_specs=[ints] * smem + [vmem] * inputs,
+        in_specs=[vmem] * inputs,
         out_specs=vmem if single else (vmem,) * len(shapes),
         scratch_shapes=list(scratch),
         compiler_params=pltpu.CompilerParams(vmem_limit_bytes=limit),
@@ -491,7 +494,7 @@
 
 def shards(seg_pos, burgers, seg_tile, quad_pos, quad_node, stiffness):
     n_seg, n_fe = lax.axis_size("seg"), lax.axis_size("fe")
-    column, block = lax.axis_index("seg"), lax.axis_index("fe")
+    column = lax.axis_index("seg")
     s_dev = seg_pos.shape[1]
     q_block = quad_pos.shape[1]
     q_dev = q_block // n_seg
@@ -499,7 +502,6 @@
     total_points = q_block * n_fe
     wide, tall, deep = stiffness.shape
     rows = wide * tall
-    where = jnp.stack([column, block]).astype(jnp.int32)
     tile = seg_tile.reshape(1, s_dev)
     nodes = quad_node.reshape(q_block // LANES, LANES)
     points = lax.dynamic_slice_in_dim(quad_pos, column * q_dev, q_dev, 1)
@@ -517,13 +519,13 @@
     cols = pltpu.VMEM((6 * LANES, q_dev), BF16)
 
     packed = call(
-        pack_kernel, [(n_seg, ROWS, s_dev)], smem=1, inputs=3, limit=PACK_LIMIT
-    )(where, seg_pos, burgers, tile)
+        pack_kernel, [(n_seg, ROWS, s_dev)], placed=True, inputs=3, limit=PACK_LIMIT
+    )(seg_pos, burgers, tile)
     groups = lax.all_to_all(packed, "seg", 0, 0, tiled=True)
     kq, kz, hot = call(
         prepare_kernel, [line, face, jax.ShapeDtypeStruct((rows + LANES, q_dev), BF16)],
-        [pltpu.VMEM((LANES, 2 * rows), BF16)], smem=1, inputs=2, flops=10**9, moved=10**6, limit=PACK_LIMIT,
-    )(where, nodes, stiff)
+        [pltpu.VMEM((LANES, 2 * rows), BF16)], placed=True, inputs=2, flops=10**9, moved=10**6, limit=PACK_LIMIT,
+    )(nodes, stiff)
 
     def traction(*refs):
         traction_kernel(STRENGTH / math.sqrt(total_segs), *refs)
@@ -538,8 +540,8 @@
 
     b, g, low, after, high = call(
         scatter_kernel, [field, line, face, face, face], [cols, pltpu.VMEM((3 * LANES, 2 * rows), BF16)],
-        smem=1, inputs=3, flops=4 * 10**9, moved=4 * 10**6,
-    )(where, nodes, t, hot)
+        placed=True, inputs=3, flops=4 * 10**9, moved=4 * 10**6,
+    )(nodes, t, hot)
 
     def fill_sides(*refs):
         sides_kernel(n_seg, *refs)
@@ -547,28 +549,28 @@
     sides, down, up = call(
         fill_sides, [(12, tall, deep), message, message],
         [pltpu.VMEM((2 * LANES, q_dev), BF16), pltpu.VMEM((LANES, q_dev), BF16), cols],
-        smem=1, inputs=7, flops=2 * 10**9, moved=10**6,
-    )(where, nodes, from_left, from_right, low, after, high, kz)
+        placed=True, inputs=7, flops=2 * 10**9, moved=10**6,
+    )(nodes, from_left, from_right, low, after, high, kz)
     above = lax.ppermute(down, "fe", down_fe)
     below = lax.ppermute(up, "fe", up_fe)
     u, ur, g, uh = call(
         operate_kernel, [field, (3, tall, deep), line, face], [pltpu.VMEM((3 * LANES, 2 * rows), BF16)],
-        smem=1, inputs=6, flops=4 * 10**9, moved=4 * 10**6,
-    )(where, nodes, b, sides, stiff, g, hot)
+        placed=True, inputs=6, flops=4 * 10**9, moved=4 * 10**6,
+    )(nodes, b, sides, stiff, g, hot)
 
     def fill_ends(*refs):
         ends_kernel(n_seg, n_fe, *refs)
 
     u, motion, sums = call(
-        fill_ends, [field, line, (ROWS, LANES)], smem=1, inputs=11, flops=10**9, moved=4 * 10**6
-    )(where, nodes, b, u, ur, stiff, above, below, uh, high, g, hot)
+        fill_ends, [field, line, (ROWS, LANES)], placed=True, inputs=11, flops=10**9, moved=4 * 10**6
+    )(nodes, b, u, ur, stiff, above, below, uh, high, g, hot)
     partial = call(
         stress_kernel, [(n_seg, ROWS, s_dev)],
         [sbuf, spreaded, pltpu.VMEM((long, LANES), F32), pltpu.VMEM((2 * ROWS, q_dev), BF16)],
         inputs=5, flops=10**10, moved=10**6,
     )(groups, kept, points, motion, sums)
     partial = lax.all_to_all(partial, "seg", 0, 0, tiled=True)
-    partial = call(unpack_kernel, [(n_fe, ROWS, s_dev)], smem=1, inputs=2)(where, tile, partial)
+    partial = call(unpack_kernel, [(n_fe, ROWS, s_dev)], placed=True, inputs=2)(tile, partial)
     partial = lax.all_to_all(partial, "fe", 0, 0, tiled=True)
 
     def finish(*refs):

time: 82.4 us -> 78.8 us (0.956)
  Pallas kernels: 30.8 us -> 28 us
    pallas_call x3, Pallas kernels: 4.64 us -> 3.53 us  [the longest x1 1.8 us: shards(): call(pack_kernel, [(n_seg, ROWS, s_dev)], placed=True, inputs=3, limit=PA...]
  transfers between devices with their start and end apart: 5 -> 5, of which waited for: 2 -> 2; matrix products, arithmetic and copies ran while one was open for 1% -> 1% of each run, Pallas kernels for 15% -> 14%
where the time goes in v6:
time: 78.8 us
  Pallas kernels  28 us (36%)
  blocking collectives  27.7 us (35%)
  starting transfers between devices  16.5 us (21%)
  waiting for transfers between devices  4.88 us (6%)
  local copies, waits for them, and re-layouts  0.89 us (1%)
    all_to_all x1, blocking collectives, shards(): partial = lax.all_to_all(partial, 'seg', 0, 0, tiled=True)  14.6 us
    all_to_all x1, blocking collectives, shards(): partial = lax.all_to_all(partial, 'fe', 0, 0, tiled=True)  13.1 us
    all_to_all x1, starting transfers between devices, shards(): groups = lax.all_to_all(packed, 'seg', 0, 0, tiled=True)  8.59 us
    ppermute x1, starting transfers between devices, shards(): above = lax.ppermute(down, 'fe', down_fe)  6.13 us
    pallas_call x1, Pallas kernels, shards(): call(traction, [line, (ROWS, q_dev // 2), weights], [sbuf, spreaded, pltp...  5.82 us
    pallas_call x1, Pallas kernels, shards(): call(scatter_kernel, [field, line, face, face, face], [cols, pltpu.VMEM((...  4.49 us
    pallas_call x1, Pallas kernels, shards(): call(prepare_kernel, [line, face, jax.ShapeDtypeStruct((rows + LANES, q_d...  3.94 us
    pallas_call x1, Pallas kernels, shards(): call(fill_sides, [(12, tall, deep), message, message], [pltpu.VMEM((2 * L...  3.33 us
  transfers between devices with their start and end apart: 5, of which 2 were waited for; matrix products, arithmetic and copies ran while one was open for 1% of the time, Pallas kernels for 14%

profile of v6, /device:TPU:1, one launch (start us, length us, event | category | flops | bytes accessed | tf_op | source)
XLA Modules:
  0.0 78.8 jit_solution(16900511704531845154)
XLA Ops:
  0.6 0.0 copy-start
  0.6 1.8 %shard_map.77 = f32[32,8,128]{2,1,0:T(8,128)} custom-call(f32[3,128]{1,0:T(4,128)} %refs_0_.1, f32[3,128]{1,0:T(4,128)} %refs_1_.1, s32[1,128]{1,0:T(1,128)} %bitcast.12), custom_call_target="tpu_custom_call" | custom-call | tf_op jit(solution)/shard_map/pallas_call | solution.py:521
  2.4 8.6 %all-to-all-start = ((f32[32,8,128]{2,1,0:T(8,128)}), f32[32,8,128]{2,1,0:T(8,128)S(1)}, u32[]{:S(2)}, u32[]{:S(2)}) async-start(f32[32,8,128]{2,1,0:T(8,128)} %shard_map.77), calls=%async_computation | async-start | bytes 262144 | tf_op jit(solution)/shard_map/all_to_all | solution.py:524
  11.0 3.9 %shard_map.78 = (f32[8,2048]{1,0:T(8,128)}, f32[8,512]{1,0:T(8,128)}, bf16[640,2048]{1,0:T(8,128)(2,1)}) custom-call(s32[512,128]{1,0:T(8,128)} %bitcast.4, f32[512,128]{1,0:T(8,128)} %bitcast.9), custom_call_target="tpu_custom_call" | custom-call | flops 1000000000 | bytes 1000000 | tf_op jit(solution)/shard_map/pallas_call | solution.py:525
  15.0 0.8 %slice.3.refs_2_ = f32[1,2048]{1,0:T(1,128)S(1)} slice(f32[8,2048]{1,0:T(8,128)} %get-tuple-element.25), slice={[0:1], [0:2048]} | slice | bytes 16384 | tf_op jit(solution)/shard_map/slice | solution.py:537
  15.8 0.0 copy-start.2
  15.9 2.8 %all-to-all-done.refs_0_.groups_ref = f32[32,8,128]{2,1,0:T(8,128)S(1)} async-done(((f32[32,8,128]{2,1,0:T(8,128)}), f32[32,8,128]{2,1,0:T(8,128)S(1)}, u32[]{:S(2)}, u32[]{:S(2)}) %all-to-all-start) | async-done | bytes 131104 | tf_op jit(solution)/shard_map/all_to_all | solution.py:524
  18.7 5.8 %shard_map.79 = (f32[8,2048]{1,0:T(8,128)S(1)}, f32[8,1024]{1,0:T(8,128)S(1)}, bf16[8,2,256,2048]{3,2,1,0:T(8,128)(2,1)S(1)}) custom-call(f32[32,8,128]{2,1,0:T(8,128)S(1)} %all-to-all-done.refs_0_.groups_ref, f32[3,2048]{1,0:T(4,128)S(1)} %constant_dynamic-slice_fusion.refs_1_.q_ref, f32[1,2048]{1,0:T(1,128)S(1)} %slice.3.refs_2_), custom_call_target="tpu_custom_call" | custom-call | flops 10000000000 | bytes 1000000 | tf_op jit(solution)/shard_map/pallas_call | solution.py:534
  24.5 0.0 copy-start.3
  24.5 0.5 collective-permute-start.1
  25.0 1.3 %collective-permute-start = (f32[8,1024]{1,0:T(8,128)S(1)}, f32[8,1024]{1,0:T(8,128)S(1)}, u32[]{:S(2)}, u32[]{:S(2)}) collective-permute-start(f32[8,1024]{1,0:T(8,128)S(1)} %get-tuple-element.30), channel_id=1, source_target_pairs={{0,8},{8,16},{16,24},{24,32},{32,40},{40,48},{48,56},{56,64},{64,7... | collective-permute-start | bytes 98312 | tf_op jit(solution)/shard_map/ppermute | solution.py:538
  26.3 4.5 %shard_map.80 = (f32[3,512,128]{2,1,0:T(8,128)S(1)}, f32[8,2048]{1,0:T(8,128)S(1)}, f32[8,512]{1,0:T(8,128)S(1)}, f32[8,512]{1,0:T(8,128)S(1)}, f32[8,512]{1,0:T(8,128)S(1)}) custom-call(s32[512,128]{1,0:T(8,128)S(1)} %bitcast.5, f32[8,2048]{1,0:T(8,128)S(1)} %get-tuple-element.27.refs_1_, bf16[640,2048]{1,0:T(8,128)(2,1)S(1)} %copy-done.1), custom_call_target="tpu_custom_call" | custom-call | flops 4000000000 | bytes 4000000 | tf_op jit(solution)/shard_map/pallas_call | solution.py:541
  30.9 0.0 collective-permute-done.refs_1_
  30.9 3.3 %shard_map.81 = (f32[12,128,128]{2,1,0:T(8,128)S(1)}, f32[8,768]{1,0:T(8,128)S(1)}, f32[8,768]{1,0:T(8,128)S(1)}) custom-call(s32[512,128]{1,0:T(8,128)S(1)} %bitcast.6, f32[8,1024]{1,0:T(8,128)S(1)} %collective-permute-done.refs_1_, f32[8,1024]{1,0:T(8,128)S(1)} %collective-permute-done.1.refs_2_, f32[8,512]{1,0:T(8,128)S(1)} %get-tuple-element.31.refs_3_, ...), custom_call_target="tpu_custom_call" | custom-call | flops 2000000000 | bytes 1000000 | tf_op jit(solution)/shard_map/pallas_call | solution.py:549
  34.2 6.1 %collective-permute-start.2 = (f32[8,768]{1,0:T(8,128)S(1)}, f32[8,768]{1,0:T(8,128)S(1)}, u32[]{:S(2)}, u32[]{:S(2)}) collective-permute-start(f32[8,768]{1,0:T(8,128)S(1)} %get-tuple-element.39), channel_id=1, source_target_pairs={{1,0},{2,1},{3,2},{4,3},{5,4},{6,5},{7,6},{0,7},{9,8},{10,9},{11,1... | collective-permute-start | bytes 73736 | tf_op jit(solution)/shard_map/ppermute | solution.py:554
  40.4 2.5 %shard_map.82 = (f32[3,512,128]{2,1,0:T(8,128)S(1)}, f32[3,128,128]{2,1,0:T(8,128)S(1)}, f32[8,2048]{1,0:T(8,128)S(1)}, f32[8,512]{1,0:T(8,128)S(1)}) custom-call(s32[512,128]{1,0:T(8,128)S(1)} %bitcast.7, f32[3,512,128]{2,1,0:T(8,128)S(1)} %get-tuple-element.29.refs_1_, f32[12,128,128]{2,1,0:T(8,128)S(1)} %get-tuple-element.35.refs_2_, ...), custom_call_target="tpu_custom_call" | custom-call | flops 4000000000 | bytes 4000000 | tf_op jit(solution)/shard_map/pallas_call | solution.py:556
  42.8 2.1 %collective-permute-done.3.refs_6_ = f32[8,768]{1,0:T(8,128)S(1)} collective-permute-done((f32[8,768]{1,0:T(8,128)S(1)}, f32[8,768]{1,0:T(8,128)S(1)}, u32[]{:S(2)}, u32[]{:S(2)}) %collective-permute-start.3) | collective-permute-done | bytes 24608 | tf_op jit(solution)/shard_map/ppermute | solution.py:555
  44.9 1.5 %shard_map.83 = (f32[3,512,128]{2,1,0:T(8,128)S(1)}, f32[8,2048]{1,0:T(8,128)S(1)}, f32[8,128]{1,0:T(8,128)S(1)}) custom-call(s32[512,128]{1,0:T(8,128)S(1)} %bitcast.8, f32[3,512,128]{2,1,0:T(8,128)S(1)} %get-tuple-element.29.refs_1_, f32[3,512,128]{2,1,0:T(8,128)S(1)} %get-tuple-element.37.refs_2_, f32[3,128,128]{2,1,0:T(8,128)S(1)} %get-tuple-element.38.refs_3_, ...), custom_call_target="tpu_custom_call" | custom-call | flops 1000000000 | bytes 4000000 | tf_op jit(solution)/shard_map/pallas_call | solution.py:564
  46.4 0.0 copy-start.4
  46.4 3.3 %shard_map.84 = f32[32,8,128]{2,1,0:T(8,128)S(1)} custom-call(f32[32,8,128]{2,1,0:T(8,128)S(1)} %all-to-all-done.refs_0_.groups_ref, bf16[8,2,256,2048]{3,2,1,0:T(8,128)(2,1)S(1)} %get-tuple-element.26.kept_ref, f32[3,2048]{1,0:T(4,128)S(1)} %constant_dynamic-slice_fusion.refs_1_.q_ref, f32[8,2048]{1,0:T(8,128)S(1)} %get-tuple-element.43.g_ref, ...), custom_call_target="tpu_custom_call" | custom-call | flops 10000000000 | bytes 1000000 | tf_op jit(solution)/shard_map/pallas_call | solution.py:567
  49.7 14.6 %all_to_all.15.refs_1_ = f32[32,8,128]{2,1,0:T(8,128)S(1)} all-to-all(f32[32,8,128]{2,1,0:T(8,128)S(1)} %shard_map.84), channel_id=1, replica_groups=mesh['seg'=32,'fe'=8] {'seg'}, dimensions={0} | all-to-all | bytes 262144 | tf_op jit(solution)/shard_map/all_to_all | solution.py:572
  64.2 0.3 shard_map.85
  64.5 13.1 %all_to_all.16.refs_0_ = f32[8,8,128]{2,1,0:T(8,128)S(1)} all-to-all(f32[8,8,128]{2,1,0:T(8,128)S(1)} %shard_map.85), channel_id=1, replica_groups=mesh['seg'=32,'fe'=8] {'fe'}, dimensions={0} | all-to-all | bytes 65536 | tf_op jit(solution)/shard_map/all_to_all | solution.py:574
  77.6 1.2 %shard_map.86 = (f32[3,512,128]{2,1,0:T(8,128)}, f32[3,128]{1,0:T(4,128)}) custom-call(f32[8,8,128]{2,1,0:T(8,128)S(1)} %all_to_all.16.refs_0_, f32[3,512,128]{2,1,0:T(8,128)S(1)} %get-tuple-element.29.refs_1_, f32[3,512,128]{2,1,0:T(8,128)S(1)} %get-tuple-element.45.refs_2_), custom_call_target="tpu_custom_call" | custom-call | tf_op jit(solution)/shard_map/pallas_call | solution.py:579
  (12 shorter events, 0.0 us)
Async XLA Ops:
  0.6 15.2 %copy-start = (f32[3,65536]{1,0:T(4,128)S(1)}, f32[3,65536]{1,0:T(4,128)}, u32[]{:S(2)}) copy-start(f32[3,65536]{1,0:T(4,128)} %param.9) | copy-start | bytes 2359300
  2.4 16.2 %all-to-all-start = ((f32[32,8,128]{2,1,0:T(8,128)}), f32[32,8,128]{2,1,0:T(8,128)S(1)}, u32[]{:S(2)}, u32[]{:S(2)}) async-start(f32[32,8,128]{2,1,0:T(8,128)} %shard_map.77), calls=%async_computation | async-start | bytes 262144 | tf_op jit(solution)/shard_map/all_to_all | solution.py:524
  15.8 10.5 %copy-start.2 = (s32[65536]{0:T(1024)S(1)}, s32[65536]{0:T(1024)}, u32[]{:S(2)}) copy-start(s32[65536]{0:T(1024)} %param.10) | copy-start | bytes 786436
  15.9 15.0 %copy-start.5 = (f32[8,512]{1,0:T(8,128)S(1)}, f32[8,512]{1,0:T(8,128)}, u32[]{:S(2)}) copy-start(f32[8,512]{1,0:T(8,128)} %get-tuple-element.34.refs_6_) | copy-start | bytes 49156
  18.7 7.7 %copy-start.1 = (bf16[640,2048]{1,0:T(8,128)(2,1)S(1)}, bf16[640,2048]{1,0:T(8,128)(2,1)}, u32[]{:S(2)}) copy-start(bf16[640,2048]{1,0:T(8,128)(2,1)} %get-tuple-element.28.refs_2_.refs_5_.refs_10_) | copy-start | bytes 7864324
  24.5 15.8 %copy-start.3 = (f32[4,128,128]{2,1,0:T(8,128)S(1)}, f32[4,128,128]{2,1,0:T(8,128)}, u32[]{:S(2)}) copy-start(f32[4,128,128]{2,1,0:T(8,128)} %param.11) | copy-start | bytes 786436
  24.5 6.3 %collective-permute-start.1 = (f32[8,1024]{1,0:T(8,128)S(1)}, f32[8,1024]{1,0:T(8,128)S(1)}, u32[]{:S(2)}, u32[]{:S(2)}) collective-permute-start(f32[8,1024]{1,0:T(8,128)S(1)} %get-tuple-element.30), channel_id=1, source_target_pairs={{8,0},{16,8},{24,16},{32,24},{40,32},{48,40},{56,48},{64,56},{72,6... | collective-permute-start | bytes 98312 | tf_op jit(solution)/shard_map/ppermute | solution.py:539
  25.0 5.9 %collective-permute-start = (f32[8,1024]{1,0:T(8,128)S(1)}, f32[8,1024]{1,0:T(8,128)S(1)}, u32[]{:S(2)}, u32[]{:S(2)}) collective-permute-start(f32[8,1024]{1,0:T(8,128)S(1)} %get-tuple-element.30), channel_id=1, source_target_pairs={{0,8},{8,16},{16,24},{24,32},{32,40},{40,48},{48,56},{56,64},{64,7... | collective-permute-start | bytes 98312 | tf_op jit(solution)/shard_map/ppermute | solution.py:538
  34.2 8.6 %collective-permute-start.2 = (f32[8,768]{1,0:T(8,128)S(1)}, f32[8,768]{1,0:T(8,128)S(1)}, u32[]{:S(2)}, u32[]{:S(2)}) collective-permute-start(f32[8,768]{1,0:T(8,128)S(1)} %get-tuple-element.39), channel_id=1, source_target_pairs={{1,0},{2,1},{3,2},{4,3},{5,4},{6,5},{7,6},{0,7},{9,8},{10,9},{11,1... | collective-permute-start | bytes 73736 | tf_op jit(solution)/shard_map/ppermute | solution.py:554
  40.3 4.5 %collective-permute-start.3 = (f32[8,768]{1,0:T(8,128)S(1)}, f32[8,768]{1,0:T(8,128)S(1)}, u32[]{:S(2)}, u32[]{:S(2)}) collective-permute-start(f32[8,768]{1,0:T(8,128)S(1)} %get-tuple-element.40), channel_id=1, source_target_pairs={{0,1},{1,2},{2,3},{3,4},{4,5},{5,6},{6,7},{7,0},{8,9},{9,10},{10,1... | collective-permute-start | bytes 73736 | tf_op jit(solution)/shard_map/ppermute | solution.py:555
  46.4 17.9 %copy-start.4 = (s32[128]{0:T(128)S(1)}, s32[128]{0:T(128)}, u32[]{:S(2)}) copy-start(s32[128]{0:T(128)} %param.8) | copy-start | bytes 1540

commit v7 on v6

--- a/solution.py
+++ b/solution.py
@@ -9,7 +9,6 @@
 
 CORE = 0.0001
 STRENGTH = 0.001
-HIGH = lax.Precision.HIGHEST
 F32 = jnp.float32
 BF16 = jnp.bfloat16
 ROWS = 8
@@ -30,6 +29,12 @@
     return hi, (x - hi.astype(F32)).astype(BF16)
 
 
+def thirds(x):
+    high, rest = split(x)
+    low = (x - high.astype(F32)) - rest.astype(F32)
+    return jnp.concatenate([high, rest, low.astype(BF16)], axis=1)
+
+
 def near_rank(tile, block):
     near = jnp.abs(tile - block) <= 1
     mask = jnp.where(near, 1.0, 0.0)
@@ -44,7 +49,9 @@
     mask, place = near_rank(tile_ref[...], where_ref[1])
     rest = jnp.broadcast_to(mask, (2, mask.shape[1]))
     segs = jnp.concatenate([pos_ref[...], burgers_ref[...], rest], axis=0)
-    packed = lax.dot_general(segs, place, NT, precision=HIGH, preferred_element_type=F32)
+    place = place.astype(BF16)
+    place = jnp.concatenate([place, place, place], axis=1)
+    packed = lax.dot_general(thirds(segs), place, NT, preferred_element_type=F32)
     out_ref[...] = jnp.broadcast_to(packed[None], out_ref.shape)
 
 
@@ -451,7 +458,9 @@
 def unpack_kernel(where_ref, tile_ref, partial_ref, out_ref):
     _, place = near_rank(tile_ref[...], where_ref[1])
     total = jnp.sum(partial_ref[...], axis=0)
-    spreaded = jnp.dot(total, place, precision=HIGH, preferred_element_type=F32)
+    place = place.astype(BF16)
+    place = jnp.concatenate([place, place, place], axis=0)
+    spreaded = jnp.dot(thirds(total), place, preferred_element_type=F32)
     total = jnp.where(iota(total.shape, 0) == 6, total, spreaded)
     out_ref[...] = jnp.broadcast_to(total[None], out_ref.shape)
 

time: 78.8 us -> 79 us (level)
  no operation moved by 1% of the time
where the time goes in v7:
time: 79 us; the launch traced here: 78.7 us
  Pallas kernels  27.9 us (35%)
  blocking collectives  27.6 us (35%)
  starting transfers between devices  16.5 us (21%)
  waiting for transfers between devices  4.88 us (6%)
  local copies, waits for them, and re-layouts  0.89 us (1%)
    all_to_all x1, blocking collectives, shards(): partial = lax.all_to_all(partial, 'seg', 0, 0, tiled=True)  14.6 us
    all_to_all x1, blocking collectives, shards(): partial = lax.all_to_all(partial, 'fe', 0, 0, tiled=True)  13.1 us
    all_to_all x1, starting transfers between devices, shards(): groups = lax.all_to_all(packed, 'seg', 0, 0, tiled=True)  8.59 us
    ppermute x1, starting transfers between devices, shards(): above = lax.ppermute(down, 'fe', down_fe)  6.13 us
    pallas_call x1, Pallas kernels, shards(): call(traction, [line, (ROWS, q_dev // 2), weights], [sbuf, spreaded, pltp...  5.82 us
    pallas_call x1, Pallas kernels, shards(): call(scatter_kernel, [field, line, face, face, face], [cols, pltpu.VMEM((...  4.49 us
    pallas_call x1, Pallas kernels, shards(): call(prepare_kernel, [line, face, jax.ShapeDtypeStruct((rows + LANES, q_d...  3.94 us
    pallas_call x1, Pallas kernels, shards(): call(fill_sides, [(12, tall, deep), message, message], [pltpu.VMEM((2 * L...  3.33 us
  transfers between devices with their start and end apart: 5, of which 2 were waited for; matrix products, arithmetic and copies ran while one was open for 1% of the time, Pallas kernels for 14%

profile of v7, /device:TPU:1, one launch (start us, length us, event | category | flops | bytes accessed | tf_op | source)
XLA Modules:
  0.0 78.7 jit_solution(1588087808382499856)
XLA Ops:
  0.6 0.0 copy-start
  0.6 1.7 %shard_map.77 = f32[32,8,128]{2,1,0:T(8,128)} custom-call(f32[3,128]{1,0:T(4,128)} %refs_0_.1, f32[3,128]{1,0:T(4,128)} %refs_1_.1, s32[1,128]{1,0:T(1,128)} %bitcast.12), custom_call_target="tpu_custom_call" | custom-call | tf_op jit(solution)/shard_map/pallas_call | solution.py:530
  2.4 8.6 %all-to-all-start = ((f32[32,8,128]{2,1,0:T(8,128)}), f32[32,8,128]{2,1,0:T(8,128)S(1)}, u32[]{:S(2)}, u32[]{:S(2)}) async-start(f32[32,8,128]{2,1,0:T(8,128)} %shard_map.77), calls=%async_computation | async-start | bytes 262144 | tf_op jit(solution)/shard_map/all_to_all | solution.py:533
  11.0 3.9 %shard_map.78 = (f32[8,2048]{1,0:T(8,128)}, f32[8,512]{1,0:T(8,128)}, bf16[640,2048]{1,0:T(8,128)(2,1)}) custom-call(s32[512,128]{1,0:T(8,128)} %bitcast.4, f32[512,128]{1,0:T(8,128)} %bitcast.9), custom_call_target="tpu_custom_call" | custom-call | flops 1000000000 | bytes 1000000 | tf_op jit(solution)/shard_map/pallas_call | solution.py:534
  14.9 0.8 %slice.3.refs_2_ = f32[1,2048]{1,0:T(1,128)S(1)} slice(f32[8,2048]{1,0:T(8,128)} %get-tuple-element.25), slice={[0:1], [0:2048]} | slice | bytes 16384 | tf_op jit(solution)/shard_map/slice | solution.py:546
  15.8 0.0 copy-start.2
  15.8 2.8 %all-to-all-done.refs_0_.groups_ref = f32[32,8,128]{2,1,0:T(8,128)S(1)} async-done(((f32[32,8,128]{2,1,0:T(8,128)}), f32[32,8,128]{2,1,0:T(8,128)S(1)}, u32[]{:S(2)}, u32[]{:S(2)}) %all-to-all-start) | async-done | bytes 131104 | tf_op jit(solution)/shard_map/all_to_all | solution.py:533
  18.6 5.8 %shard_map.79 = (f32[8,2048]{1,0:T(8,128)S(1)}, f32[8,1024]{1,0:T(8,128)S(1)}, bf16[8,2,256,2048]{3,2,1,0:T(8,128)(2,1)S(1)}) custom-call(f32[32,8,128]{2,1,0:T(8,128)S(1)} %all-to-all-done.refs_0_.groups_ref, f32[3,2048]{1,0:T(4,128)S(1)} %constant_dynamic-slice_fusion.refs_1_.q_ref, f32[1,2048]{1,0:T(1,128)S(1)} %slice.3.refs_2_), custom_call_target="tpu_custom_call" | custom-call | flops 10000000000 | bytes 1000000 | tf_op jit(solution)/shard_map/pallas_call | solution.py:543
  24.4 0.0 copy-start.3
  24.4 0.5 collective-permute-start.1
  24.9 1.3 %collective-permute-start = (f32[8,1024]{1,0:T(8,128)S(1)}, f32[8,1024]{1,0:T(8,128)S(1)}, u32[]{:S(2)}, u32[]{:S(2)}) collective-permute-start(f32[8,1024]{1,0:T(8,128)S(1)} %get-tuple-element.30), channel_id=1, source_target_pairs={{0,8},{8,16},{16,24},{24,32},{32,40},{40,48},{48,56},{56,64},{64,7... | collective-permute-start | bytes 98312 | tf_op jit(solution)/shard_map/ppermute | solution.py:547
  26.3 4.5 %shard_map.80 = (f32[3,512,128]{2,1,0:T(8,128)S(1)}, f32[8,2048]{1,0:T(8,128)S(1)}, f32[8,512]{1,0:T(8,128)S(1)}, f32[8,512]{1,0:T(8,128)S(1)}, f32[8,512]{1,0:T(8,128)S(1)}) custom-call(s32[512,128]{1,0:T(8,128)S(1)} %bitcast.5, f32[8,2048]{1,0:T(8,128)S(1)} %get-tuple-element.27.refs_1_, bf16[640,2048]{1,0:T(8,128)(2,1)S(1)} %copy-done.1), custom_call_target="tpu_custom_call" | custom-call | flops 4000000000 | bytes 4000000 | tf_op jit(solution)/shard_map/pallas_call | solution.py:550
  30.8 0.0 collective-permute-done.1.refs_2_
  30.8 3.3 %shard_map.81 = (f32[12,128,128]{2,1,0:T(8,128)S(1)}, f32[8,768]{1,0:T(8,128)S(1)}, f32[8,768]{1,0:T(8,128)S(1)}) custom-call(s32[512,128]{1,0:T(8,128)S(1)} %bitcast.6, f32[8,1024]{1,0:T(8,128)S(1)} %collective-permute-done.refs_1_, f32[8,1024]{1,0:T(8,128)S(1)} %collective-permute-done.1.refs_2_, f32[8,512]{1,0:T(8,128)S(1)} %get-tuple-element.31.refs_3_, ...), custom_call_target="tpu_custom_call" | custom-call | flops 2000000000 | bytes 1000000 | tf_op jit(solution)/shard_map/pallas_call | solution.py:558
  34.1 6.1 %collective-permute-start.2 = (f32[8,768]{1,0:T(8,128)S(1)}, f32[8,768]{1,0:T(8,128)S(1)}, u32[]{:S(2)}, u32[]{:S(2)}) collective-permute-start(f32[8,768]{1,0:T(8,128)S(1)} %get-tuple-element.39), channel_id=1, source_target_pairs={{1,0},{2,1},{3,2},{4,3},{5,4},{6,5},{7,6},{0,7},{9,8},{10,9},{11,1... | collective-permute-start | bytes 73736 | tf_op jit(solution)/shard_map/ppermute | solution.py:563
  40.3 2.5 %shard_map.82 = (f32[3,512,128]{2,1,0:T(8,128)S(1)}, f32[3,128,128]{2,1,0:T(8,128)S(1)}, f32[8,2048]{1,0:T(8,128)S(1)}, f32[8,512]{1,0:T(8,128)S(1)}) custom-call(s32[512,128]{1,0:T(8,128)S(1)} %bitcast.7, f32[3,512,128]{2,1,0:T(8,128)S(1)} %get-tuple-element.29.refs_1_, f32[12,128,128]{2,1,0:T(8,128)S(1)} %get-tuple-element.35.refs_2_, ...), custom_call_target="tpu_custom_call" | custom-call | flops 4000000000 | bytes 4000000 | tf_op jit(solution)/shard_map/pallas_call | solution.py:565
  42.8 2.1 %collective-permute-done.3.refs_6_ = f32[8,768]{1,0:T(8,128)S(1)} collective-permute-done((f32[8,768]{1,0:T(8,128)S(1)}, f32[8,768]{1,0:T(8,128)S(1)}, u32[]{:S(2)}, u32[]{:S(2)}) %collective-permute-start.3) | collective-permute-done | bytes 24608 | tf_op jit(solution)/shard_map/ppermute | solution.py:564
  44.8 1.5 %shard_map.83 = (f32[3,512,128]{2,1,0:T(8,128)S(1)}, f32[8,2048]{1,0:T(8,128)S(1)}, f32[8,128]{1,0:T(8,128)S(1)}) custom-call(s32[512,128]{1,0:T(8,128)S(1)} %bitcast.8, f32[3,512,128]{2,1,0:T(8,128)S(1)} %get-tuple-element.29.refs_1_, f32[3,512,128]{2,1,0:T(8,128)S(1)} %get-tuple-element.37.refs_2_, f32[3,128,128]{2,1,0:T(8,128)S(1)} %get-tuple-element.38.refs_3_, ...), custom_call_target="tpu_custom_call" | custom-call | flops 1000000000 | bytes 4000000 | tf_op jit(solution)/shard_map/pallas_call | solution.py:573
  46.3 0.0 copy-start.4
  46.3 3.3 %shard_map.84 = f32[32,8,128]{2,1,0:T(8,128)S(1)} custom-call(f32[32,8,128]{2,1,0:T(8,128)S(1)} %all-to-all-done.refs_0_.groups_ref, bf16[8,2,256,2048]{3,2,1,0:T(8,128)(2,1)S(1)} %get-tuple-element.26.kept_ref, f32[3,2048]{1,0:T(4,128)S(1)} %constant_dynamic-slice_fusion.refs_1_.q_ref, f32[8,2048]{1,0:T(8,128)S(1)} %get-tuple-element.43.g_ref, ...), custom_call_target="tpu_custom_call" | custom-call | flops 10000000000 | bytes 1000000 | tf_op jit(solution)/shard_map/pallas_call | solution.py:576
  49.6 14.6 %all_to_all.15.refs_1_ = f32[32,8,128]{2,1,0:T(8,128)S(1)} all-to-all(f32[32,8,128]{2,1,0:T(8,128)S(1)} %shard_map.84), channel_id=1, replica_groups=mesh['seg'=32,'fe'=8] {'seg'}, dimensions={0} | all-to-all | bytes 262144 | tf_op jit(solution)/shard_map/all_to_all | solution.py:581
  64.2 0.3 shard_map.85
  64.4 13.1 %all_to_all.16.refs_0_ = f32[8,8,128]{2,1,0:T(8,128)S(1)} all-to-all(f32[8,8,128]{2,1,0:T(8,128)S(1)} %shard_map.85), channel_id=1, replica_groups=mesh['seg'=32,'fe'=8] {'fe'}, dimensions={0} | all-to-all | bytes 65536 | tf_op jit(solution)/shard_map/all_to_all | solution.py:583
  77.5 1.2 %shard_map.86 = (f32[3,512,128]{2,1,0:T(8,128)}, f32[3,128]{1,0:T(4,128)}) custom-call(f32[8,8,128]{2,1,0:T(8,128)S(1)} %all_to_all.16.refs_0_, f32[3,512,128]{2,1,0:T(8,128)S(1)} %get-tuple-element.29.refs_1_, f32[3,512,128]{2,1,0:T(8,128)S(1)} %get-tuple-element.45.refs_2_), custom_call_target="tpu_custom_call" | custom-call | tf_op jit(solution)/shard_map/pallas_call | solution.py:588
  (12 shorter events, 0.0 us)
Async XLA Ops:
  0.6 15.1 %copy-start = (f32[3,65536]{1,0:T(4,128)S(1)}, f32[3,65536]{1,0:T(4,128)}, u32[]{:S(2)}) copy-start(f32[3,65536]{1,0:T(4,128)} %param.9) | copy-start | bytes 2359300
  2.4 16.2 %all-to-all-start = ((f32[32,8,128]{2,1,0:T(8,128)}), f32[32,8,128]{2,1,0:T(8,128)S(1)}, u32[]{:S(2)}, u32[]{:S(2)}) async-start(f32[32,8,128]{2,1,0:T(8,128)} %shard_map.77), calls=%async_computation | async-start | bytes 262144 | tf_op jit(solution)/shard_map/all_to_all | solution.py:533
  15.8 10.5 %copy-start.2 = (s32[65536]{0:T(1024)S(1)}, s32[65536]{0:T(1024)}, u32[]{:S(2)}) copy-start(s32[65536]{0:T(1024)} %param.10) | copy-start | bytes 786436
  15.8 15.0 %copy-start.5 = (f32[8,512]{1,0:T(8,128)S(1)}, f32[8,512]{1,0:T(8,128)}, u32[]{:S(2)}) copy-start(f32[8,512]{1,0:T(8,128)} %get-tuple-element.34.refs_6_) | copy-start | bytes 49156
  18.6 7.7 %copy-start.1 = (bf16[640,2048]{1,0:T(8,128)(2,1)S(1)}, bf16[640,2048]{1,0:T(8,128)(2,1)}, u32[]{:S(2)}) copy-start(bf16[640,2048]{1,0:T(8,128)(2,1)} %get-tuple-element.28.refs_2_.refs_5_.refs_10_) | copy-start | bytes 7864324
  24.4 15.8 %copy-start.3 = (f32[4,128,128]{2,1,0:T(8,128)S(1)}, f32[4,128,128]{2,1,0:T(8,128)}, u32[]{:S(2)}) copy-start(f32[4,128,128]{2,1,0:T(8,128)} %param.11) | copy-start | bytes 786436
  24.4 6.3 %collective-permute-start.1 = (f32[8,1024]{1,0:T(8,128)S(1)}, f32[8,1024]{1,0:T(8,128)S(1)}, u32[]{:S(2)}, u32[]{:S(2)}) collective-permute-start(f32[8,1024]{1,0:T(8,128)S(1)} %get-tuple-element.30), channel_id=1, source_target_pairs={{8,0},{16,8},{24,16},{32,24},{40,32},{48,40},{56,48},{64,56},{72,6... | collective-permute-start | bytes 98312 | tf_op jit(solution)/shard_map/ppermute | solution.py:548
  24.9 5.9 %collective-permute-start = (f32[8,1024]{1,0:T(8,128)S(1)}, f32[8,1024]{1,0:T(8,128)S(1)}, u32[]{:S(2)}, u32[]{:S(2)}) collective-permute-start(f32[8,1024]{1,0:T(8,128)S(1)} %get-tuple-element.30), channel_id=1, source_target_pairs={{0,8},{8,16},{16,24},{24,32},{32,40},{40,48},{48,56},{56,64},{64,7... | collective-permute-start | bytes 98312 | tf_op jit(solution)/shard_map/ppermute | solution.py:547
  34.1 8.6 %collective-permute-start.2 = (f32[8,768]{1,0:T(8,128)S(1)}, f32[8,768]{1,0:T(8,128)S(1)}, u32[]{:S(2)}, u32[]{:S(2)}) collective-permute-start(f32[8,768]{1,0:T(8,128)S(1)} %get-tuple-element.39), channel_id=1, source_target_pairs={{1,0},{2,1},{3,2},{4,3},{5,4},{6,5},{7,6},{0,7},{9,8},{10,9},{11,1... | collective-permute-start | bytes 73736 | tf_op jit(solution)/shard_map/ppermute | solution.py:563
  40.3 4.5 %collective-permute-start.3 = (f32[8,768]{1,0:T(8,128)S(1)}, f32[8,768]{1,0:T(8,128)S(1)}, u32[]{:S(2)}, u32[]{:S(2)}) collective-permute-start(f32[8,768]{1,0:T(8,128)S(1)} %get-tuple-element.40), channel_id=1, source_target_pairs={{0,1},{1,2},{2,3},{3,4},{4,5},{5,6},{6,7},{7,0},{8,9},{9,10},{10,1... | collective-permute-start | bytes 73736 | tf_op jit(solution)/shard_map/ppermute | solution.py:564
  46.3 17.9 %copy-start.4 = (s32[128]{0:T(128)S(1)}, s32[128]{0:T(128)}, u32[]{:S(2)}) copy-start(s32[128]{0:T(128)} %param.8) | copy-start | bytes 1540
